TPU v7x, 1024 devices: a whole 4x4x32 slice. The times are simulated.
1024 devices in a mesh: ab: 128 (over z, y), cd: 8 (over x, core).
Axes of the slice: x: 4, y: 4, z: 32, core: 2. Of those that a mesh axis runs over, the one named last changes fastest.
Arguments:
- integrals: float32 [131072, 4096], P('ab', 'cd'), may hold values from -0.375 to 0.375
- amplitudes: float32 [1024, 4096], P('ab', 'cd'), may hold values from -6 to 6
- allowed: int32 [1024, 32], P('ab', 'cd'), may hold values 0 or 1
Outputs:
- residual: float32 [1024, 131072], P('cd', 'ab')
All inputs are finite; a program needn't handle non-finite values. No bound on the sum of `allowed` on one device may be relied on, other than what follows from the above.
Results may differ from a plain program's by a relative error of at most 0.00007.
Values sent between devices are 32-bit elements; how exact they have to be, the bound alone decides.
No kernel may reach another device: no remote copies, remote signals or barrier semaphores. Data moves between devices by JAX's collectives and lax.ppermute only.
A program may use at most 32 MiB of HBM per device.

v0:
```python
import jax
import jax.numpy as jnp
from jax import lax
from jax.sharding import PartitionSpec as P

BLK = 128


def masked_slab(integrals, allowed):
    rows, cols = integrals.shape
    weights = allowed.astype(jnp.float32)[:, None, :, None]
    kept = integrals.reshape(rows // BLK, BLK, cols // BLK, BLK) * weights
    return kept.reshape(rows, cols)


def per_device(integrals, amplitudes, allowed):
    kept = masked_slab(integrals, allowed)
    gathered = lax.all_gather(amplitudes, "ab", axis=0, tiled=True)
    return lax.psum_scatter(
        lax.dot_general(
            gathered,
            kept,
            (((1,), (1,)), ((), ())),
            precision=lax.Precision.HIGHEST,
            preferred_element_type=jnp.float32,
        ),
        "cd",
        scatter_dimension=0,
        tiled=True,
    )


def solution(mesh):
    in_specs = (P("ab", "cd"), P("ab", "cd"), P("ab", "cd"))
    out_specs = P("cd", "ab")
    return jax.shard_map(
        per_device, mesh=mesh, in_specs=in_specs, out_specs=out_specs, check_vma=False
    )
```

profile of v0, /device:TPU:24, one launch (start us, length us, event | category | flops | bytes accessed | tf_op | source)
XLA Modules:
  0.0 350.8 jit_solution(12461642859710141140)
XLA Ops:
  6.5 0.0 copy-start
  6.5 0.0 all-gather.2.cloned.1.call-start
  6.5 0.7 all-gather.2.cloned.1.call-update
  7.3 0.0 reduce-scatter.2.cloned.1.call-start
  7.3 0.7 convert_element_type.3
  8.0 0.1 copy.4
  8.1 276.8 %all-gather.2.cloned.1.call-done = f32[1024,512]{1,0:T(8,128)} async-done(((f32[8,512]{1,0:T(8,128)}), f32[1024,512]{1,0:T(8,128)}) %all-gather.2.cloned.1.call-update) | async-done | bytes 2097168 | tf_op jit(solution)/shard_map/all_gather | solution.py:18
  284.9 0.3 mul.11
  285.3 0.0 copy-done
  285.3 9.5 %convolution_bitcast_fusion = f32[1024,1024]{0,1:T(8,128)} fusion(f32[1024,512]{1,0:T(8,128)} %all-gather.2.cloned.1.call-done, f32[1024,512]{1,0:T(8,128)S(1)} %copy-done, f32[128,8,4,128]{3,2,1,0:T(4,128)S(1)} %bitcast.8), kind=kOutput, calls=%fused_computation | convolution fusion | flops 6442975232 | bytes 10485760 | tf_op jit(solution)/shard_map/dot_general | solution.py:20
  294.8 0.0 reduce-scatter.2.cloned.1.call-update
  294.8 47.1 %reduce-scatter.2.cloned.1.call-done = f32[128,1024]{0,1:T(8,128)} async-done(((f32[1024,1024]{0,1:T(8,128)}), f32[128,1024]{0,1:T(8,128)}) %reduce-scatter.2.cloned.1.call-update) | async-done | bytes 524304 | tf_op jit(solution)/shard_map/reduce_scatter | solution.py:19
  341.9 2.0 copy.5
Async XLA Ops:
  6.5 278.7 %copy-start = (f32[1024,512]{1,0:T(8,128)S(1)}, f32[1024,512]{1,0:T(8,128)}, u32[]{:S(2)}) copy-start(f32[1024,512]{1,0:T(8,128)} %param.3) | copy-start | bytes 6291460
  6.5 278.4 %all-gather.2.cloned.1.call-start = ((), (), s32[]{:S(2)}) async-start(), calls=%async_computation.1 | async-start | bytes 2113536 | tf_op jit(solution)/shard_map/all_gather | solution.py:18
  7.3 334.6 %reduce-scatter.2.cloned.1.call-start = ((), (), s32[]{:S(2)}) async-start(), calls=%async_computation.2 | async-start | bytes 4718592 | tf_op jit(solution)/shard_map/reduce_scatter | solution.py:19
Sparse Core Ops, SparseCore 0:
  11.5 273.4 all-gather.1
  294.9 46.9 reduce-scatter.1
where the time goes:
time: 352 us; the launch traced here: 351 us
  waiting for transfers between devices  325 us (92%)
  between operations  13.4 us (4%)
  matrix products  9.52 us (3%)
    all_gather x1, waiting for transfers between devices, per_device(): gathered = lax.all_gather(amplitudes, 'ab', axis=0, tiled=True)  277 us
    reduce_scatter x1, waiting for transfers between devices, per_device(): lax.psum_scatter(lax.dot_general(gathered, kept, (((1,), (1,)), ((), ()))...  47.1 us
    dot_general x1, matrix products, per_device(): lax.dot_general(gathered, kept, (((1,), (1,)), ((), ())), precision=lax.P...  9.52 us
  transfers between devices with their start and end apart: 2, of which 2 were waited for; matrix products, arithmetic and copies ran while one was open for 0% of the time, Pallas kernels for 0%

commit v1 on v0

v1 whole, which is shorter than its diff:
```python
import jax
import jax.numpy as jnp
from jax import lax
from jax.experimental import pallas as pl
from jax.experimental.pallas import tpu as pltpu
from jax.sharding import Mesh, PartitionSpec as P

BLK = 128
NT = (((1,), (1,)), ((), ()))
COLS = 256


def split(wide):
    high = wide.astype(jnp.bfloat16)
    return high, (wide - high.astype(jnp.float32)).astype(jnp.bfloat16)


def ladder_body(par_ref, allowed_ref, t_ref, v_ref, *rest):
    got_ref = rest[0] if len(rest) == 4 else None
    out_ref, th_ref, tl_ref = rest[-3:]
    step = pl.program_id(0)

    @pl.when(step == 0)
    def _():
        for xx in range(4):
            for low in range(4):
                rows = jnp.concatenate([t_ref[yy, low, xx, 0] for yy in range(4)], axis=0)
                high, rest_ = split(rows)
                at = (xx * 4 + low) * 32
                th_ref[at : at + 32, :] = high
                tl_ref[at : at + 32, :] = rest_

    rows = []
    for a in range(COLS // BLK):
        row = []
        for c in range(v_ref.shape[1] // BLK):
            weight = allowed_ref[step * (COLS // BLK) + a, c].astype(jnp.float32)
            row.append(v_ref[a * BLK : (a + 1) * BLK, c * BLK : (c + 1) * BLK] * weight)
        rows.append(jnp.concatenate(row, axis=1))
    vh, vl = split(jnp.concatenate(rows, axis=0))

    def dot(left, right):
        return lax.dot_general(left, right, NT, preferred_element_type=jnp.float32)

    th, tl = th_ref[...], tl_ref[...]
    total = dot(tl, vh) + dot(th, vl) + dot(th, vh)
    if got_ref is not None:
        total = total + got_ref[...]
    out_ref[...] = total


def ladder(par, allowed, amps, slab, got=None):
    width, depth = slab.shape
    in_specs = [
        pl.BlockSpec((4, 4, 4, 1, 8, depth), lambda i, par, allowed: (0, 0, 0, par[0], 0, 0)),
        pl.BlockSpec((COLS, depth), lambda i, par, allowed: (i, 0)),
    ]
    args = [amps, slab]
    if got is not None:
        in_specs.append(pl.BlockSpec((512, COLS), lambda i, par, allowed: (0, i)))
        args.append(got)
    return pl.pallas_call(
        ladder_body,
        out_shape=jax.ShapeDtypeStruct((512, width), jnp.float32),
        grid_spec=pltpu.PrefetchScalarGridSpec(
            num_scalar_prefetch=2,
            grid=(width // COLS,),
            in_specs=in_specs,
            out_specs=pl.BlockSpec((512, COLS), lambda i, par, allowed: (0, i)),
            scratch_shapes=[pltpu.VMEM((512, depth), jnp.bfloat16)] * 2,
        ),
        compiler_params=pltpu.CompilerParams(vmem_limit_bytes=32 * 2**20),
        cost_estimate=pl.CostEstimate(
            flops=6 * 512 * width * depth, bytes_accessed=8 * 2**20, transcendentals=0
        ),
    )(par, allowed, *args)


def everywhere(block, axes, size):
    spread = jnp.broadcast_to(block[None], (size, *block.shape))
    return lax.all_to_all(spread, axes, 0, 0)


def per_device(integrals, amplitudes, allowed):
    with jax.named_scope("gather_far"):
        far = everywhere(amplitudes, "zh", 8)
    with jax.named_scope("gather_near"):
        near = everywhere(far, "zl", 4)
    with jax.named_scope("gather_y"):
        amps = everywhere(near, "y", 4).reshape(4, 4, 4, 2, 8, 512)
    core = lax.axis_index("core").astype(jnp.int32)
    with jax.named_scope("other_half"):
        other = ladder((1 - core)[None], allowed, amps, integrals)
        got = lax.ppermute(other, "core", [(0, 1), (1, 0)])
    with jax.named_scope("own_half"):
        own = ladder(core[None], allowed, amps, integrals, got)
    with jax.named_scope("reduce_x"):
        parts = lax.all_to_all(own.reshape(4, 128, 1024), "x", 0, 0)
        return jnp.sum(parts, axis=0)


def solution(mesh):
    fine = Mesh(mesh.devices.reshape(8, 4, 4, 4, 2), ("zh", "zl", "y", "x", "core"))
    rows, cols = ("zh", "zl", "y"), ("x", "core")
    return jax.shard_map(
        per_device, mesh=fine, in_specs=(P(rows, cols),) * 3, out_specs=P(cols, rows), check_vma=False
    )
```

time: 352 us -> 153 us (0.43)
  waiting for transfers between devices: 325 us -> 26.9 us
  blocking collectives: 0 us -> 105 us
  between operations: 13.4 us -> 0.04 us
  matrix products: 9.52 us -> 0 us
  Pallas kernels: 0 us -> 7.14 us
  starting transfers between devices: 0.04 us -> 6.74 us
    all_gather x1 -> x0, waiting for transfers between devices: 277 us -> none  [per_device(): gathered = lax.all_gather(amplitudes, 'ab', axis=0, tiled=True)]
    all_to_all x0 -> x3, blocking collectives: none -> 105 us  [the longest x2 74 us: everywhere(): return lax.all_to_all(spread, axes, 0, 0)]
    reduce_scatter x1 -> x0, waiting for transfers between devices: 47.1 us -> none  [per_device(): lax.psum_scatter(lax.dot_general(gathered, kept, (((1,), (1,)), ((), ()))...]
    all_to_all x0 -> x1, waiting for transfers between devices: none -> 22.8 us  [everywhere(): return lax.all_to_all(spread, axes, 0, 0)]
    dot_general x1 -> x0, matrix products: 9.52 us -> none  [per_device(): lax.dot_general(gathered, kept, (((1,), (1,)), ((), ())), precision=lax.P...]
    pallas_call x0 -> x2, Pallas kernels: none -> 7.14 us  [ladder(): pl.pallas_call(ladder_body, out_shape=jax.ShapeDtypeStruct((512, width),...]
    all_to_all x0 -> x1, starting transfers between devices: none -> 4.82 us  [everywhere(): return lax.all_to_all(spread, axes, 0, 0)]
    ppermute x0 -> x1, waiting for transfers between devices: none -> 4.13 us  [per_device(): got = lax.ppermute(other, 'core', [(0, 1), (1, 0)])]
where the time goes in v1:
time: 153 us; the launch traced here: 151 us
  blocking collectives  105 us (69%)
  waiting for transfers between devices  26.9 us (18%)
  Pallas kernels  7.14 us (5%)
  starting transfers between devices  6.74 us (4%)
  local copies, waits for them, and re-layouts  4.05 us (3%)
    all_to_all x2, blocking collectives, everywhere(): return lax.all_to_all(spread, axes, 0, 0)  74 us
    all_to_all x1, blocking collectives, per_device(): parts = lax.all_to_all(own.reshape(4, 128, 1024), 'x', 0, 0)  30.7 us
    all_to_all x1, waiting for transfers between devices, everywhere(): return lax.all_to_all(spread, axes, 0, 0)  22.8 us
    pallas_call x2, Pallas kernels, ladder(): pl.pallas_call(ladder_body, out_shape=jax.ShapeDtypeStruct((512, width),...  7.14 us
    all_to_all x1, starting transfers between devices, everywhere(): return lax.all_to_all(spread, axes, 0, 0)  4.82 us
    ppermute x1, waiting for transfers between devices, per_device(): got = lax.ppermute(other, 'core', [(0, 1), (1, 0)])  4.13 us
  transfers between devices with their start and end apart: 2, of which 2 were waited for; matrix products, arithmetic and copies ran while one was open for 0% of the time, Pallas kernels for 0%

profile of v1, /device:TPU:24, one launch (start us, length us, event | category | flops | bytes accessed | tf_op | source)
XLA Modules:
  0.0 150.6 jit_solution(8711027754480603637)
XLA Ops:
  0.0 0.7 broadcast_in_dim.11
  0.7 55.9 %all_to_all.20 = f32[8,8,512]{2,1,0:T(8,128)S(1)} all-to-all(f32[8,8,512]{2,1,0:T(8,128)S(1)} %broadcast_in_dim.11), channel_id=1, replica_groups=mesh['zh'=8,'zl'=4,'y'=4,'x'=4,'core'=2] {'zh'}, dimensions={0} | all-to-all | bytes 262144 | tf_op jit(solution)/shard_map/gather_far/all_to_all | solution.py:81
  56.7 18.1 %all_to_all.21 = f32[4,8,8,512]{3,2,1,0:T(8,128)S(1)} all-to-all(f32[4,8,8,512]{3,2,1,0:T(8,128)S(1)} %broadcast_in_dim.12), channel_id=1, replica_groups=mesh['zh'=8,'zl'=4,'y'=4,'x'=4,'core'=2] {'zl'}, dimensions={0} | all-to-all | bytes 1048576 | tf_op jit(solution)/shard_map/gather_near/all_to_all | solution.py:81
  74.8 1.6 %broadcast_in_dim.13 = f32[4,4,8,8,512]{4,3,2,1,0:T(8,128)} broadcast(f32[4,8,8,512]{3,2,1,0:T(8,128)S(1)} %all_to_all.21), dimensions={1,2,3,4} | broadcast | bytes 2621440 | tf_op jit(solution)/shard_map/gather_y/broadcast_in_dim | solution.py:80
  76.4 0.0 copy-start.2
  76.4 4.8 %all-to-all-start.2 = ((f32[4,4,8,8,512]{4,3,2,1,0:T(8,128)}), f32[4,4,8,8,512]{4,3,2,1,0:T(8,128)S(1)}, u32[]{:S(2)}, u32[]{:S(2)}) async-start(f32[4,4,8,8,512]{4,3,2,1,0:T(8,128)} %broadcast_in_dim.13), calls=%async_computation.2 | async-start | bytes 4194304 | tf_op jit(solution)/shard_map/gather_y/all_to_all | solution.py:81
  81.2 0.0 copy-done.2
  81.2 0.1 copy.5.allowed_ref
  81.3 22.8 %all-to-all-done.2 = f32[4,4,8,8,512]{4,3,2,1,0:T(8,128)S(1)} async-done(((f32[4,4,8,8,512]{4,3,2,1,0:T(8,128)}), f32[4,4,8,8,512]{4,3,2,1,0:T(8,128)S(1)}, u32[]{:S(2)}, u32[]{:S(2)}) %all-to-all-start.2) | async-done | bytes 2097184 | tf_op jit(solution)/shard_map/gather_y/all_to_all | solution.py:81
  104.1 0.0 copy-start
  104.1 1.6 %copy-done = f32[1024,512]{1,0:T(8,128)S(1)} copy-done((f32[1024,512]{1,0:T(8,128)S(1)}, f32[1024,512]{1,0:T(8,128)}, u32[]{:S(2)}) %copy-start) | copy-done | bytes 2097176
  105.7 0.0 copy-start.1
  105.7 3.5 %other_half.1 = f32[512,1024]{1,0:T(8,128)S(1)} custom-call(s32[1]{0:T(128)} %bitcast.2.par_ref, s32[8,4]{1,0:T(8,128)S(1)} %copy.5.allowed_ref, f32[4,4,4,2,8,512]{5,4,3,2,1,0:T(8,128)S(1)} %bitcast.4, f32[1024,512]{1,0:T(8,128)S(1)} %copy-done), custom_call_target="tpu_custom_call" | custom-call | flops 1610612736 | bytes 8388608 | tf_op jit(solution)/shard_map/other_half/pallas_call | solution.py:62
  109.2 1.9 %collective-permute-start = (f32[512,1024]{1,0:T(8,128)S(1)}, f32[512,1024]{1,0:T(8,128)S(1)}, u32[]{:S(2)}, u32[]{:S(2)}) collective-permute-start(f32[512,1024]{1,0:T(8,128)S(1)} %other_half.1), channel_id=1, source_target_pairs={{0,1},{1,0},{2,3},{3,2},{4,5},{5,4},{6,7},{7,6},{8,9},{9,8},{10,11... | collective-permute-start | bytes 6291464 | tf_op jit(solution)/shard_map/other_half/ppermute | solution.py:94
  111.1 4.1 %collective-permute-done.rest_0_ = f32[512,1024]{1,0:T(8,128)S(1)} collective-permute-done((f32[512,1024]{1,0:T(8,128)S(1)}, f32[512,1024]{1,0:T(8,128)S(1)}, u32[]{:S(2)}, u32[]{:S(2)}) %collective-permute-start) | collective-permute-done | bytes 2097184 | tf_op jit(solution)/shard_map/other_half/ppermute | solution.py:94
  115.2 0.0 copy-done.1
  115.2 3.7 %own_half.1 = f32[512,1024]{1,0:T(8,128)S(1)} custom-call(s32[1]{0:T(128)} %bitcast.par_ref, s32[8,4]{1,0:T(8,128)S(1)} %copy.5.allowed_ref, f32[4,4,4,2,8,512]{5,4,3,2,1,0:T(8,128)S(1)} %bitcast.5, f32[1024,512]{1,0:T(8,128)S(1)} %copy-done.1, f32[512,1024]{1,0:T(8,128)S(1)} %collective-permute-done.rest_0_), custom_call_target="tpu_custom_call" | custom-call | flops 1610612736 | bytes 8388608 | tf_op jit(solution)/shard_map/own_half/pallas_call | solution.py:62
  118.9 30.7 %all_to_all.22 = f32[4,128,1024]{2,1,0:T(8,128)S(1)} all-to-all(f32[4,128,1024]{2,1,0:T(8,128)S(1)} %bitcast.6), channel_id=1, replica_groups=mesh['zh'=8,'zl'=4,'y'=4,'x'=4,'core'=2] {'x'}, dimensions={0} | all-to-all | bytes 4194304 | tf_op jit(solution)/shard_map/reduce_x/all_to_all | solution.py:98
  149.6 1.0 reduce_sum.9
  (1 shorter events, 0.0 us)
Async XLA Ops:
  76.4 4.8 %copy-start.2 = (s32[8,4]{0,1:T(4,128)S(1)}, s32[8,4]{0,1:T(4,128)}, u32[]{:S(2)}) copy-start(s32[8,4]{0,1:T(4,128)} %param.5) | copy-start | bytes 388
  76.4 27.7 %all-to-all-start.2 = ((f32[4,4,8,8,512]{4,3,2,1,0:T(8,128)}), f32[4,4,8,8,512]{4,3,2,1,0:T(8,128)S(1)}, u32[]{:S(2)}, u32[]{:S(2)}) async-start(f32[4,4,8,8,512]{4,3,2,1,0:T(8,128)} %broadcast_in_dim.13), calls=%async_computation.2 | async-start | bytes 4194304 | tf_op jit(solution)/shard_map/gather_y/all_to_all | solution.py:81
  104.1 1.6 %copy-start = (f32[1024,512]{1,0:T(8,128)S(1)}, f32[1024,512]{1,0:T(8,128)}, u32[]{:S(2)}) copy-start(f32[1024,512]{1,0:T(8,128)} %v_ref.3) | copy-start | bytes 6291460
  105.7 9.5 %copy-start.1 = (f32[1024,512]{1,0:T(8,128)S(1)}, f32[1024,512]{1,0:T(8,128)}, u32[]{:S(2)}) copy-start(f32[1024,512]{1,0:T(8,128)} %v_ref.3) | copy-start | bytes 6291460
  109.2 6.1 %collective-permute-start = (f32[512,1024]{1,0:T(8,128)S(1)}, f32[512,1024]{1,0:T(8,128)S(1)}, u32[]{:S(2)}, u32[]{:S(2)}) collective-permute-start(f32[512,1024]{1,0:T(8,128)S(1)} %other_half.1), channel_id=1, source_target_pairs={{0,1},{1,0},{2,3},{3,2},{4,5},{5,4},{6,7},{7,6},{8,9},{9,8},{10,11... | collective-permute-start | bytes 6291464 | tf_op jit(solution)/shard_map/other_half/ppermute | solution.py:94

commit v2 on v0

v2 whole, which is shorter than its diff:
```python
import functools

import jax
import jax.numpy as jnp
from jax import lax
from jax.experimental import pallas as pl
from jax.experimental.pallas import tpu as pltpu
from jax.sharding import Mesh, PartitionSpec as P

BLK = 128
NT = (((1,), (1,)), ((), ()))
COLS = 256
PARAMS = pltpu.CompilerParams(vmem_limit_bytes=16 * 2**20)


def split(wide):
    high = wide.astype(jnp.bfloat16)
    return high, (wide - high.astype(jnp.float32)).astype(jnp.bfloat16)


def mask_body(allowed_ref, v_ref, kept_ref, high_ref, low_ref):
    step = pl.program_id(0)
    for a in range(COLS // BLK):
        rows = pl.ds(a * BLK, BLK)
        for c in range(v_ref.shape[1] // BLK):
            cols = pl.ds(c * BLK, BLK)
            weight = allowed_ref[step * (COLS // BLK) + a, c].astype(jnp.float32)
            kept = v_ref[rows, cols] * weight
            kept_ref[rows, cols] = kept
            high_ref[rows, cols], low_ref[rows, cols] = split(kept)


def masked(integrals, allowed):
    rows, depth = integrals.shape
    block = pl.BlockSpec((COLS, depth), lambda i, allowed: (i, 0))
    return pl.pallas_call(
        mask_body,
        out_shape=[jax.ShapeDtypeStruct((rows, depth), t) for t in (jnp.float32, jnp.bfloat16, jnp.bfloat16)],
        grid_spec=pltpu.PrefetchScalarGridSpec(
            num_scalar_prefetch=1, grid=(rows // COLS,), in_specs=[block], out_specs=[block] * 3
        ),
        compiler_params=PARAMS,
        cost_estimate=pl.CostEstimate(flops=2**21, bytes_accessed=6 * 2**20, transcendentals=0),
    )(allowed, integrals)


def parts_body(v_ref, high_ref, low_ref):
    high_ref[...], low_ref[...] = split(v_ref[...])


def parts_of(slab):
    rows, depth = slab.shape
    block = pl.BlockSpec((COLS, depth), lambda i: (i, 0))
    return pl.pallas_call(
        parts_body,
        out_shape=[jax.ShapeDtypeStruct((rows, depth), jnp.bfloat16)] * 2,
        grid=(rows // COLS,),
        in_specs=[block],
        out_specs=[block] * 2,
        compiler_params=PARAMS,
        cost_estimate=pl.CostEstimate(flops=2**21, bytes_accessed=4 * 2**20, transcendentals=0),
    )(slab)


def ladder_body(count, core_ref, *refs):
    t_refs, (oh_ref, ol_ref, sh_ref, sl_ref, out_ref, th_ref, tl_ref) = refs[:count], refs[count:]
    core = core_ref[0]
    size = 32 * count

    @pl.when(pl.program_id(0) == 0)
    def _():
        for side in range(2):
            source = core if side == 0 else 1 - core
            for xx in range(4):
                wide = jnp.concatenate([t[low, source, xx] for low in range(4) for t in t_refs], axis=0)
                at = pl.ds(xx * size, size)
                th_ref[side, at, :], tl_ref[side, at, :] = split(wide)

    def dot(left, right):
        return lax.dot_general(left, right, NT, preferred_element_type=jnp.float32)

    total = None
    for side, (vh_ref, vl_ref) in enumerate(((oh_ref, ol_ref), (sh_ref, sl_ref))):
        th, tl, vh = th_ref[side], tl_ref[side], vh_ref[...]
        term = dot(tl, vh) + dot(th, vl_ref[...]) + dot(th, vh)
        total = term if total is None else total + term
    out_ref[...] = total


def ladder(core, chunks, slabs):
    width, depth = slabs[0].shape
    rows = 128 * len(chunks)
    return pl.pallas_call(
        functools.partial(ladder_body, len(chunks)),
        out_shape=jax.ShapeDtypeStruct((rows, width), jnp.float32),
        grid_spec=pltpu.PrefetchScalarGridSpec(
            num_scalar_prefetch=1,
            grid=(width // COLS,),
            in_specs=[pl.BlockSpec((4, 2, 4, 8, depth), lambda i, core: (0, 0, 0, 0, 0))] * len(chunks)
            + [pl.BlockSpec((COLS, depth), lambda i, core: (i, 0))] * 4,
            out_specs=pl.BlockSpec((rows, COLS), lambda i, core: (0, i)),
            scratch_shapes=[pltpu.VMEM((2, rows, depth), jnp.bfloat16)] * 2,
        ),
        compiler_params=PARAMS,
        cost_estimate=pl.CostEstimate(
            flops=12 * rows * width * depth, bytes_accessed=4 * 2**20, transcendentals=0
        ),
    )(core, *chunks, *slabs)


def finish_body(y_ref, own_ref, sides_ref, across_ref, out_ref):
    me = y_ref[0]

    def put(offset, part_ref, k):
        place = lax.rem(me + offset, 4)
        for low in range(4):
            out_ref[low, place] = (part_ref[0, low, k] + part_ref[1, low, k]) + (part_ref[2, low, k] + part_ref[3, low, k])

    put(0, own_ref, 0)
    put(3, sides_ref, 0)
    put(1, sides_ref, 1)
    put(2, across_ref, 0)


def finish(y, own, sides, across):
    whole = lambda a: pl.BlockSpec(a.shape, lambda i, y: (0,) * a.ndim)
    out = jax.ShapeDtypeStruct((4, 4, 8, 1024), jnp.float32)
    return pl.pallas_call(
        finish_body,
        out_shape=out,
        grid_spec=pltpu.PrefetchScalarGridSpec(
            num_scalar_prefetch=1, grid=(1,), in_specs=[whole(a) for a in (own, sides, across)], out_specs=whole(out)
        ),
        compiler_params=PARAMS,
        cost_estimate=pl.CostEstimate(flops=2**19, bytes_accessed=5 * 2**19, transcendentals=0),
    )(y, own, sides, across)


def around(value, hops):
    return lax.ppermute(value, "y", [(i, (i + hops) % 4) for i in range(4)])


def over_x(partial):
    return lax.all_to_all(partial.reshape(4, 4, -1, 8, 1024), "x", 0, 0)


def per_device(integrals, amplitudes, allowed):
    core = lax.axis_index("core").astype(jnp.int32)[None]
    me = lax.axis_index("y").astype(jnp.int32)[None]
    with jax.named_scope("slab"):
        kept, own_high, own_low = masked(integrals, allowed)
        slabs = (own_high, own_low, *parts_of(lax.ppermute(kept, "core", [(0, 1), (1, 0)])))
    with jax.named_scope("gather_far"):
        far = lax.all_to_all(jnp.broadcast_to(amplitudes[None], (8, 8, 512)), "zh", 0, 0)
    with jax.named_scope("gather_near"):
        by_core = far.reshape(1, 4, 2, 8, 512).swapaxes(1, 2)
        spread = jnp.broadcast_to(by_core, (4, 2, 4, 8, 512)).reshape(8, 4, 8, 512)
        near = lax.all_to_all(spread, ("zl", "core"), 0, 0).reshape(4, 2, 4, 8, 512)
    with jax.named_scope("gather_y"):
        below, above = around(near, 1), around(near, 3)
        across = around(near, 2)
    with jax.named_scope("own_y"):
        own = over_x(ladder(core, [near], slabs))
    with jax.named_scope("sides_y"):
        sides = over_x(ladder(core, [below, above], slabs))
    with jax.named_scope("across_y"):
        opposite = over_x(ladder(core, [across], slabs))
    return finish(me, own, sides, opposite).reshape(128, 1024)


def solution(mesh):
    fine = Mesh(mesh.devices.reshape(8, 4, 4, 4, 2), ("zh", "zl", "y", "x", "core"))
    rows, cols = ("zh", "zl", "y"), ("x", "core")
    return jax.shard_map(
        per_device, mesh=fine, in_specs=(P(rows, cols),) * 3, out_specs=P(cols, rows), check_vma=False
    )
```

time: 352 us -> 140 us (0.40)
  waiting for transfers between devices: 325 us -> 25.4 us
  blocking collectives: 0 us -> 55.9 us
  starting transfers between devices: 0.04 us -> 30.3 us
  Pallas kernels: 0 us -> 18.9 us
  between operations: 13.4 us -> 0.15 us
  matrix products: 9.52 us -> 0 us
  local copies, waits for them, and re-layouts: 2.46 us -> 8.27 us
    all_gather x1 -> x0, waiting for transfers between devices: 277 us -> none  [per_device(): gathered = lax.all_gather(amplitudes, 'ab', axis=0, tiled=True)]
    all_to_all x0 -> x1, blocking collectives: none -> 55.9 us  [per_device(): lax.all_to_all(jnp.broadcast_to(amplitudes[None], (8, 8, 512)), 'zh', 0, 0)]
    reduce_scatter x1 -> x0, waiting for transfers between devices: 47.1 us -> none  [per_device(): lax.psum_scatter(lax.dot_general(gathered, kept, (((1,), (1,)), ((), ()))...]
    all_to_all x0 -> x4, waiting for transfers between devices: none -> 21.7 us  [the longest x3 13 us: over_x(): return lax.all_to_all(partial.reshape(4, 4, -1, 8, 1024), 'x', 0, 0)]
    pallas_call x0 -> x6, Pallas kernels: none -> 18.9 us  [the longest x3 11.7 us: ladder(): pl.pallas_call(functools.partial(ladder_body, len(chunks)), out_shape=jax...]
    all_to_all x0 -> x4, starting transfers between devices: none -> 18.7 us  [the longest x3 13.5 us: over_x(): return lax.all_to_all(partial.reshape(4, 4, -1, 8, 1024), 'x', 0, 0)]
    ppermute x0 -> x4, starting transfers between devices: none -> 11.5 us  [the longest x3 9.13 us: around(): return lax.ppermute(value, 'y', [(i, (i + hops) % 4) for i in range(4)])]
    dot_general x1 -> x0, matrix products: 9.52 us -> none  [per_device(): lax.dot_general(gathered, kept, (((1,), (1,)), ((), ())), precision=lax.P...]
  transfers between devices with their start and end apart: 2 -> 8, of which waited for: 2 -> 3; matrix products, arithmetic and copies ran while one was open for 0% -> 0% of each run, Pallas kernels for 0% -> 12%
where the time goes in v2:
time: 140 us; the launch traced here: 139 us
  blocking collectives  55.9 us (40%)
  starting transfers between devices  30.3 us (22%)
  waiting for transfers between devices  25.4 us (18%)
  Pallas kernels  18.9 us (13%)
  local copies, waits for them, and re-layouts  8.27 us (6%)
    all_to_all x1, blocking collectives, per_device(): lax.all_to_all(jnp.broadcast_to(amplitudes[None], (8, 8, 512)), 'zh', 0, 0)  55.9 us
    all_to_all x3, starting transfers between devices, over_x(): return lax.all_to_all(partial.reshape(4, 4, -1, 8, 1024), 'x', 0, 0)  13.5 us
    all_to_all x3, waiting for transfers between devices, over_x(): return lax.all_to_all(partial.reshape(4, 4, -1, 8, 1024), 'x', 0, 0)  13 us
    pallas_call x3, Pallas kernels, ladder(): pl.pallas_call(functools.partial(ladder_body, len(chunks)), out_shape=jax...  11.7 us
    ppermute x3, starting transfers between devices, around(): return lax.ppermute(value, 'y', [(i, (i + hops) % 4) for i in range(4)])  9.13 us
    all_to_all x1, waiting for transfers between devices, per_device(): near = lax.all_to_all(spread, ('zl', 'core'), 0, 0).reshape(4, 2, 4, 8, 512)  8.77 us
    unnamed x17, local copies, waits for them, and re-layouts  6.67 us
    all_to_all x1, starting transfers between devices, per_device(): near = lax.all_to_all(spread, ('zl', 'core'), 0, 0).reshape(4, 2, 4, 8, 512)  5.19 us
  transfers between devices with their start and end apart: 8, of which 3 were waited for; matrix products, arithmetic and copies ran while one was open for 0% of the time, Pallas kernels for 12%

profile of v2, /device:TPU:24, one launch (start us, length us, event | category | flops | bytes accessed | tf_op | source)
XLA Modules:
  0.0 138.9 jit_solution(17940112961661973592)
XLA Ops:
  0.0 0.0 copy-start.7
  0.0 0.7 broadcast_in_dim.21
  0.7 55.9 %all_to_all.25 = f32[8,8,512]{2,1,0:T(8,128)S(1)} all-to-all(f32[8,8,512]{2,1,0:T(8,128)S(1)} %broadcast_in_dim.21), channel_id=1, replica_groups=mesh['zh'=8,'zl'=4,'y'=4,'x'=4,'core'=2] {'zh'}, dimensions={0} | all-to-all | bytes 262144 | tf_op jit(solution)/shard_map/gather_far/all_to_all | solution.py:154
  56.7 0.9 broadcast_in_dim.23
  57.5 5.2 %all-to-all-start.1 = ((f32[8,4,8,512]{3,2,1,0:T(8,128)}), f32[8,4,8,512]{3,2,1,0:T(8,128)}, u32[]{:S(2)}, u32[]{:S(2)}) async-start(f32[8,4,8,512]{3,2,1,0:T(8,128)} %bitcast.5), calls=%async_computation.1 | async-start | bytes 1048576 | tf_op jit(solution)/shard_map/gather_near/all_to_all | solution.py:158
  62.7 0.0 copy-done.7
  62.7 0.1 copy.6.allowed_ref
  62.8 0.0 copy-start.4
  62.8 1.6 %copy-done.4 = f32[1024,512]{1,0:T(8,128)S(1)} copy-done((f32[1024,512]{1,0:T(8,128)S(1)}, f32[1024,512]{1,0:T(8,128)}, u32[]{:S(2)}) %copy-start.4) | copy-done | bytes 2097176
  64.4 2.6 %slab.2 = (f32[1024,512]{1,0:T(8,128)}, bf16[1024,512]{1,0:T(8,128)(2,1)S(1)}, bf16[1024,512]{1,0:T(8,128)(2,1)S(1)}) custom-call(s32[8,4]{1,0:T(8,128)S(1)} %copy.6.allowed_ref, f32[1024,512]{1,0:T(8,128)S(1)} %copy-done.4), custom_call_target="tpu_custom_call" | custom-call | flops 2097152 | bytes 6291456 | tf_op jit(solution)/shard_map/slab/pallas_call | solution.py:36
  67.0 2.4 %collective-permute-start = (f32[1024,512]{1,0:T(8,128)}, f32[1024,512]{1,0:T(8,128)}, u32[]{:S(2)}, u32[]{:S(2)}) collective-permute-start(f32[1024,512]{1,0:T(8,128)} %get-tuple-element.12), channel_id=1, source_target_pairs={{0,1},{1,0},{2,3},{3,2},{4,5},{5,4},{6,7},{7,6},{8,9},{9,8},{10,11... | collective-permute-start | bytes 6291464 | tf_op jit(solution)/shard_map/slab/ppermute | solution.py:152
  69.4 8.8 %all-to-all-done.1 = f32[8,4,8,512]{3,2,1,0:T(8,128)} async-done(((f32[8,4,8,512]{3,2,1,0:T(8,128)}), f32[8,4,8,512]{3,2,1,0:T(8,128)}, u32[]{:S(2)}, u32[]{:S(2)}) %all-to-all-start.1) | async-done | bytes 524320 | tf_op jit(solution)/shard_map/gather_near/all_to_all | solution.py:158
  78.2 3.1 %collective-permute-start.3 = (f32[4,2,4,8,512]{4,3,2,1,0:T(8,128)}, f32[4,2,4,8,512]{4,3,2,1,0:T(8,128)}, u32[]{:S(2)}, u32[]{:S(2)}) collective-permute-start(f32[4,2,4,8,512]{4,3,2,1,0:T(8,128)} %bitcast.6.refs_0_), channel_id=1, source_target_pairs={{0,16},{8,24},{16,0},{24,8},{1,17},{9,25},{17,1},{25,9},{2,18},{10... | collective-permute-start | bytes 1572872 | tf_op jit(solution)/shard_map/gather_y/ppermute | solution.py:140
  81.3 0.0 collective-permute-done.v_ref
  81.3 2.5 %slab.3 = (bf16[1024,512]{1,0:T(8,128)(2,1)S(1)}, bf16[1024,512]{1,0:T(8,128)(2,1)S(1)}) custom-call(f32[1024,512]{1,0:T(8,128)} %collective-permute-done.v_ref), custom_call_target="tpu_custom_call" | custom-call | flops 2097152 | bytes 4194304 | tf_op jit(solution)/shard_map/slab/pallas_call | solution.py:54
  83.8 0.0 copy-start
  83.9 4.1 %own_y.1 = f32[128,1024]{1,0:T(8,128)S(1)} custom-call(s32[1]{0:T(128)} %bitcast.1.core_ref, f32[4,2,4,8,512]{4,3,2,1,0:T(8,128)} %bitcast.6.refs_0_, bf16[1024,512]{1,0:T(8,128)(2,1)S(1)} %get-tuple-element.10.refs_1_.refs_2_, bf16[1024,512]{1,0:T(8,128)(2,1)S(1)} %get-tuple-element.11.refs_2_.refs_3_, ...), custom_call_target="tpu_custom_call" | custom-call | flops 805306368 | bytes 4194304 | tf_op jit(solution)/shard_map/own_y/pallas_call | solution.py:93
  88.0 0.0 copy-done
  88.0 0.0 copy-start.6
  88.0 0.8 copy-done.6
  88.8 4.3 %all-to-all-start.2 = ((f32[4,4,1,8,1024]{4,3,2,1,0:T(8,128)}), f32[4,4,1,8,1024]{4,3,2,1,0:T(8,128)}, u32[]{:S(2)}, u32[]{:S(2)}) async-start(f32[4,4,1,8,1024]{4,3,2,1,0:T(8,128)} %bitcast.15), calls=%async_computation.2 | async-start | bytes 1048576 | tf_op jit(solution)/shard_map/own_y/all_to_all | solution.py:144
  93.1 4.1 %collective-permute-start.1 = (f32[4,2,4,8,512]{4,3,2,1,0:T(8,128)}, f32[4,2,4,8,512]{4,3,2,1,0:T(8,128)}, u32[]{:S(2)}, u32[]{:S(2)}) collective-permute-start(f32[4,2,4,8,512]{4,3,2,1,0:T(8,128)} %bitcast.6.refs_0_), channel_id=1, source_target_pairs={{0,8},{8,16},{16,24},{24,0},{1,9},{9,17},{17,25},{25,1},{2,10},{10... | collective-permute-start | bytes 1572872 | tf_op jit(solution)/shard_map/gather_y/ppermute | solution.py:140
  97.2 1.9 %collective-permute-start.2 = (f32[4,2,4,8,512]{4,3,2,1,0:T(8,128)}, f32[4,2,4,8,512]{4,3,2,1,0:T(8,128)}, u32[]{:S(2)}, u32[]{:S(2)}) collective-permute-start(f32[4,2,4,8,512]{4,3,2,1,0:T(8,128)} %bitcast.6.refs_0_), channel_id=1, source_target_pairs={{0,24},{8,0},{16,8},{24,16},{1,25},{9,1},{17,9},{25,17},{2,26},{10... | collective-permute-start | bytes 1572872 | tf_op jit(solution)/shard_map/gather_y/ppermute | solution.py:140
  99.1 0.0 collective-permute-done.3.refs_0_
  99.1 0.0 copy-start.1
  99.1 1.2 copy-done.1
  100.3 3.7 %across_y.1 = f32[128,1024]{1,0:T(8,128)S(1)} custom-call(s32[1]{0:T(128)} %bitcast.1.core_ref, f32[4,2,4,8,512]{4,3,2,1,0:T(8,128)} %collective-permute-done.3.refs_0_, bf16[1024,512]{1,0:T(8,128)(2,1)S(1)} %get-tuple-element.10.refs_1_.refs_2_, bf16[1024,512]{1,0:T(8,128)(2,1)S(1)} %get-tuple-element.11.refs_2_.refs_3_, ...), custom_call_target="tpu_custom_call" | custom-call | flops 805306368 | bytes 4194304 | tf_op jit(solution)/shard_map/across_y/pallas_call | solution.py:93
  104.1 0.0 copy-start.5
  104.1 0.8 copy-done.5
  104.9 0.0 all-to-all-done.2.own_ref
  104.9 4.8 %all-to-all-start.4 = ((f32[4,4,1,8,1024]{4,3,2,1,0:T(8,128)}), f32[4,4,1,8,1024]{4,3,2,1,0:T(8,128)}, u32[]{:S(2)}, u32[]{:S(2)}) async-start(f32[4,4,1,8,1024]{4,3,2,1,0:T(8,128)} %bitcast.14), calls=%async_computation.4 | async-start | bytes 1048576 | tf_op jit(solution)/shard_map/across_y/all_to_all | solution.py:144
  109.7 0.0 collective-permute-done.1.refs_0_
  109.7 3.7 %collective-permute-done.2.refs_1_ = f32[4,2,4,8,512]{4,3,2,1,0:T(8,128)} collective-permute-done((f32[4,2,4,8,512]{4,3,2,1,0:T(8,128)}, f32[4,2,4,8,512]{4,3,2,1,0:T(8,128)}, u32[]{:S(2)}, u32[]{:S(2)}) %collective-permute-start.2) | collective-permute-done | bytes 524320 | tf_op jit(solution)/shard_map/gather_y/ppermute | solution.py:140
  113.4 0.0 copy-start.2
  113.4 1.2 copy-done.2
  114.6 3.8 %sides_y.1 = f32[256,1024]{1,0:T(8,128)S(1)} custom-call(s32[1]{0:T(128)} %bitcast.1.core_ref, f32[4,2,4,8,512]{4,3,2,1,0:T(8,128)} %collective-permute-done.1.refs_0_, f32[4,2,4,8,512]{4,3,2,1,0:T(8,128)} %collective-permute-done.2.refs_1_, bf16[1024,512]{1,0:T(8,128)(2,1)S(1)} %get-tuple-element.10.refs_1_.refs_2_, ...), custom_call_target="tpu_custom_call" | custom-call | flops 1610612736 | bytes 4194304 | tf_op jit(solution)/shard_map/sides_y/pallas_call | solution.py:93
  118.4 0.0 copy-start.3
  118.4 1.0 copy-done.3
  119.4 0.0 all-to-all-done.4.across_ref
  119.4 4.5 %all-to-all-start.3 = ((f32[4,4,2,8,1024]{4,3,2,1,0:T(8,128)}), f32[4,4,2,8,1024]{4,3,2,1,0:T(8,128)S(1)}, u32[]{:S(2)}, u32[]{:S(2)}) async-start(f32[4,4,2,8,1024]{4,3,2,1,0:T(8,128)} %bitcast.13), calls=%async_computation.3 | async-start | bytes 2097152 | tf_op jit(solution)/shard_map/sides_y/all_to_all | solution.py:144
  123.9 13.0 %all-to-all-done.3.sides_ref = f32[4,4,2,8,1024]{4,3,2,1,0:T(8,128)S(1)} async-done(((f32[4,4,2,8,1024]{4,3,2,1,0:T(8,128)}), f32[4,4,2,8,1024]{4,3,2,1,0:T(8,128)S(1)}, u32[]{:S(2)}, u32[]{:S(2)}) %all-to-all-start.3) | async-done | bytes 1048608 | tf_op jit(solution)/shard_map/sides_y/all_to_all | solution.py:144
  136.8 2.1 %shard_map.37 = f32[4,4,8,1024]{3,2,1,0:T(8,128)} custom-call(s32[1]{0:T(128)} %bitcast.y_ref, f32[4,4,1,8,1024]{4,3,2,1,0:T(8,128)} %all-to-all-done.2.own_ref, f32[4,4,2,8,1024]{4,3,2,1,0:T(8,128)S(1)} %all-to-all-done.3.sides_ref, f32[4,4,1,8,1024]{4,3,2,1,0:T(8,128)} %all-to-all-done.4.across_ref), custom_call_target="tpu_custom_call" | custom-call | flops 524288 | bytes 2621440 | tf_op jit(solution)/shard_map/pallas_call | solution.py:128
  (1 shorter events, 0.0 us)
Async XLA Ops:
  0.0 62.7 %copy-start.7 = (s32[8,4]{0,1:T(4,128)S(1)}, s32[8,4]{0,1:T(4,128)}, u32[]{:S(2)}) copy-start(s32[8,4]{0,1:T(4,128)} %param.5) | copy-start | bytes 388
  57.5 20.7 %all-to-all-start.1 = ((f32[8,4,8,512]{3,2,1,0:T(8,128)}), f32[8,4,8,512]{3,2,1,0:T(8,128)}, u32[]{:S(2)}, u32[]{:S(2)}) async-start(f32[8,4,8,512]{3,2,1,0:T(8,128)} %bitcast.5), calls=%async_computation.1 | async-start | bytes 1048576 | tf_op jit(solution)/shard_map/gather_near/all_to_all | solution.py:158
  62.8 1.6 %copy-start.4 = (f32[1024,512]{1,0:T(8,128)S(1)}, f32[1024,512]{1,0:T(8,128)}, u32[]{:S(2)}) copy-start(f32[1024,512]{1,0:T(8,128)} %v_ref.1) | copy-start | bytes 6291460
  67.0 14.3 %collective-permute-start = (f32[1024,512]{1,0:T(8,128)}, f32[1024,512]{1,0:T(8,128)}, u32[]{:S(2)}, u32[]{:S(2)}) collective-permute-start(f32[1024,512]{1,0:T(8,128)} %get-tuple-element.12), channel_id=1, source_target_pairs={{0,1},{1,0},{2,3},{3,2},{4,5},{5,4},{6,7},{7,6},{8,9},{9,8},{10,11... | collective-permute-start | bytes 6291464 | tf_op jit(solution)/shard_map/slab/ppermute | solution.py:152
  78.2 20.9 %collective-permute-start.3 = (f32[4,2,4,8,512]{4,3,2,1,0:T(8,128)}, f32[4,2,4,8,512]{4,3,2,1,0:T(8,128)}, u32[]{:S(2)}, u32[]{:S(2)}) collective-permute-start(f32[4,2,4,8,512]{4,3,2,1,0:T(8,128)} %bitcast.6.refs_0_), channel_id=1, source_target_pairs={{0,16},{8,24},{16,0},{24,8},{1,17},{9,25},{17,1},{25,9},{2,18},{10... | collective-permute-start | bytes 1572872 | tf_op jit(solution)/shard_map/gather_y/ppermute | solution.py:140
  83.8 4.1 %copy-start = (bf16[1024,512]{1,0:T(8,128)(2,1)}, bf16[1024,512]{1,0:T(8,128)(2,1)S(1)}, u32[]{:S(2)}) copy-start(bf16[1024,512]{1,0:T(8,128)(2,1)S(1)} %get-tuple-element.14.refs_4_.refs_5_) | copy-start | bytes 3145732
  88.0 0.8 copy-start.6
  88.8 16.1 %all-to-all-start.2 = ((f32[4,4,1,8,1024]{4,3,2,1,0:T(8,128)}), f32[4,4,1,8,1024]{4,3,2,1,0:T(8,128)}, u32[]{:S(2)}, u32[]{:S(2)}) async-start(f32[4,4,1,8,1024]{4,3,2,1,0:T(8,128)} %bitcast.15), calls=%async_computation.2 | async-start | bytes 1048576 | tf_op jit(solution)/shard_map/own_y/all_to_all | solution.py:144
  93.1 16.6 %collective-permute-start.1 = (f32[4,2,4,8,512]{4,3,2,1,0:T(8,128)}, f32[4,2,4,8,512]{4,3,2,1,0:T(8,128)}, u32[]{:S(2)}, u32[]{:S(2)}) collective-permute-start(f32[4,2,4,8,512]{4,3,2,1,0:T(8,128)} %bitcast.6.refs_0_), channel_id=1, source_target_pairs={{0,8},{8,16},{16,24},{24,0},{1,9},{9,17},{17,25},{25,1},{2,10},{10... | collective-permute-start | bytes 1572872 | tf_op jit(solution)/shard_map/gather_y/ppermute | solution.py:140
  97.2 16.2 %collective-permute-start.2 = (f32[4,2,4,8,512]{4,3,2,1,0:T(8,128)}, f32[4,2,4,8,512]{4,3,2,1,0:T(8,128)}, u32[]{:S(2)}, u32[]{:S(2)}) collective-permute-start(f32[4,2,4,8,512]{4,3,2,1,0:T(8,128)} %bitcast.6.refs_0_), channel_id=1, source_target_pairs={{0,24},{8,0},{16,8},{24,16},{1,25},{9,1},{17,9},{25,17},{2,26},{10... | collective-permute-start | bytes 1572872 | tf_op jit(solution)/shard_map/gather_y/ppermute | solution.py:140
  99.1 1.2 copy-start.1
  104.1 0.8 copy-start.5
  104.9 14.5 %all-to-all-start.4 = ((f32[4,4,1,8,1024]{4,3,2,1,0:T(8,128)}), f32[4,4,1,8,1024]{4,3,2,1,0:T(8,128)}, u32[]{:S(2)}, u32[]{:S(2)}) async-start(f32[4,4,1,8,1024]{4,3,2,1,0:T(8,128)} %bitcast.14), calls=%async_computation.4 | async-start | bytes 1048576 | tf_op jit(solution)/shard_map/across_y/all_to_all | solution.py:144
  113.4 1.2 copy-start.2
  118.4 1.0 copy-start.3
  119.4 17.4 %all-to-all-start.3 = ((f32[4,4,2,8,1024]{4,3,2,1,0:T(8,128)}), f32[4,4,2,8,1024]{4,3,2,1,0:T(8,128)S(1)}, u32[]{:S(2)}, u32[]{:S(2)}) async-start(f32[4,4,2,8,1024]{4,3,2,1,0:T(8,128)} %bitcast.13), calls=%async_computation.3 | async-start | bytes 2097152 | tf_op jit(solution)/shard_map/sides_y/all_to_all | solution.py:144

commit v3 on v2

v3 whole, which is shorter than its diff:
```python
import functools

import jax
import jax.numpy as jnp
from jax import lax
from jax.experimental import pallas as pl
from jax.experimental.pallas import tpu as pltpu
from jax.sharding import Mesh, PartitionSpec as P

BLK = 128
NT = (((1,), (1,)), ((), ()))
COLS = 256
PARAMS = pltpu.CompilerParams(vmem_limit_bytes=48 * 2**20)
COST = pl.CostEstimate(flops=1, bytes_accessed=1, transcendentals=0)


def split(wide):
    high = wide.astype(jnp.bfloat16)
    return high, (wide - high.astype(jnp.float32)).astype(jnp.bfloat16)


def mask_body(allowed_ref, v_ref, kept_ref):
    step = pl.program_id(0)
    for a in range(COLS // BLK):
        rows = pl.ds(a * BLK, BLK)
        for c in range(v_ref.shape[1] // BLK):
            cols = pl.ds(c * BLK, BLK)
            weight = allowed_ref[step * (COLS // BLK) + a, c].astype(jnp.float32)
            kept_ref[rows, cols] = v_ref[rows, cols] * weight


def masked(integrals, allowed):
    rows, depth = integrals.shape
    block = pl.BlockSpec((COLS, depth), lambda i, allowed: (i, 0))
    return pl.pallas_call(
        mask_body,
        out_shape=jax.ShapeDtypeStruct((rows, depth), jnp.float32),
        grid_spec=pltpu.PrefetchScalarGridSpec(
            num_scalar_prefetch=1, grid=(rows // COLS,), in_specs=[block], out_specs=block
        ),
        compiler_params=PARAMS,
        cost_estimate=COST,
    )(allowed, integrals)


def ladder_body(count, core_ref, *refs):
    t_refs, (own_ref, got_ref, out_ref, t_parts) = refs[:count], refs[count:]
    core = core_ref[0]
    size = 32 * count
    rows = 4 * size

    @pl.when(pl.program_id(0) == 0)
    def _():
        for side in range(2):
            source = core if side == 0 else 1 - core
            for xx in range(4):
                wide = jnp.concatenate([t[low, source, xx] for low in range(4) for t in t_refs], axis=0)
                high, low_part = split(wide)
                t_parts[side, pl.ds(xx * size, size), :] = high
                t_parts[side, pl.ds(rows + xx * size, size), :] = low_part

    def dot(left, right):
        return lax.dot_general(left, right, NT, preferred_element_type=jnp.float32)

    total = None
    for side, v_ref in enumerate((own_ref, got_ref)):
        high, low_part = split(v_ref[...])
        both = dot(t_parts[side], high)
        term = (both[rows:] + dot(t_parts[side, :rows], low_part)) + both[:rows]
        total = term if total is None else total + term
    out_ref[...] = total


def ladder(core, chunks, slabs):
    width, depth = slabs[0].shape
    rows = 128 * len(chunks)
    return pl.pallas_call(
        functools.partial(ladder_body, len(chunks)),
        out_shape=jax.ShapeDtypeStruct((rows, width), jnp.float32),
        grid_spec=pltpu.PrefetchScalarGridSpec(
            num_scalar_prefetch=1,
            grid=(width // COLS,),
            in_specs=[pl.BlockSpec((4, 2, 4, 8, depth), lambda i, core: (0, 0, 0, 0, 0))] * len(chunks)
            + [pl.BlockSpec((COLS, depth), lambda i, core: (i, 0))] * 2,
            out_specs=pl.BlockSpec((rows, COLS), lambda i, core: (0, i)),
            scratch_shapes=[pltpu.VMEM((2, 2 * rows, depth), jnp.bfloat16)],
        ),
        compiler_params=PARAMS,
        cost_estimate=COST,
    )(core, *chunks, *slabs)


def finish_body(y_ref, own_ref, sides_ref, across_ref, out_ref):
    me = y_ref[0]

    def put(offset, part_ref, k):
        place = lax.rem(me + offset, 4)
        out_ref[0, place] = (part_ref[0, 0, k] + part_ref[1, 0, k]) + (part_ref[2, 0, k] + part_ref[3, 0, k])

    put(0, own_ref, 0)
    put(3, sides_ref, 0)
    put(1, sides_ref, 1)
    put(2, across_ref, 0)


def finish(y, own, sides, across):
    def part(count):
        return pl.BlockSpec((4, 1, count, 8, 1024), lambda low, y: (0, low, 0, 0, 0))

    return pl.pallas_call(
        finish_body,
        out_shape=jax.ShapeDtypeStruct((4, 4, 8, 1024), jnp.float32),
        grid_spec=pltpu.PrefetchScalarGridSpec(
            num_scalar_prefetch=1,
            grid=(4,),
            in_specs=[part(1), part(2), part(1)],
            out_specs=pl.BlockSpec((1, 4, 8, 1024), lambda low, y: (low, 0, 0, 0)),
        ),
        compiler_params=PARAMS,
        cost_estimate=COST,
    )(y, own, sides, across)


def around(value, hops):
    return lax.ppermute(value, "y", [(i, (i + hops) % 4) for i in range(4)])


def over_x(partial):
    return lax.all_to_all(partial.reshape(4, 4, -1, 8, 1024), "x", 0, 0)


def per_device(integrals, amplitudes, allowed):
    core = lax.axis_index("core").astype(jnp.int32)[None]
    me = lax.axis_index("y").astype(jnp.int32)[None]
    with jax.named_scope("slab"):
        kept = masked(integrals, allowed)
        slabs = (kept, lax.ppermute(kept, "core", [(0, 1), (1, 0)]))
    with jax.named_scope("gather_far"):
        far = lax.all_to_all(jnp.broadcast_to(amplitudes[None], (8, 8, 512)), "zh", 0, 0)
    with jax.named_scope("gather_near"):
        by_core = far.reshape(1, 4, 2, 8, 512).swapaxes(1, 2)
        spread = jnp.broadcast_to(by_core, (4, 2, 4, 8, 512)).reshape(8, 4, 8, 512)
        near = lax.all_to_all(spread, ("zl", "core"), 0, 0).reshape(4, 2, 4, 8, 512)
    with jax.named_scope("gather_y"):
        below, above = around(near, 1), around(near, 3)
        across = around(near, 2)
    with jax.named_scope("own_y"):
        own = over_x(ladder(core, [near], slabs))
    with jax.named_scope("sides_y"):
        sides = over_x(ladder(core, [below, above], slabs))
    with jax.named_scope("across_y"):
        opposite = over_x(ladder(core, [across], slabs))
    return finish(me, own, sides, opposite).reshape(128, 1024)


def solution(mesh):
    fine = Mesh(mesh.devices.reshape(8, 4, 4, 4, 2), ("zh", "zl", "y", "x", "core"))
    rows, cols = ("zh", "zl", "y"), ("x", "core")
    return jax.shard_map(
        per_device, mesh=fine, in_specs=(P(rows, cols),) * 3, out_specs=P(cols, rows), check_vma=False
    )
```

time: 140 us -> 135 us (0.964)
  local copies, waits for them, and re-layouts: 8.27 us -> 4.07 us
  Pallas kernels: 18.9 us -> 15.9 us
  waiting for transfers between devices: 25.4 us -> 28.2 us
    pallas_call x3 -> x2, Pallas kernels: 7.2 us -> 2.39 us  [the longest x1 1.54 us: finish(): pl.pallas_call(finish_body, out_shape=jax.ShapeDtypeStruct((4, 4, 8, 1024...]
    unnamed x17 -> x7, local copies, waits for them, and re-layouts: 6.67 us -> 2.47 us
    pallas_call x3, Pallas kernels: 11.7 us -> 13.5 us  [ladder(): pl.pallas_call(functools.partial(ladder_body, len(chunks)), out_shape=jax...]
    all_to_all x1, waiting for transfers between devices: 8.77 us -> 10.5 us  [per_device(): near = lax.all_to_all(spread, ('zl', 'core'), 0, 0).reshape(4, 2, 4, 8, 512)]
  transfers between devices with their start and end apart: 8 -> 8, of which waited for: 3 -> 3; matrix products, arithmetic and copies ran while one was open for 0% -> 0% of each run, Pallas kernels for 12% -> 11%
where the time goes in v3:
time: 135 us
  blocking collectives  55.9 us (41%)
  starting transfers between devices  30.4 us (23%)
  waiting for transfers between devices  28.2 us (21%)
  Pallas kernels  15.9 us (12%)
  local copies, waits for them, and re-layouts  4.07 us (3%)
    all_to_all x1, blocking collectives, per_device(): lax.all_to_all(jnp.broadcast_to(amplitudes[None], (8, 8, 512)), 'zh', 0, 0)  55.9 us
    all_to_all x3, starting transfers between devices, over_x(): return lax.all_to_all(partial.reshape(4, 4, -1, 8, 1024), 'x', 0, 0)  13.6 us
    pallas_call x3, Pallas kernels, ladder(): pl.pallas_call(functools.partial(ladder_body, len(chunks)), out_shape=jax...  13.5 us
    all_to_all x3, waiting for transfers between devices, over_x(): return lax.all_to_all(partial.reshape(4, 4, -1, 8, 1024), 'x', 0, 0)  12.9 us
    all_to_all x1, waiting for transfers between devices, per_device(): near = lax.all_to_all(spread, ('zl', 'core'), 0, 0).reshape(4, 2, 4, 8, 512)  10.5 us
    ppermute x3, starting transfers between devices, around(): return lax.ppermute(value, 'y', [(i, (i + hops) % 4) for i in range(4)])  9.13 us
    all_to_all x1, starting transfers between devices, per_device(): near = lax.all_to_all(spread, ('zl', 'core'), 0, 0).reshape(4, 2, 4, 8, 512)  5.19 us
    ppermute x3, waiting for transfers between devices, around(): return lax.ppermute(value, 'y', [(i, (i + hops) % 4) for i in range(4)])  4.86 us
  transfers between devices with their start and end apart: 8, of which 3 were waited for; matrix products, arithmetic and copies ran while one was open for 0% of the time, Pallas kernels for 11%

profile of v3, /device:TPU:24, one launch (start us, length us, event | category | flops | bytes accessed | tf_op | source)
XLA Modules:
  0.0 134.6 jit_solution(1581204160065649162)
XLA Ops:
  0.0 0.0 copy-start.2
  0.0 0.7 broadcast_in_dim.21
  0.7 55.9 %all_to_all.25 = f32[8,8,512]{2,1,0:T(8,128)S(1)} all-to-all(f32[8,8,512]{2,1,0:T(8,128)S(1)} %broadcast_in_dim.21), channel_id=1, replica_groups=mesh['zh'=8,'zl'=4,'y'=4,'x'=4,'core'=2] {'zh'}, dimensions={0} | all-to-all | bytes 262144 | tf_op jit(solution)/shard_map/gather_far/all_to_all | solution.py:139
  56.7 0.9 broadcast_in_dim.23
  57.5 5.2 %all-to-all-start.1 = ((f32[8,4,8,512]{3,2,1,0:T(8,128)}), f32[8,4,8,512]{3,2,1,0:T(8,128)}, u32[]{:S(2)}, u32[]{:S(2)}) async-start(f32[8,4,8,512]{3,2,1,0:T(8,128)} %bitcast.5), calls=%async_computation.1 | async-start | bytes 1048576 | tf_op jit(solution)/shard_map/gather_near/all_to_all | solution.py:143
  62.7 0.0 copy-done.2
  62.7 0.1 copy.6.allowed_ref
  62.8 0.0 copy-start
  62.8 1.6 %copy-done = f32[1024,512]{1,0:T(8,128)S(1)} copy-done((f32[1024,512]{1,0:T(8,128)S(1)}, f32[1024,512]{1,0:T(8,128)}, u32[]{:S(2)}) %copy-start) | copy-done | bytes 2097176
  64.4 0.8 slab.1.refs_1_.refs_2_
  65.3 2.4 %collective-permute-start = (f32[1024,512]{1,0:T(8,128)S(1)}, f32[1024,512]{1,0:T(8,128)}, u32[]{:S(2)}, u32[]{:S(2)}) collective-permute-start(f32[1024,512]{1,0:T(8,128)S(1)} %slab.1.refs_1_.refs_2_), channel_id=1, source_target_pairs={{0,1},{1,0},{2,3},{3,2},{4,5},{5,4},{6,7},{7,6},{8,9},{9,8},{10,11... | collective-permute-start | bytes 6291464 | tf_op jit(solution)/shard_map/slab/ppermute | solution.py:137
  67.7 10.5 %all-to-all-done.1 = f32[8,4,8,512]{3,2,1,0:T(8,128)} async-done(((f32[8,4,8,512]{3,2,1,0:T(8,128)}), f32[8,4,8,512]{3,2,1,0:T(8,128)}, u32[]{:S(2)}, u32[]{:S(2)}) %all-to-all-start.1) | async-done | bytes 524320 | tf_op jit(solution)/shard_map/gather_near/all_to_all | solution.py:143
  78.2 3.1 %collective-permute-start.3 = (f32[4,2,4,8,512]{4,3,2,1,0:T(8,128)}, f32[4,2,4,8,512]{4,3,2,1,0:T(8,128)S(1)}, u32[]{:S(2)}, u32[]{:S(2)}) collective-permute-start(f32[4,2,4,8,512]{4,3,2,1,0:T(8,128)} %bitcast.6.refs_0_), channel_id=1, source_target_pairs={{0,16},{8,24},{16,0},{24,8},{1,17},{9,25},{17,1},{25,9},{2,18},{10... | collective-permute-start | bytes 1572872 | tf_op jit(solution)/shard_map/gather_y/ppermute | solution.py:125
  81.3 0.0 collective-permute-done.refs_2_.refs_3_
  81.3 4.6 %own_y.1 = f32[128,1024]{1,0:T(8,128)} custom-call(s32[1]{0:T(128)} %bitcast.1.core_ref, f32[4,2,4,8,512]{4,3,2,1,0:T(8,128)} %bitcast.6.refs_0_, f32[1024,512]{1,0:T(8,128)S(1)} %slab.1.refs_1_.refs_2_, f32[1024,512]{1,0:T(8,128)} %collective-permute-done.refs_2_.refs_3_), custom_call_target="tpu_custom_call" | custom-call | flops 1 | bytes 1 | tf_op jit(solution)/shard_map/own_y/pallas_call | solution.py:77
  85.9 4.3 %all-to-all-start.2 = ((f32[4,4,1,8,1024]{4,3,2,1,0:T(8,128)}), f32[4,4,1,8,1024]{4,3,2,1,0:T(8,128)S(1)}, u32[]{:S(2)}, u32[]{:S(2)}) async-start(f32[4,4,1,8,1024]{4,3,2,1,0:T(8,128)} %bitcast.7), calls=%async_computation.2 | async-start | bytes 1048576 | tf_op jit(solution)/shard_map/own_y/all_to_all | solution.py:129
  90.2 4.1 %collective-permute-start.1 = (f32[4,2,4,8,512]{4,3,2,1,0:T(8,128)}, f32[4,2,4,8,512]{4,3,2,1,0:T(8,128)}, u32[]{:S(2)}, u32[]{:S(2)}) collective-permute-start(f32[4,2,4,8,512]{4,3,2,1,0:T(8,128)} %bitcast.6.refs_0_), channel_id=1, source_target_pairs={{0,8},{8,16},{16,24},{24,0},{1,9},{9,17},{17,25},{25,1},{2,10},{10... | collective-permute-start | bytes 1572872 | tf_op jit(solution)/shard_map/gather_y/ppermute | solution.py:125
  94.3 1.9 %collective-permute-start.2 = (f32[4,2,4,8,512]{4,3,2,1,0:T(8,128)}, f32[4,2,4,8,512]{4,3,2,1,0:T(8,128)}, u32[]{:S(2)}, u32[]{:S(2)}) collective-permute-start(f32[4,2,4,8,512]{4,3,2,1,0:T(8,128)} %bitcast.6.refs_0_), channel_id=1, source_target_pairs={{0,24},{8,0},{16,8},{24,16},{1,25},{9,1},{17,9},{25,17},{2,26},{10... | collective-permute-start | bytes 1572872 | tf_op jit(solution)/shard_map/gather_y/ppermute | solution.py:125
  96.2 0.0 collective-permute-done.3.refs_0_
  96.2 3.6 %across_y.1 = f32[128,1024]{1,0:T(8,128)S(1)} custom-call(s32[1]{0:T(128)} %bitcast.1.core_ref, f32[4,2,4,8,512]{4,3,2,1,0:T(8,128)S(1)} %collective-permute-done.3.refs_0_, f32[1024,512]{1,0:T(8,128)S(1)} %slab.1.refs_1_.refs_2_, f32[1024,512]{1,0:T(8,128)} %collective-permute-done.refs_2_.refs_3_), custom_call_target="tpu_custom_call" | custom-call | flops 1 | bytes 1 | tf_op jit(solution)/shard_map/across_y/pallas_call | solution.py:77
  99.9 0.0 copy-start.1
  99.9 0.8 copy-done.1
  100.7 0.0 all-to-all-done.2.own_ref
  100.7 4.8 %all-to-all-start.4 = ((f32[4,4,1,8,1024]{4,3,2,1,0:T(8,128)}), f32[4,4,1,8,1024]{4,3,2,1,0:T(8,128)S(1)}, u32[]{:S(2)}, u32[]{:S(2)}) async-start(f32[4,4,1,8,1024]{4,3,2,1,0:T(8,128)} %bitcast.13), calls=%async_computation.4 | async-start | bytes 1048576 | tf_op jit(solution)/shard_map/across_y/all_to_all | solution.py:129
  105.5 0.0 collective-permute-done.1.refs_0_
  105.5 4.9 %collective-permute-done.2.refs_1_ = f32[4,2,4,8,512]{4,3,2,1,0:T(8,128)} collective-permute-done((f32[4,2,4,8,512]{4,3,2,1,0:T(8,128)}, f32[4,2,4,8,512]{4,3,2,1,0:T(8,128)}, u32[]{:S(2)}, u32[]{:S(2)}) %collective-permute-start.2) | collective-permute-done | bytes 524320 | tf_op jit(solution)/shard_map/gather_y/ppermute | solution.py:125
  110.4 5.3 %sides_y.1 = f32[256,1024]{1,0:T(8,128)} custom-call(s32[1]{0:T(128)} %bitcast.1.core_ref, f32[4,2,4,8,512]{4,3,2,1,0:T(8,128)} %collective-permute-done.1.refs_0_, f32[4,2,4,8,512]{4,3,2,1,0:T(8,128)} %collective-permute-done.2.refs_1_, f32[1024,512]{1,0:T(8,128)S(1)} %slab.1.refs_1_.refs_2_, f32[1024,512]{1,0:T(8,128)} %collective-permute-done.refs_2_.refs_3_), custom_call_target="tpu_custom_call" | custom-call | flops 1 | bytes 1 | tf_op jit(solution)/shard_map/sides_y/pallas_call | solution.py:77
  115.7 0.0 all-to-all-done.4.across_ref
  115.7 4.5 %all-to-all-start.3 = ((f32[4,4,2,8,1024]{4,3,2,1,0:T(8,128)}), f32[4,4,2,8,1024]{4,3,2,1,0:T(8,128)S(1)}, u32[]{:S(2)}, u32[]{:S(2)}) async-start(f32[4,4,2,8,1024]{4,3,2,1,0:T(8,128)} %bitcast.8), calls=%async_computation.3 | async-start | bytes 2097152 | tf_op jit(solution)/shard_map/sides_y/all_to_all | solution.py:129
  120.2 12.9 %all-to-all-done.3.sides_ref = f32[4,4,2,8,1024]{4,3,2,1,0:T(8,128)S(1)} async-done(((f32[4,4,2,8,1024]{4,3,2,1,0:T(8,128)}), f32[4,4,2,8,1024]{4,3,2,1,0:T(8,128)S(1)}, u32[]{:S(2)}, u32[]{:S(2)}) %all-to-all-start.3) | async-done | bytes 1048608 | tf_op jit(solution)/shard_map/sides_y/all_to_all | solution.py:129
  133.1 1.5 %shard_map.37 = f32[4,4,8,1024]{3,2,1,0:T(8,128)} custom-call(s32[1]{0:T(128)} %bitcast.y_ref, f32[4,4,1,8,1024]{4,3,2,1,0:T(8,128)S(1)} %all-to-all-done.2.own_ref, f32[4,4,2,8,1024]{4,3,2,1,0:T(8,128)S(1)} %all-to-all-done.3.sides_ref, f32[4,4,1,8,1024]{4,3,2,1,0:T(8,128)S(1)} %all-to-all-done.4.across_ref), custom_call_target="tpu_custom_call" | custom-call | flops 1 | bytes 1 | tf_op jit(solution)/shard_map/pallas_call | solution.py:110
  (1 shorter events, 0.0 us)
Async XLA Ops:
  0.0 62.7 %copy-start.2 = (s32[8,4]{0,1:T(4,128)S(1)}, s32[8,4]{0,1:T(4,128)}, u32[]{:S(2)}) copy-start(s32[8,4]{0,1:T(4,128)} %param.5) | copy-start | bytes 388
  57.5 20.7 %all-to-all-start.1 = ((f32[8,4,8,512]{3,2,1,0:T(8,128)}), f32[8,4,8,512]{3,2,1,0:T(8,128)}, u32[]{:S(2)}, u32[]{:S(2)}) async-start(f32[8,4,8,512]{3,2,1,0:T(8,128)} %bitcast.5), calls=%async_computation.1 | async-start | bytes 1048576 | tf_op jit(solution)/shard_map/gather_near/all_to_all | solution.py:143
  62.8 1.6 %copy-start = (f32[1024,512]{1,0:T(8,128)S(1)}, f32[1024,512]{1,0:T(8,128)}, u32[]{:S(2)}) copy-start(f32[1024,512]{1,0:T(8,128)} %v_ref.1) | copy-start | bytes 6291460
  65.3 16.1 %collective-permute-start = (f32[1024,512]{1,0:T(8,128)S(1)}, f32[1024,512]{1,0:T(8,128)}, u32[]{:S(2)}, u32[]{:S(2)}) collective-permute-start(f32[1024,512]{1,0:T(8,128)S(1)} %slab.1.refs_1_.refs_2_), channel_id=1, source_target_pairs={{0,1},{1,0},{2,3},{3,2},{4,5},{5,4},{6,7},{7,6},{8,9},{9,8},{10,11... | collective-permute-start | bytes 6291464 | tf_op jit(solution)/shard_map/slab/ppermute | solution.py:137
  78.2 18.1 %collective-permute-start.3 = (f32[4,2,4,8,512]{4,3,2,1,0:T(8,128)}, f32[4,2,4,8,512]{4,3,2,1,0:T(8,128)S(1)}, u32[]{:S(2)}, u32[]{:S(2)}) collective-permute-start(f32[4,2,4,8,512]{4,3,2,1,0:T(8,128)} %bitcast.6.refs_0_), channel_id=1, source_target_pairs={{0,16},{8,24},{16,0},{24,8},{1,17},{9,25},{17,1},{25,9},{2,18},{10... | collective-permute-start | bytes 1572872 | tf_op jit(solution)/shard_map/gather_y/ppermute | solution.py:125
  85.9 14.8 %all-to-all-start.2 = ((f32[4,4,1,8,1024]{4,3,2,1,0:T(8,128)}), f32[4,4,1,8,1024]{4,3,2,1,0:T(8,128)S(1)}, u32[]{:S(2)}, u32[]{:S(2)}) async-start(f32[4,4,1,8,1024]{4,3,2,1,0:T(8,128)} %bitcast.7), calls=%async_computation.2 | async-start | bytes 1048576 | tf_op jit(solution)/shard_map/own_y/all_to_all | solution.py:129
  90.2 15.3 %collective-permute-start.1 = (f32[4,2,4,8,512]{4,3,2,1,0:T(8,128)}, f32[4,2,4,8,512]{4,3,2,1,0:T(8,128)}, u32[]{:S(2)}, u32[]{:S(2)}) collective-permute-start(f32[4,2,4,8,512]{4,3,2,1,0:T(8,128)} %bitcast.6.refs_0_), channel_id=1, source_target_pairs={{0,8},{8,16},{16,24},{24,0},{1,9},{9,17},{17,25},{25,1},{2,10},{10... | collective-permute-start | bytes 1572872 | tf_op jit(solution)/shard_map/gather_y/ppermute | solution.py:125
  94.3 16.1 %collective-permute-start.2 = (f32[4,2,4,8,512]{4,3,2,1,0:T(8,128)}, f32[4,2,4,8,512]{4,3,2,1,0:T(8,128)}, u32[]{:S(2)}, u32[]{:S(2)}) collective-permute-start(f32[4,2,4,8,512]{4,3,2,1,0:T(8,128)} %bitcast.6.refs_0_), channel_id=1, source_target_pairs={{0,24},{8,0},{16,8},{24,16},{1,25},{9,1},{17,9},{25,17},{2,26},{10... | collective-permute-start | bytes 1572872 | tf_op jit(solution)/shard_map/gather_y/ppermute | solution.py:125
  99.9 0.8 copy-start.1
  100.7 15.0 %all-to-all-start.4 = ((f32[4,4,1,8,1024]{4,3,2,1,0:T(8,128)}), f32[4,4,1,8,1024]{4,3,2,1,0:T(8,128)S(1)}, u32[]{:S(2)}, u32[]{:S(2)}) async-start(f32[4,4,1,8,1024]{4,3,2,1,0:T(8,128)} %bitcast.13), calls=%async_computation.4 | async-start | bytes 1048576 | tf_op jit(solution)/shard_map/across_y/all_to_all | solution.py:129
  115.7 17.4 %all-to-all-start.3 = ((f32[4,4,2,8,1024]{4,3,2,1,0:T(8,128)}), f32[4,4,2,8,1024]{4,3,2,1,0:T(8,128)S(1)}, u32[]{:S(2)}, u32[]{:S(2)}) async-start(f32[4,4,2,8,1024]{4,3,2,1,0:T(8,128)} %bitcast.8), calls=%async_computation.3 | async-start | bytes 2097152 | tf_op jit(solution)/shard_map/sides_y/all_to_all | solution.py:129

commit v4 on v3

--- a/solution.py
+++ b/solution.py
@@ -44,7 +44,8 @@
 
 
 def ladder_body(count, core_ref, *refs):
-    t_refs, (own_ref, got_ref, out_ref, t_parts) = refs[:count], refs[count:]
+    *t_refs, own_ref, got_ref, _, out_ref, t_parts = refs
+    span = 4 * count // len(t_refs)
     core = core_ref[0]
     size = 32 * count
     rows = 4 * size
@@ -54,7 +55,10 @@
         for side in range(2):
             source = core if side == 0 else 1 - core
             for xx in range(4):
-                wide = jnp.concatenate([t[low, source, xx] for low in range(4) for t in t_refs], axis=0)
+                rows_of = [
+                    t_refs[y * (4 // span) + low // span][low % span, source, xx] for low in range(4) for y in range(count)
+                ]
+                wide = jnp.concatenate(rows_of, axis=0)
                 high, low_part = split(wide)
                 t_parts[side, pl.ds(xx * size, size), :] = high
                 t_parts[side, pl.ds(rows + xx * size, size), :] = low_part
@@ -71,23 +75,26 @@
     out_ref[...] = total
 
 
-def ladder(core, chunks, slabs):
+def ladder(core, chunks, slabs, after):
     width, depth = slabs[0].shape
-    rows = 128 * len(chunks)
+    span = chunks[0].shape[0]
+    count = len(chunks) * span // 4
+    rows = 128 * count
     return pl.pallas_call(
-        functools.partial(ladder_body, len(chunks)),
+        functools.partial(ladder_body, count),
         out_shape=jax.ShapeDtypeStruct((rows, width), jnp.float32),
         grid_spec=pltpu.PrefetchScalarGridSpec(
             num_scalar_prefetch=1,
             grid=(width // COLS,),
-            in_specs=[pl.BlockSpec((4, 2, 4, 8, depth), lambda i, core: (0, 0, 0, 0, 0))] * len(chunks)
-            + [pl.BlockSpec((COLS, depth), lambda i, core: (i, 0))] * 2,
+            in_specs=[pl.BlockSpec((span, 2, 4, 8, depth), lambda i, core: (0, 0, 0, 0, 0))] * len(chunks)
+            + [pl.BlockSpec((COLS, depth), lambda i, core: (i, 0))] * 2
+            + [pl.BlockSpec(memory_space=pl.ANY)],
             out_specs=pl.BlockSpec((rows, COLS), lambda i, core: (0, i)),
             scratch_shapes=[pltpu.VMEM((2, 2 * rows, depth), jnp.bfloat16)],
         ),
         compiler_params=PARAMS,
         cost_estimate=COST,
-    )(core, *chunks, *slabs)
+    )(core, *chunks, *slabs, after)
 
 
 def finish_body(y_ref, own_ref, sides_ref, across_ref, out_ref):
@@ -143,14 +150,15 @@
         near = lax.all_to_all(spread, ("zl", "core"), 0, 0).reshape(4, 2, 4, 8, 512)
     with jax.named_scope("gather_y"):
         below, above = around(near, 1), around(near, 3)
-        across = around(near, 2)
+        across = [around(above[:2], 3), around(below[2:], 1)]
     with jax.named_scope("own_y"):
-        own = over_x(ladder(core, [near], slabs))
+        own = ladder(core, [near], slabs, near)
     with jax.named_scope("sides_y"):
-        sides = over_x(ladder(core, [below, above], slabs))
+        sides = ladder(core, [below, above], slabs, own)
     with jax.named_scope("across_y"):
-        opposite = over_x(ladder(core, [across], slabs))
-    return finish(me, own, sides, opposite).reshape(128, 1024)
+        opposite = ladder(core, across, slabs, sides)
+    with jax.named_scope("reduce_x"):
+        return finish(me, over_x(own), over_x(sides), over_x(opposite)).reshape(128, 1024)
 
 
 def solution(mesh):

time: 135 us -> 144 us (1.067)
  blocking collectives: 55.9 us -> 68.1 us
  waiting for transfers between devices: 28.2 us -> 23.5 us
    all_to_all x0 -> x1, blocking collectives: none -> 12.2 us  [over_x(): return lax.all_to_all(partial.reshape(4, 4, -1, 8, 1024), 'x', 0, 0)]
    all_to_all x3 -> x2, starting transfers between devices: 13.6 us -> 7.81 us  [over_x(): return lax.all_to_all(partial.reshape(4, 4, -1, 8, 1024), 'x', 0, 0)]
    ppermute x3 -> x4, starting transfers between devices: 9.13 us -> 14.1 us  [around(): return lax.ppermute(value, 'y', [(i, (i + hops) % 4) for i in range(4)])]
    ppermute x3 -> x4, waiting for transfers between devices: 4.86 us -> 0.89 us  [around(): return lax.ppermute(value, 'y', [(i, (i + hops) % 4) for i in range(4)])]
    slice x0 -> x2, local copies, waits for them, and re-layouts: none -> 1.94 us  [per_device(): across = [around(above[:2], 3), around(below[2:], 1)]]
    all_to_all x3 -> x2, waiting for transfers between devices: 12.9 us -> 12.3 us  [over_x(): return lax.all_to_all(partial.reshape(4, 4, -1, 8, 1024), 'x', 0, 0)]
  transfers between devices with their start and end apart: 8 -> 8, of which waited for: 3 -> 3; matrix products, arithmetic and copies ran while one was open for 0% -> 1% of each run, Pallas kernels for 11% -> 10%
where the time goes in v4:
time: 144 us; the launch traced here: 142 us
  blocking collectives  68.1 us (47%)
  starting transfers between devices  29.5 us (20%)
  waiting for transfers between devices  23.5 us (16%)
  Pallas kernels  15.7 us (11%)
  local copies, waits for them, and re-layouts  5.22 us (4%)
    all_to_all x1, blocking collectives, per_device(): lax.all_to_all(jnp.broadcast_to(amplitudes[None], (8, 8, 512)), 'zh', 0, 0)  55.9 us
    ppermute x4, starting transfers between devices, around(): return lax.ppermute(value, 'y', [(i, (i + hops) % 4) for i in range(4)])  14.1 us
    pallas_call x3, Pallas kernels, ladder(): pl.pallas_call(functools.partial(ladder_body, count), out_shape=jax.Shape...  13.4 us
    all_to_all x2, waiting for transfers between devices, over_x(): return lax.all_to_all(partial.reshape(4, 4, -1, 8, 1024), 'x', 0, 0)  12.3 us
    all_to_all x1, blocking collectives, over_x(): return lax.all_to_all(partial.reshape(4, 4, -1, 8, 1024), 'x', 0, 0)  12.2 us
    all_to_all x1, waiting for transfers between devices, per_device(): near = lax.all_to_all(spread, ('zl', 'core'), 0, 0).reshape(4, 2, 4, 8, 512)  10.4 us
    all_to_all x2, starting transfers between devices, over_x(): return lax.all_to_all(partial.reshape(4, 4, -1, 8, 1024), 'x', 0, 0)  7.81 us
    all_to_all x1, starting transfers between devices, per_device(): near = lax.all_to_all(spread, ('zl', 'core'), 0, 0).reshape(4, 2, 4, 8, 512)  5.19 us
  transfers between devices with their start and end apart: 8, of which 3 were waited for; matrix products, arithmetic and copies ran while one was open for 1% of the time, Pallas kernels for 10%

profile of v4, /device:TPU:24, one launch (start us, length us, event | category | flops | bytes accessed | tf_op | source)
XLA Modules:
  0.0 142.2 jit_solution(10914409373502526953)
XLA Ops:
  0.0 0.0 copy-start.1
  0.0 0.7 broadcast_in_dim.21
  0.7 55.9 %all_to_all.25 = f32[8,8,512]{2,1,0:T(8,128)S(1)} all-to-all(f32[8,8,512]{2,1,0:T(8,128)S(1)} %broadcast_in_dim.21), channel_id=1, replica_groups=mesh['zh'=8,'zl'=4,'y'=4,'x'=4,'core'=2] {'zh'}, dimensions={0} | all-to-all | bytes 262144 | tf_op jit(solution)/shard_map/gather_far/all_to_all | solution.py:146
  56.7 0.9 broadcast_in_dim.23
  57.5 5.2 %all-to-all-start.1 = ((f32[8,4,8,512]{3,2,1,0:T(8,128)}), f32[8,4,8,512]{3,2,1,0:T(8,128)S(1)}, u32[]{:S(2)}, u32[]{:S(2)}) async-start(f32[8,4,8,512]{3,2,1,0:T(8,128)} %bitcast.5), calls=%async_computation.1 | async-start | bytes 1048576 | tf_op jit(solution)/shard_map/gather_near/all_to_all | solution.py:150
  62.7 0.0 copy-done.1
  62.7 0.1 copy.6.allowed_ref
  62.8 0.0 copy-start
  62.8 1.6 %copy-done = f32[1024,512]{1,0:T(8,128)S(1)} copy-done((f32[1024,512]{1,0:T(8,128)S(1)}, f32[1024,512]{1,0:T(8,128)}, u32[]{:S(2)}) %copy-start) | copy-done | bytes 2097176
  64.4 0.8 slab.1.refs_1_.refs_2_
  65.3 2.4 %collective-permute-start = (f32[1024,512]{1,0:T(8,128)S(1)}, f32[1024,512]{1,0:T(8,128)}, u32[]{:S(2)}, u32[]{:S(2)}) collective-permute-start(f32[1024,512]{1,0:T(8,128)S(1)} %slab.1.refs_1_.refs_2_), channel_id=1, source_target_pairs={{0,1},{1,0},{2,3},{3,2},{4,5},{5,4},{6,7},{7,6},{8,9},{9,8},{10,11... | collective-permute-start | bytes 6291464 | tf_op jit(solution)/shard_map/slab/ppermute | solution.py:144
  67.7 10.4 %all-to-all-done.1 = f32[8,4,8,512]{3,2,1,0:T(8,128)S(1)} async-done(((f32[8,4,8,512]{3,2,1,0:T(8,128)}), f32[8,4,8,512]{3,2,1,0:T(8,128)S(1)}, u32[]{:S(2)}, u32[]{:S(2)}) %all-to-all-start.1) | async-done | bytes 524320 | tf_op jit(solution)/shard_map/gather_near/all_to_all | solution.py:150
  78.1 2.6 %collective-permute-start.2 = (f32[4,2,4,8,512]{4,3,2,1,0:T(8,128)S(1)}, f32[4,2,4,8,512]{4,3,2,1,0:T(8,128)}, u32[]{:S(2)}, u32[]{:S(2)}) collective-permute-start(f32[4,2,4,8,512]{4,3,2,1,0:T(8,128)S(1)} %bitcast.13), channel_id=1, source_target_pairs={{0,24},{8,0},{16,8},{24,16},{1,25},{9,1},{17,9},{25,17},{2,26},{10... | collective-permute-start | bytes 1572872 | tf_op jit(solution)/shard_map/gather_y/ppermute | solution.py:132
  80.7 4.4 %collective-permute-start.1 = (f32[4,2,4,8,512]{4,3,2,1,0:T(8,128)S(1)}, f32[4,2,4,8,512]{4,3,2,1,0:T(8,128)}, u32[]{:S(2)}, u32[]{:S(2)}) collective-permute-start(f32[4,2,4,8,512]{4,3,2,1,0:T(8,128)S(1)} %bitcast.14), channel_id=1, source_target_pairs={{0,8},{8,16},{16,24},{24,0},{1,9},{9,17},{17,25},{25,1},{2,10},{10... | collective-permute-start | bytes 1572872 | tf_op jit(solution)/shard_map/gather_y/ppermute | solution.py:132
  85.1 0.0 collective-permute-done.refs_2_.refs_3_
  85.2 4.4 %own_y.1.refs_4_ = f32[128,1024]{1,0:T(8,128)} custom-call(s32[1]{0:T(128)} %bitcast.1.core_ref, f32[4,2,4,8,512]{4,3,2,1,0:T(8,128)S(1)} %bitcast.15, f32[1024,512]{1,0:T(8,128)S(1)} %slab.1.refs_1_.refs_2_, f32[1024,512]{1,0:T(8,128)} %collective-permute-done.refs_2_.refs_3_, f32[4,2,4,8,512]{4,3,2,1,0:T(8,128)S(1)} %bitcast.16), custom_call_target="tpu_custom_call" | custom-call | flops 1 | bytes 1 | tf_op jit(solution)/shard_map/own_y/pallas_call | solution.py:83
  89.6 4.3 %all-to-all-start.2 = ((f32[4,4,1,8,1024]{4,3,2,1,0:T(8,128)}), f32[4,4,1,8,1024]{4,3,2,1,0:T(8,128)S(1)}, u32[]{:S(2)}, u32[]{:S(2)}) async-start(f32[4,4,1,8,1024]{4,3,2,1,0:T(8,128)} %bitcast.7), calls=%async_computation.2 | async-start | bytes 1048576 | tf_op jit(solution)/shard_map/reduce_x/all_to_all | solution.py:136
  93.9 0.9 collective-permute-done.2.refs_1_
  94.8 1.0 slice.8
  95.7 1.9 %collective-permute-start.3 = (f32[2,2,4,8,512]{4,3,2,1,0:T(8,128)S(1)}, f32[2,2,4,8,512]{4,3,2,1,0:T(8,128)S(1)}, u32[]{:S(2)}, u32[]{:S(2)}) collective-permute-start(f32[2,2,4,8,512]{4,3,2,1,0:T(8,128)S(1)} %slice.8), channel_id=1, source_target_pairs={{0,24},{8,0},{16,8},{24,16},{1,25},{9,1},{17,9},{25,17},{2,26},{10... | collective-permute-start | bytes 786440 | tf_op jit(solution)/shard_map/gather_y/ppermute | solution.py:132
  97.7 0.0 collective-permute-done.1.refs_0_
  97.7 1.0 slice.9
  98.6 5.1 %collective-permute-start.4 = (f32[2,2,4,8,512]{4,3,2,1,0:T(8,128)S(1)}, f32[2,2,4,8,512]{4,3,2,1,0:T(8,128)S(1)}, u32[]{:S(2)}, u32[]{:S(2)}) collective-permute-start(f32[2,2,4,8,512]{4,3,2,1,0:T(8,128)S(1)} %slice.9), channel_id=1, source_target_pairs={{0,8},{8,16},{16,24},{24,0},{1,9},{9,17},{17,25},{25,1},{2,10},{10... | collective-permute-start | bytes 786440 | tf_op jit(solution)/shard_map/gather_y/ppermute | solution.py:132
  103.8 5.3 %sides_y.1.refs_4_ = f32[256,1024]{1,0:T(8,128)} custom-call(s32[1]{0:T(128)} %bitcast.1.core_ref, f32[4,2,4,8,512]{4,3,2,1,0:T(8,128)} %collective-permute-done.1.refs_0_, f32[4,2,4,8,512]{4,3,2,1,0:T(8,128)} %collective-permute-done.2.refs_1_, f32[1024,512]{1,0:T(8,128)S(1)} %slab.1.refs_1_.refs_2_, f32[1024,512]{1,0:T(8,128)} %collective-permute-done.refs_2_.refs_3_, ...), custom_call_target="tpu_custom_call" | custom-call | flops 1 | bytes 1 | tf_op jit(solution)/shard_map/sides_y/pallas_call | solution.py:83
  109.1 0.0 collective-permute-done.3.refs_0_
  109.1 0.0 collective-permute-done.4.refs_1_
  109.1 3.6 %across_y.1 = f32[128,1024]{1,0:T(8,128)S(1)} custom-call(s32[1]{0:T(128)} %bitcast.1.core_ref, f32[2,2,4,8,512]{4,3,2,1,0:T(8,128)S(1)} %collective-permute-done.3.refs_0_, f32[2,2,4,8,512]{4,3,2,1,0:T(8,128)S(1)} %collective-permute-done.4.refs_1_, f32[1024,512]{1,0:T(8,128)S(1)} %slab.1.refs_1_.refs_2_, f32[1024,512]{1,0:T(8,128)} %collective-permute-done.refs_2_.refs_3_, ...), custom_call_target="tpu_custom_call" | custom-call | flops 1 | bytes 1 | tf_op jit(solution)/shard_map/across_y/pallas_call | solution.py:83
  112.7 0.0 all-to-all-done.2.own_ref
  112.7 12.2 %all_to_all.26.across_ref = f32[4,4,1,8,1024]{4,3,2,1,0:T(8,128)S(1)} all-to-all(f32[4,4,1,8,1024]{4,3,2,1,0:T(8,128)S(1)} %bitcast.17), channel_id=1, replica_groups=mesh['zh'=8,'zl'=4,'y'=4,'x'=4,'core'=2] {'x'}, dimensions={0} | all-to-all | bytes 1048576 | tf_op jit(solution)/shard_map/reduce_x/all_to_all | solution.py:136
  124.9 3.5 %all-to-all-start.3 = ((f32[4,4,2,8,1024]{4,3,2,1,0:T(8,128)}), f32[4,4,2,8,1024]{4,3,2,1,0:T(8,128)S(1)}, u32[]{:S(2)}, u32[]{:S(2)}) async-start(f32[4,4,2,8,1024]{4,3,2,1,0:T(8,128)} %bitcast.8), calls=%async_computation.3 | async-start | bytes 2097152 | tf_op jit(solution)/shard_map/reduce_x/all_to_all | solution.py:136
  128.5 12.2 %all-to-all-done.3.sides_ref = f32[4,4,2,8,1024]{4,3,2,1,0:T(8,128)S(1)} async-done(((f32[4,4,2,8,1024]{4,3,2,1,0:T(8,128)}), f32[4,4,2,8,1024]{4,3,2,1,0:T(8,128)S(1)}, u32[]{:S(2)}, u32[]{:S(2)}) %all-to-all-start.3) | async-done | bytes 1048608 | tf_op jit(solution)/shard_map/reduce_x/all_to_all | solution.py:136
  140.7 1.5 %reduce_x.1 = f32[4,4,8,1024]{3,2,1,0:T(8,128)} custom-call(s32[1]{0:T(128)} %bitcast.y_ref, f32[4,4,1,8,1024]{4,3,2,1,0:T(8,128)S(1)} %all-to-all-done.2.own_ref, f32[4,4,2,8,1024]{4,3,2,1,0:T(8,128)S(1)} %all-to-all-done.3.sides_ref, f32[4,4,1,8,1024]{4,3,2,1,0:T(8,128)S(1)} %all_to_all.26.across_ref), custom_call_target="tpu_custom_call" | custom-call | flops 1 | bytes 1 | tf_op jit(solution)/shard_map/reduce_x/pallas_call | solution.py:117
  (1 shorter events, 0.0 us)
Async XLA Ops:
  0.0 62.7 %copy-start.1 = (s32[8,4]{0,1:T(4,128)S(1)}, s32[8,4]{0,1:T(4,128)}, u32[]{:S(2)}) copy-start(s32[8,4]{0,1:T(4,128)} %param.5) | copy-start | bytes 388
  57.5 20.5 %all-to-all-start.1 = ((f32[8,4,8,512]{3,2,1,0:T(8,128)}), f32[8,4,8,512]{3,2,1,0:T(8,128)S(1)}, u32[]{:S(2)}, u32[]{:S(2)}) async-start(f32[8,4,8,512]{3,2,1,0:T(8,128)} %bitcast.5), calls=%async_computation.1 | async-start | bytes 1048576 | tf_op jit(solution)/shard_map/gather_near/all_to_all | solution.py:150
  62.8 1.6 %copy-start = (f32[1024,512]{1,0:T(8,128)S(1)}, f32[1024,512]{1,0:T(8,128)}, u32[]{:S(2)}) copy-start(f32[1024,512]{1,0:T(8,128)} %v_ref.1) | copy-start | bytes 6291460
  65.3 19.9 %collective-permute-start = (f32[1024,512]{1,0:T(8,128)S(1)}, f32[1024,512]{1,0:T(8,128)}, u32[]{:S(2)}, u32[]{:S(2)}) collective-permute-start(f32[1024,512]{1,0:T(8,128)S(1)} %slab.1.refs_1_.refs_2_), channel_id=1, source_target_pairs={{0,1},{1,0},{2,3},{3,2},{4,5},{5,4},{6,7},{7,6},{8,9},{9,8},{10,11... | collective-permute-start | bytes 6291464 | tf_op jit(solution)/shard_map/slab/ppermute | solution.py:144
  78.1 16.7 %collective-permute-start.2 = (f32[4,2,4,8,512]{4,3,2,1,0:T(8,128)S(1)}, f32[4,2,4,8,512]{4,3,2,1,0:T(8,128)}, u32[]{:S(2)}, u32[]{:S(2)}) collective-permute-start(f32[4,2,4,8,512]{4,3,2,1,0:T(8,128)S(1)} %bitcast.13), channel_id=1, source_target_pairs={{0,24},{8,0},{16,8},{24,16},{1,25},{9,1},{17,9},{25,17},{2,26},{10... | collective-permute-start | bytes 1572872 | tf_op jit(solution)/shard_map/gather_y/ppermute | solution.py:132
  80.7 16.9 %collective-permute-start.1 = (f32[4,2,4,8,512]{4,3,2,1,0:T(8,128)S(1)}, f32[4,2,4,8,512]{4,3,2,1,0:T(8,128)}, u32[]{:S(2)}, u32[]{:S(2)}) collective-permute-start(f32[4,2,4,8,512]{4,3,2,1,0:T(8,128)S(1)} %bitcast.14), channel_id=1, source_target_pairs={{0,8},{8,16},{16,24},{24,0},{1,9},{9,17},{17,25},{25,1},{2,10},{10... | collective-permute-start | bytes 1572872 | tf_op jit(solution)/shard_map/gather_y/ppermute | solution.py:132
  89.6 23.2 %all-to-all-start.2 = ((f32[4,4,1,8,1024]{4,3,2,1,0:T(8,128)}), f32[4,4,1,8,1024]{4,3,2,1,0:T(8,128)S(1)}, u32[]{:S(2)}, u32[]{:S(2)}) async-start(f32[4,4,1,8,1024]{4,3,2,1,0:T(8,128)} %bitcast.7), calls=%async_computation.2 | async-start | bytes 1048576 | tf_op jit(solution)/shard_map/reduce_x/all_to_all | solution.py:136
  95.7 13.4 %collective-permute-start.3 = (f32[2,2,4,8,512]{4,3,2,1,0:T(8,128)S(1)}, f32[2,2,4,8,512]{4,3,2,1,0:T(8,128)S(1)}, u32[]{:S(2)}, u32[]{:S(2)}) collective-permute-start(f32[2,2,4,8,512]{4,3,2,1,0:T(8,128)S(1)} %slice.8), channel_id=1, source_target_pairs={{0,24},{8,0},{16,8},{24,16},{1,25},{9,1},{17,9},{25,17},{2,26},{10... | collective-permute-start | bytes 786440 | tf_op jit(solution)/shard_map/gather_y/ppermute | solution.py:132
  98.6 10.5 %collective-permute-start.4 = (f32[2,2,4,8,512]{4,3,2,1,0:T(8,128)S(1)}, f32[2,2,4,8,512]{4,3,2,1,0:T(8,128)S(1)}, u32[]{:S(2)}, u32[]{:S(2)}) collective-permute-start(f32[2,2,4,8,512]{4,3,2,1,0:T(8,128)S(1)} %slice.9), channel_id=1, source_target_pairs={{0,8},{8,16},{16,24},{24,0},{1,9},{9,17},{17,25},{25,1},{2,10},{10... | collective-permute-start | bytes 786440 | tf_op jit(solution)/shard_map/gather_y/ppermute | solution.py:132
  124.9 15.8 %all-to-all-start.3 = ((f32[4,4,2,8,1024]{4,3,2,1,0:T(8,128)}), f32[4,4,2,8,1024]{4,3,2,1,0:T(8,128)S(1)}, u32[]{:S(2)}, u32[]{:S(2)}) async-start(f32[4,4,2,8,1024]{4,3,2,1,0:T(8,128)} %bitcast.8), calls=%async_computation.3 | async-start | bytes 2097152 | tf_op jit(solution)/shard_map/reduce_x/all_to_all | solution.py:136

commit v5 on v4

--- a/solution.py
+++ b/solution.py
@@ -45,7 +45,6 @@
 
 def ladder_body(count, core_ref, *refs):
     *t_refs, own_ref, got_ref, _, out_ref, t_parts = refs
-    span = 4 * count // len(t_refs)
     core = core_ref[0]
     size = 32 * count
     rows = 4 * size
@@ -55,10 +54,7 @@
         for side in range(2):
             source = core if side == 0 else 1 - core
             for xx in range(4):
-                rows_of = [
-                    t_refs[y * (4 // span) + low // span][low % span, source, xx] for low in range(4) for y in range(count)
-                ]
-                wide = jnp.concatenate(rows_of, axis=0)
+                wide = jnp.concatenate([t[low, source, xx] for low in range(4) for t in t_refs], axis=0)
                 high, low_part = split(wide)
                 t_parts[side, pl.ds(xx * size, size), :] = high
                 t_parts[side, pl.ds(rows + xx * size, size), :] = low_part
@@ -77,8 +73,7 @@
 
 def ladder(core, chunks, slabs, after):
     width, depth = slabs[0].shape
-    span = chunks[0].shape[0]
-    count = len(chunks) * span // 4
+    count = len(chunks)
     rows = 128 * count
     return pl.pallas_call(
         functools.partial(ladder_body, count),
@@ -86,14 +81,14 @@
         grid_spec=pltpu.PrefetchScalarGridSpec(
             num_scalar_prefetch=1,
             grid=(width // COLS,),
-            in_specs=[pl.BlockSpec((span, 2, 4, 8, depth), lambda i, core: (0, 0, 0, 0, 0))] * len(chunks)
+            in_specs=[pl.BlockSpec((4, 2, 4, 8, depth), lambda i, core: (0, 0, 0, 0, 0))] * len(chunks)
             + [pl.BlockSpec((COLS, depth), lambda i, core: (i, 0))] * 2
             + [pl.BlockSpec(memory_space=pl.ANY)],
             out_specs=pl.BlockSpec((rows, COLS), lambda i, core: (0, i)),
             scratch_shapes=[pltpu.VMEM((2, 2 * rows, depth), jnp.bfloat16)],
         ),
         compiler_params=PARAMS,
-        cost_estimate=COST,
+        cost_estimate=pl.CostEstimate(flops=12 * rows * width * depth, bytes_accessed=16 * 2**20, transcendentals=0),
     )(core, *chunks, *slabs, after)
 
 
@@ -150,13 +145,13 @@
         near = lax.all_to_all(spread, ("zl", "core"), 0, 0).reshape(4, 2, 4, 8, 512)
     with jax.named_scope("gather_y"):
         below, above = around(near, 1), around(near, 3)
-        across = [around(above[:2], 3), around(below[2:], 1)]
+        across = around(near, 2)
     with jax.named_scope("own_y"):
         own = ladder(core, [near], slabs, near)
     with jax.named_scope("sides_y"):
         sides = ladder(core, [below, above], slabs, own)
     with jax.named_scope("across_y"):
-        opposite = ladder(core, across, slabs, sides)
+        opposite = ladder(core, [across], slabs, sides)
     with jax.named_scope("reduce_x"):
         return finish(me, over_x(own), over_x(sides), over_x(opposite)).reshape(128, 1024)
 

time: 144 us -> 149 us (1.035)
  the two profiles are of different devices: /device:TPU:24 before, /device:TPU:2 now
where the time goes in v5:
time: 149 us; the launch traced here: 148 us
  blocking collectives  68.6 us (46%)
  waiting for transfers between devices  32.2 us (22%)
  starting transfers between devices  28.3 us (19%)
  Pallas kernels  15.9 us (11%)
  local copies, waits for them, and re-layouts  3.28 us (2%)
    all_to_all x1, blocking collectives, per_device(): lax.all_to_all(jnp.broadcast_to(amplitudes[None], (8, 8, 512)), 'zh', 0, 0)  55.9 us
    pallas_call x3, Pallas kernels, ladder(): pl.pallas_call(functools.partial(ladder_body, count), out_shape=jax.Shape...  13.5 us
    all_to_all x1, blocking collectives, over_x(): return lax.all_to_all(partial.reshape(4, 4, -1, 8, 1024), 'x', 0, 0)  12.6 us
    ppermute x3, waiting for transfers between devices, around(): return lax.ppermute(value, 'y', [(i, (i + hops) % 4) for i in range(4)])  12.3 us
    ppermute x3, starting transfers between devices, around(): return lax.ppermute(value, 'y', [(i, (i + hops) % 4) for i in range(4)])  10.9 us
    all_to_all x1, waiting for transfers between devices, per_device(): near = lax.all_to_all(spread, ('zl', 'core'), 0, 0).reshape(4, 2, 4, 8, 512)  10.4 us
    all_to_all x2, starting transfers between devices, over_x(): return lax.all_to_all(partial.reshape(4, 4, -1, 8, 1024), 'x', 0, 0)  9.76 us
    all_to_all x2, waiting for transfers between devices, over_x(): return lax.all_to_all(partial.reshape(4, 4, -1, 8, 1024), 'x', 0, 0)  9.44 us
  transfers between devices with their start and end apart: 7, of which 4 were waited for; matrix products, arithmetic and copies ran while one was open for 0% of the time, Pallas kernels for 10%

profile of v5, /device:TPU:2, one launch (start us, length us, event | category | flops | bytes accessed | tf_op | source)
XLA Modules:
  0.0 148.3 jit_solution(13410236854821630584)
XLA Ops:
  0.0 0.0 copy-start.1
  0.0 0.7 broadcast_in_dim.21
  0.7 55.9 %all_to_all.25 = f32[8,8,512]{2,1,0:T(8,128)S(1)} all-to-all(f32[8,8,512]{2,1,0:T(8,128)S(1)} %broadcast_in_dim.21), channel_id=1, replica_groups=mesh['zh'=8,'zl'=4,'y'=4,'x'=4,'core'=2] {'zh'}, dimensions={0} | all-to-all | bytes 262144 | tf_op jit(solution)/shard_map/gather_far/all_to_all | solution.py:141
  56.7 0.9 broadcast_in_dim.23
  57.5 5.2 %all-to-all-start.1 = ((f32[8,4,8,512]{3,2,1,0:T(8,128)}), f32[8,4,8,512]{3,2,1,0:T(8,128)S(1)}, u32[]{:S(2)}, u32[]{:S(2)}) async-start(f32[8,4,8,512]{3,2,1,0:T(8,128)} %bitcast.5), calls=%async_computation.1 | async-start | bytes 1048576 | tf_op jit(solution)/shard_map/gather_near/all_to_all | solution.py:145
  62.7 0.0 copy-done.1
  62.7 0.1 copy.6.allowed_ref
  62.8 0.0 copy-start
  62.8 1.6 %copy-done = f32[1024,512]{1,0:T(8,128)S(1)} copy-done((f32[1024,512]{1,0:T(8,128)S(1)}, f32[1024,512]{1,0:T(8,128)}, u32[]{:S(2)}) %copy-start) | copy-done | bytes 2097176
  64.4 0.8 slab.1.refs_1_.refs_2_
  65.3 2.4 %collective-permute-start = (f32[1024,512]{1,0:T(8,128)S(1)}, f32[1024,512]{1,0:T(8,128)}, u32[]{:S(2)}, u32[]{:S(2)}) collective-permute-start(f32[1024,512]{1,0:T(8,128)S(1)} %slab.1.refs_1_.refs_2_), channel_id=1, source_target_pairs={{0,1},{1,0},{2,3},{3,2},{4,5},{5,4},{6,7},{7,6},{8,9},{9,8},{10,11... | collective-permute-start | bytes 6291464 | tf_op jit(solution)/shard_map/slab/ppermute | solution.py:139
  67.7 10.4 %all-to-all-done.1 = f32[8,4,8,512]{3,2,1,0:T(8,128)S(1)} async-done(((f32[8,4,8,512]{3,2,1,0:T(8,128)}), f32[8,4,8,512]{3,2,1,0:T(8,128)S(1)}, u32[]{:S(2)}, u32[]{:S(2)}) %all-to-all-start.1) | async-done | bytes 524320 | tf_op jit(solution)/shard_map/gather_near/all_to_all | solution.py:145
  78.1 4.9 %collective-permute-start.2 = (f32[4,2,4,8,512]{4,3,2,1,0:T(8,128)S(1)}, f32[4,2,4,8,512]{4,3,2,1,0:T(8,128)}, u32[]{:S(2)}, u32[]{:S(2)}) collective-permute-start(f32[4,2,4,8,512]{4,3,2,1,0:T(8,128)S(1)} %bitcast.13), channel_id=1, source_target_pairs={{0,24},{8,0},{16,8},{24,16},{1,25},{9,1},{17,9},{25,17},{2,26},{10... | collective-permute-start | bytes 1572872 | tf_op jit(solution)/shard_map/gather_y/ppermute | solution.py:127
  83.0 1.9 %collective-permute-start.1 = (f32[4,2,4,8,512]{4,3,2,1,0:T(8,128)S(1)}, f32[4,2,4,8,512]{4,3,2,1,0:T(8,128)}, u32[]{:S(2)}, u32[]{:S(2)}) collective-permute-start(f32[4,2,4,8,512]{4,3,2,1,0:T(8,128)S(1)} %bitcast.14), channel_id=1, source_target_pairs={{0,8},{8,16},{16,24},{24,0},{1,9},{9,17},{17,25},{25,1},{2,10},{10... | collective-permute-start | bytes 1572872 | tf_op jit(solution)/shard_map/gather_y/ppermute | solution.py:127
  84.9 4.1 %collective-permute-start.3 = (f32[4,2,4,8,512]{4,3,2,1,0:T(8,128)S(1)}, f32[4,2,4,8,512]{4,3,2,1,0:T(8,128)}, u32[]{:S(2)}, u32[]{:S(2)}) collective-permute-start(f32[4,2,4,8,512]{4,3,2,1,0:T(8,128)S(1)} %bitcast.15), channel_id=1, source_target_pairs={{0,16},{8,24},{16,0},{24,8},{1,17},{9,25},{17,1},{25,9},{2,18},{10... | collective-permute-start | bytes 1572872 | tf_op jit(solution)/shard_map/gather_y/ppermute | solution.py:127
  89.1 0.0 collective-permute-done.refs_2_.refs_3_
  89.1 4.4 %own_y.1.refs_4_ = f32[128,1024]{1,0:T(8,128)} custom-call(s32[1]{0:T(128)} %bitcast.1.core_ref, f32[4,2,4,8,512]{4,3,2,1,0:T(8,128)S(1)} %bitcast.16, f32[1024,512]{1,0:T(8,128)S(1)} %slab.1.refs_1_.refs_2_, f32[1024,512]{1,0:T(8,128)} %collective-permute-done.refs_2_.refs_3_, f32[4,2,4,8,512]{4,3,2,1,0:T(8,128)S(1)} %bitcast.17), custom_call_target="tpu_custom_call" | custom-call | flops 805306368 | bytes 16777216 | tf_op jit(solution)/shard_map/own_y/pallas_call | solution.py:78
  93.5 4.8 %all-to-all-start.2 = ((f32[4,4,1,8,1024]{4,3,2,1,0:T(8,128)}), f32[4,4,1,8,1024]{4,3,2,1,0:T(8,128)S(1)}, u32[]{:S(2)}, u32[]{:S(2)}) async-start(f32[4,4,1,8,1024]{4,3,2,1,0:T(8,128)} %bitcast.7), calls=%async_computation.2 | async-start | bytes 1048576 | tf_op jit(solution)/shard_map/reduce_x/all_to_all | solution.py:131
  98.3 6.9 %collective-permute-done.2.refs_1_ = f32[4,2,4,8,512]{4,3,2,1,0:T(8,128)} collective-permute-done((f32[4,2,4,8,512]{4,3,2,1,0:T(8,128)S(1)}, f32[4,2,4,8,512]{4,3,2,1,0:T(8,128)}, u32[]{:S(2)}, u32[]{:S(2)}) %collective-permute-start.2) | collective-permute-done | bytes 524320 | tf_op jit(solution)/shard_map/gather_y/ppermute | solution.py:127
  105.2 5.4 %collective-permute-done.1.refs_0_ = f32[4,2,4,8,512]{4,3,2,1,0:T(8,128)} collective-permute-done((f32[4,2,4,8,512]{4,3,2,1,0:T(8,128)S(1)}, f32[4,2,4,8,512]{4,3,2,1,0:T(8,128)}, u32[]{:S(2)}, u32[]{:S(2)}) %collective-permute-start.1) | collective-permute-done | bytes 524320 | tf_op jit(solution)/shard_map/gather_y/ppermute | solution.py:127
  110.6 5.3 %sides_y.1.refs_3_ = f32[256,1024]{1,0:T(8,128)} custom-call(s32[1]{0:T(128)} %bitcast.1.core_ref, f32[4,2,4,8,512]{4,3,2,1,0:T(8,128)} %collective-permute-done.1.refs_0_, f32[4,2,4,8,512]{4,3,2,1,0:T(8,128)} %collective-permute-done.2.refs_1_, f32[1024,512]{1,0:T(8,128)S(1)} %slab.1.refs_1_.refs_2_, f32[1024,512]{1,0:T(8,128)} %collective-permute-done.refs_2_.refs_3_, ...), custom_call_target="tpu_custom_call" | custom-call | flops 1610612736 | bytes 16777216 | tf_op jit(solution)/shard_map/sides_y/pallas_call | solution.py:78
  115.9 0.0 collective-permute-done.3.refs_0_
  115.9 3.8 %across_y.1 = f32[128,1024]{1,0:T(8,128)S(1)} custom-call(s32[1]{0:T(128)} %bitcast.1.core_ref, f32[4,2,4,8,512]{4,3,2,1,0:T(8,128)} %collective-permute-done.3.refs_0_, f32[1024,512]{1,0:T(8,128)S(1)} %slab.1.refs_1_.refs_2_, f32[1024,512]{1,0:T(8,128)} %collective-permute-done.refs_2_.refs_3_, f32[256,1024]{1,0:T(8,128)} %sides_y.1.refs_3_), custom_call_target="tpu_custom_call" | custom-call | flops 805306368 | bytes 16777216 | tf_op jit(solution)/shard_map/across_y/pallas_call | solution.py:78
  119.7 0.0 all-to-all-done.2.own_ref
  119.8 12.6 %all_to_all.26.across_ref = f32[4,4,1,8,1024]{4,3,2,1,0:T(8,128)S(1)} all-to-all(f32[4,4,1,8,1024]{4,3,2,1,0:T(8,128)S(1)} %bitcast.18), channel_id=1, replica_groups=mesh['zh'=8,'zl'=4,'y'=4,'x'=4,'core'=2] {'x'}, dimensions={0} | all-to-all | bytes 1048576 | tf_op jit(solution)/shard_map/reduce_x/all_to_all | solution.py:131
  132.4 4.9 %all-to-all-start.3 = ((f32[4,4,2,8,1024]{4,3,2,1,0:T(8,128)}), f32[4,4,2,8,1024]{4,3,2,1,0:T(8,128)S(1)}, u32[]{:S(2)}, u32[]{:S(2)}) async-start(f32[4,4,2,8,1024]{4,3,2,1,0:T(8,128)} %bitcast.8), calls=%async_computation.3 | async-start | bytes 2097152 | tf_op jit(solution)/shard_map/reduce_x/all_to_all | solution.py:131
  137.3 9.4 %all-to-all-done.3.sides_ref = f32[4,4,2,8,1024]{4,3,2,1,0:T(8,128)S(1)} async-done(((f32[4,4,2,8,1024]{4,3,2,1,0:T(8,128)}), f32[4,4,2,8,1024]{4,3,2,1,0:T(8,128)S(1)}, u32[]{:S(2)}, u32[]{:S(2)}) %all-to-all-start.3) | async-done | bytes 1048608 | tf_op jit(solution)/shard_map/reduce_x/all_to_all | solution.py:131
  146.8 1.5 %reduce_x.1 = f32[4,4,8,1024]{3,2,1,0:T(8,128)} custom-call(s32[1]{0:T(128)} %bitcast.y_ref, f32[4,4,1,8,1024]{4,3,2,1,0:T(8,128)S(1)} %all-to-all-done.2.own_ref, f32[4,4,2,8,1024]{4,3,2,1,0:T(8,128)S(1)} %all-to-all-done.3.sides_ref, f32[4,4,1,8,1024]{4,3,2,1,0:T(8,128)S(1)} %all_to_all.26.across_ref), custom_call_target="tpu_custom_call" | custom-call | flops 1 | bytes 1 | tf_op jit(solution)/shard_map/reduce_x/pallas_call | solution.py:112
  (1 shorter events, 0.0 us)
Async XLA Ops:
  0.0 62.7 %copy-start.1 = (s32[8,4]{0,1:T(4,128)S(1)}, s32[8,4]{0,1:T(4,128)}, u32[]{:S(2)}) copy-start(s32[8,4]{0,1:T(4,128)} %param.5) | copy-start | bytes 388
  57.5 20.5 %all-to-all-start.1 = ((f32[8,4,8,512]{3,2,1,0:T(8,128)}), f32[8,4,8,512]{3,2,1,0:T(8,128)S(1)}, u32[]{:S(2)}, u32[]{:S(2)}) async-start(f32[8,4,8,512]{3,2,1,0:T(8,128)} %bitcast.5), calls=%async_computation.1 | async-start | bytes 1048576 | tf_op jit(solution)/shard_map/gather_near/all_to_all | solution.py:145
  62.8 1.6 %copy-start = (f32[1024,512]{1,0:T(8,128)S(1)}, f32[1024,512]{1,0:T(8,128)}, u32[]{:S(2)}) copy-start(f32[1024,512]{1,0:T(8,128)} %v_ref.1) | copy-start | bytes 6291460
  65.3 23.8 %collective-permute-start = (f32[1024,512]{1,0:T(8,128)S(1)}, f32[1024,512]{1,0:T(8,128)}, u32[]{:S(2)}, u32[]{:S(2)}) collective-permute-start(f32[1024,512]{1,0:T(8,128)S(1)} %slab.1.refs_1_.refs_2_), channel_id=1, source_target_pairs={{0,1},{1,0},{2,3},{3,2},{4,5},{5,4},{6,7},{7,6},{8,9},{9,8},{10,11... | collective-permute-start | bytes 6291464 | tf_op jit(solution)/shard_map/slab/ppermute | solution.py:139
  78.1 27.1 %collective-permute-start.2 = (f32[4,2,4,8,512]{4,3,2,1,0:T(8,128)S(1)}, f32[4,2,4,8,512]{4,3,2,1,0:T(8,128)}, u32[]{:S(2)}, u32[]{:S(2)}) collective-permute-start(f32[4,2,4,8,512]{4,3,2,1,0:T(8,128)S(1)} %bitcast.13), channel_id=1, source_target_pairs={{0,24},{8,0},{16,8},{24,16},{1,25},{9,1},{17,9},{25,17},{2,26},{10... | collective-permute-start | bytes 1572872 | tf_op jit(solution)/shard_map/gather_y/ppermute | solution.py:127
  83.0 27.6 %collective-permute-start.1 = (f32[4,2,4,8,512]{4,3,2,1,0:T(8,128)S(1)}, f32[4,2,4,8,512]{4,3,2,1,0:T(8,128)}, u32[]{:S(2)}, u32[]{:S(2)}) collective-permute-start(f32[4,2,4,8,512]{4,3,2,1,0:T(8,128)S(1)} %bitcast.14), channel_id=1, source_target_pairs={{0,8},{8,16},{16,24},{24,0},{1,9},{9,17},{17,25},{25,1},{2,10},{10... | collective-permute-start | bytes 1572872 | tf_op jit(solution)/shard_map/gather_y/ppermute | solution.py:127
  84.9 31.0 %collective-permute-start.3 = (f32[4,2,4,8,512]{4,3,2,1,0:T(8,128)S(1)}, f32[4,2,4,8,512]{4,3,2,1,0:T(8,128)}, u32[]{:S(2)}, u32[]{:S(2)}) collective-permute-start(f32[4,2,4,8,512]{4,3,2,1,0:T(8,128)S(1)} %bitcast.15), channel_id=1, source_target_pairs={{0,16},{8,24},{16,0},{24,8},{1,17},{9,25},{17,1},{25,9},{2,18},{10... | collective-permute-start | bytes 1572872 | tf_op jit(solution)/shard_map/gather_y/ppermute | solution.py:127
  93.5 26.3 %all-to-all-start.2 = ((f32[4,4,1,8,1024]{4,3,2,1,0:T(8,128)}), f32[4,4,1,8,1024]{4,3,2,1,0:T(8,128)S(1)}, u32[]{:S(2)}, u32[]{:S(2)}) async-start(f32[4,4,1,8,1024]{4,3,2,1,0:T(8,128)} %bitcast.7), calls=%async_computation.2 | async-start | bytes 1048576 | tf_op jit(solution)/shard_map/reduce_x/all_to_all | solution.py:131
  132.4 14.4 %all-to-all-start.3 = ((f32[4,4,2,8,1024]{4,3,2,1,0:T(8,128)}), f32[4,4,2,8,1024]{4,3,2,1,0:T(8,128)S(1)}, u32[]{:S(2)}, u32[]{:S(2)}) async-start(f32[4,4,2,8,1024]{4,3,2,1,0:T(8,128)} %bitcast.8), calls=%async_computation.3 | async-start | bytes 2097152 | tf_op jit(solution)/shard_map/reduce_x/all_to_all | solution.py:131

commit v6 on v3

v6 whole, which is shorter than its diff:
```python
import functools

import jax
import jax.numpy as jnp
from jax import lax
from jax.experimental import pallas as pl
from jax.experimental.pallas import tpu as pltpu
from jax.sharding import Mesh, PartitionSpec as P

BLK = 128
NT = (((1,), (1,)), ((), ()))
COLS = 256
PARAMS = pltpu.CompilerParams(vmem_limit_bytes=48 * 2**20)
COST = pl.CostEstimate(flops=1, bytes_accessed=1, transcendentals=0)


def split(wide):
    high = wide.astype(jnp.bfloat16)
    return high, (wide - high.astype(jnp.float32)).astype(jnp.bfloat16)


def mask_body(allowed_ref, v_ref, kept_ref):
    step = pl.program_id(0)
    for a in range(COLS // BLK):
        rows = pl.ds(a * BLK, BLK)
        for c in range(v_ref.shape[1] // BLK):
            cols = pl.ds(c * BLK, BLK)
            weight = allowed_ref[step * (COLS // BLK) + a, c].astype(jnp.float32)
            kept_ref[rows, cols] = v_ref[rows, cols] * weight


def masked(integrals, allowed):
    rows, depth = integrals.shape
    block = pl.BlockSpec((COLS, depth), lambda i, allowed: (i, 0))
    return pl.pallas_call(
        mask_body,
        out_shape=jax.ShapeDtypeStruct((rows, depth), jnp.float32),
        grid_spec=pltpu.PrefetchScalarGridSpec(
            num_scalar_prefetch=1, grid=(rows // COLS,), in_specs=[block], out_specs=block
        ),
        compiler_params=PARAMS,
        cost_estimate=COST,
    )(allowed, integrals)


def ladder_body(count, waits, where_ref, *refs):
    t_refs, (own_ref, got_ref) = refs[:count], refs[count : count + 2]
    out_refs, t_parts = refs[count + 2 + waits : -1], refs[-1]
    core, x = where_ref[0], where_ref[1]
    size = 32 * count
    rows = 4 * size

    @pl.when(pl.program_id(0) == 0)
    def _():
        for side in range(2):
            source = core if side == 0 else 1 - core
            for k in range(4):
                to = lax.rem(x + k, 4)
                wide = jnp.concatenate([t[low, source, to] for low in range(4) for t in t_refs], axis=0)
                high, low_part = split(wide)
                t_parts[side, pl.ds(k * size, size), :] = high
                t_parts[side, pl.ds(rows + k * size, size), :] = low_part
        if len(out_refs) > 4:
            out_refs[4][...] = t_refs[0][...]

    def dot(left, right):
        return lax.dot_general(left, right, NT, preferred_element_type=jnp.float32)

    total = None
    for side, v_ref in enumerate((own_ref, got_ref)):
        high, low_part = split(v_ref[...])
        both = dot(t_parts[side], high)
        term = (both[rows:] + dot(t_parts[side, :rows], low_part)) + both[:rows]
        total = term if total is None else total + term
    for k in range(4):
        out_refs[k][...] = total[k * size : (k + 1) * size]


def ladder(where, chunks, slabs, after=(), echo=False):
    width, depth = slabs[0].shape
    count = len(chunks)
    size = 32 * count
    whole = pl.BlockSpec((4, 2, 4, 8, depth), lambda i, where: (0, 0, 0, 0, 0))
    return pl.pallas_call(
        functools.partial(ladder_body, count, len(after)),
        out_shape=[jax.ShapeDtypeStruct((size, width), jnp.float32)] * 4
        + [jax.ShapeDtypeStruct(chunks[0].shape, jnp.float32)] * echo,
        grid_spec=pltpu.PrefetchScalarGridSpec(
            num_scalar_prefetch=1,
            grid=(width // COLS,),
            in_specs=[whole] * count
            + [pl.BlockSpec((COLS, depth), lambda i, where: (i, 0))] * 2
            + [pl.BlockSpec(memory_space=pl.ANY)] * len(after),
            out_specs=[pl.BlockSpec((size, COLS), lambda i, where: (0, i))] * 4 + [whole] * echo,
            scratch_shapes=[pltpu.VMEM((2, 8 * size, depth), jnp.bfloat16)],
        ),
        compiler_params=PARAMS,
        cost_estimate=pl.CostEstimate(
            flops=48 * size * width * depth, bytes_accessed=16 * 2**20, transcendentals=0
        ),
    )(where, *chunks, *slabs, *after)


def finish_body(y_ref, *refs):
    me = y_ref[0]
    own, sides, across, out_ref = refs[:4], refs[4:8], refs[8:12], refs[12]

    def put(offset, parts, k):
        a, b, c, d = (part[0, k] for part in parts)
        out_ref[0, lax.rem(me + offset, 4)] = (a + b) + (c + d)

    put(0, own, 0)
    put(3, sides, 0)
    put(1, sides, 1)
    put(2, across, 0)


def finish(y, *chunks):
    parts = [part.reshape(4, -1, 8, 1024) for chunk in chunks for part in chunk]
    return pl.pallas_call(
        finish_body,
        out_shape=jax.ShapeDtypeStruct((4, 4, 8, 1024), jnp.float32),
        grid_spec=pltpu.PrefetchScalarGridSpec(
            num_scalar_prefetch=1,
            grid=(4,),
            in_specs=[pl.BlockSpec((1, *part.shape[1:]), lambda low, y: (low, 0, 0, 0)) for part in parts],
            out_specs=pl.BlockSpec((1, 4, 8, 1024), lambda low, y: (low, 0, 0, 0)),
        ),
        compiler_params=PARAMS,
        cost_estimate=COST,
    )(y, *parts)


def shift(value, axis, hops):
    return lax.ppermute(value, axis, [(i, (i + hops) % 4) for i in range(4)])


def over_x(parts):
    return [parts[0]] + [shift(parts[k], "x", k) for k in (2, 1, 3)]


def per_device(integrals, amplitudes, allowed):
    core, x, y = (lax.axis_index(axis).astype(jnp.int32) for axis in ("core", "x", "y"))
    where = jnp.stack([core, x])
    with jax.named_scope("slab"):
        kept = masked(integrals, allowed)
        slabs = (kept, lax.ppermute(kept, "core", [(0, 1), (1, 0)]))
    with jax.named_scope("gather_far"):
        far = lax.all_to_all(jnp.broadcast_to(amplitudes[None], (8, 8, 512)), "zh", 0, 0)
    with jax.named_scope("gather_near"):
        by_core = far.reshape(1, 4, 2, 8, 512).swapaxes(1, 2)
        spread = jnp.broadcast_to(by_core, (4, 2, 4, 8, 512)).reshape(8, 4, 8, 512)
        near = lax.all_to_all(spread, ("zl", "core"), 0, 0).reshape(4, 2, 4, 8, 512)
    with jax.named_scope("gather_sides"):
        below, above = shift(near, "y", 1), shift(near, "y", 3)
    with jax.named_scope("own_y"):
        *own, echo = ladder(where, [near], slabs, echo=True)
        own_sums = over_x(own)
    with jax.named_scope("gather_across"):
        across = shift(echo, "y", 2)
    with jax.named_scope("sides_y"):
        sides = ladder(where, [below, above], slabs, [own[0]])
        sides_sums = over_x(sides)
    with jax.named_scope("across_y"):
        opposite = ladder(where, [across], slabs, [sides[0], *own_sums[1:]])
        across_sums = over_x(opposite)
    with jax.named_scope("finish"):
        return finish(y[None], own_sums, sides_sums, across_sums).reshape(128, 1024)


def solution(mesh):
    fine = Mesh(mesh.devices.reshape(8, 4, 4, 4, 2), ("zh", "zl", "y", "x", "core"))
    rows, cols = ("zh", "zl", "y"), ("x", "core")
    return jax.shard_map(
        per_device, mesh=fine, in_specs=(P(rows, cols),) * 3, out_specs=P(cols, rows), check_vma=False
    )
```

time: 135 us -> 148 us (1.096)
  the two profiles are of different devices: /device:TPU:24 before, /device:TPU:6 now
where the time goes in v6:
time: 148 us
  blocking collectives  55.9 us (38%)
  starting transfers between devices  46.8 us (32%)
  waiting for transfers between devices  24.3 us (16%)
  Pallas kernels  16.9 us (11%)
  local copies, waits for them, and re-layouts  3.28 us (2%)
    all_to_all x1, blocking collectives, per_device(): lax.all_to_all(jnp.broadcast_to(amplitudes[None], (8, 8, 512)), 'zh', 0, 0)  55.9 us
    ppermute x12, starting transfers between devices, shift(): return lax.ppermute(value, axis, [(i, (i + hops) % 4) for i in range(4)])  39.2 us
    pallas_call x3, Pallas kernels, ladder(): pl.pallas_call(functools.partial(ladder_body, count, len(after)), out_sha...  14.6 us
    ppermute x12, waiting for transfers between devices, shift(): return lax.ppermute(value, axis, [(i, (i + hops) % 4) for i in range(4)])  13.9 us
    all_to_all x1, waiting for transfers between devices, per_device(): near = lax.all_to_all(spread, ('zl', 'core'), 0, 0).reshape(4, 2, 4, 8, 512)  10.4 us
    all_to_all x1, starting transfers between devices, per_device(): near = lax.all_to_all(spread, ('zl', 'core'), 0, 0).reshape(4, 2, 4, 8, 512)  5.19 us
  transfers between devices with their start and end apart: 14, of which 4 were waited for; matrix products, arithmetic and copies ran while one was open for 0% of the time, Pallas kernels for 7%

profile of v6, /device:TPU:6, one launch (start us, length us, event | category | flops | bytes accessed | tf_op | source)
XLA Modules:
  0.0 147.5 jit_solution(11644691443219915623)
XLA Ops:
  0.0 0.0 copy-start.1
  0.0 0.7 broadcast_in_dim.17
  0.7 55.9 %all_to_all.10 = f32[8,8,512]{2,1,0:T(8,128)S(1)} all-to-all(f32[8,8,512]{2,1,0:T(8,128)S(1)} %broadcast_in_dim.17), channel_id=1, replica_groups=mesh['zh'=8,'zl'=4,'y'=4,'x'=4,'core'=2] {'zh'}, dimensions={0} | all-to-all | bytes 262144 | tf_op jit(solution)/shard_map/gather_far/all_to_all | solution.py:149
  56.7 0.9 broadcast_in_dim.19
  57.5 5.2 %all-to-all-start.1 = ((f32[8,4,8,512]{3,2,1,0:T(8,128)}), f32[8,4,8,512]{3,2,1,0:T(8,128)S(1)}, u32[]{:S(2)}, u32[]{:S(2)}) async-start(f32[8,4,8,512]{3,2,1,0:T(8,128)} %bitcast.6), calls=%async_computation.1 | async-start | bytes 1048576 | tf_op jit(solution)/shard_map/gather_near/all_to_all | solution.py:153
  62.7 0.0 copy-done.1
  62.7 0.1 copy.6.allowed_ref
  62.8 0.0 copy-start
  62.8 1.6 %copy-done = f32[1024,512]{1,0:T(8,128)S(1)} copy-done((f32[1024,512]{1,0:T(8,128)S(1)}, f32[1024,512]{1,0:T(8,128)}, u32[]{:S(2)}) %copy-start) | copy-done | bytes 2097176
  64.4 0.8 slab.1.refs_1_.refs_2_
  65.3 2.4 %collective-permute-start = (f32[1024,512]{1,0:T(8,128)S(1)}, f32[1024,512]{1,0:T(8,128)}, u32[]{:S(2)}, u32[]{:S(2)}) collective-permute-start(f32[1024,512]{1,0:T(8,128)S(1)} %slab.1.refs_1_.refs_2_), channel_id=1, source_target_pairs={{0,1},{1,0},{2,3},{3,2},{4,5},{5,4},{6,7},{7,6},{8,9},{9,8},{10,11... | collective-permute-start | bytes 6291464 | tf_op jit(solution)/shard_map/slab/ppermute | solution.py:147
  67.7 10.4 %all-to-all-done.1 = f32[8,4,8,512]{3,2,1,0:T(8,128)S(1)} async-done(((f32[8,4,8,512]{3,2,1,0:T(8,128)}), f32[8,4,8,512]{3,2,1,0:T(8,128)S(1)}, u32[]{:S(2)}, u32[]{:S(2)}) %all-to-all-start.1) | async-done | bytes 524320 | tf_op jit(solution)/shard_map/gather_near/all_to_all | solution.py:153
  78.1 4.9 %collective-permute-start.5 = (f32[4,2,4,8,512]{4,3,2,1,0:T(8,128)S(1)}, f32[4,2,4,8,512]{4,3,2,1,0:T(8,128)S(1)}, u32[]{:S(2)}, u32[]{:S(2)}) collective-permute-start(f32[4,2,4,8,512]{4,3,2,1,0:T(8,128)S(1)} %bitcast.23), channel_id=1, source_target_pairs={{0,24},{8,0},{16,8},{24,16},{1,25},{9,1},{17,9},{25,17},{2,26},{10... | collective-permute-start | bytes 1572872 | tf_op jit(solution)/shard_map/gather_sides/ppermute | solution.py:135
  83.0 1.9 %collective-permute-start.4 = (f32[4,2,4,8,512]{4,3,2,1,0:T(8,128)S(1)}, f32[4,2,4,8,512]{4,3,2,1,0:T(8,128)S(1)}, u32[]{:S(2)}, u32[]{:S(2)}) collective-permute-start(f32[4,2,4,8,512]{4,3,2,1,0:T(8,128)S(1)} %bitcast.24), channel_id=1, source_target_pairs={{0,8},{8,16},{16,24},{24,0},{1,9},{9,17},{17,25},{25,1},{2,10},{10... | collective-permute-start | bytes 1572872 | tf_op jit(solution)/shard_map/gather_sides/ppermute | solution.py:135
  84.9 0.1 pad_add_fusion.where_ref
  85.0 0.0 collective-permute-done.refs_2_.refs_3_
  85.0 4.3 %own_y.1 = (f32[32,1024]{1,0:T(8,128)S(1)}, f32[32,1024]{1,0:T(8,128)S(1)}, f32[32,1024]{1,0:T(8,128)S(1)}, f32[32,1024]{1,0:T(8,128)S(1)}, f32[4,2,4,8,512]{4,3,2,1,0:T(8,128)S(1)}) custom-call(s32[2]{0:T(128)S(1)} %pad_add_fusion.where_ref, f32[4,2,4,8,512]{4,3,2,1,0:T(8,128)S(1)} %bitcast.25, f32[1024,512]{1,0:T(8,128)S(1)} %slab.1.refs_1_.refs_2_, ...), custom_call_target="tpu_custom_call" | custom-call | flops 805306368 | bytes 16777216 | tf_op jit(solution)/shard_map/own_y/pallas_call | solution.py:84
  89.3 4.1 %collective-permute-start.9 = (f32[4,2,4,8,512]{4,3,2,1,0:T(8,128)S(1)}, f32[4,2,4,8,512]{4,3,2,1,0:T(8,128)S(1)}, u32[]{:S(2)}, u32[]{:S(2)}) collective-permute-start(f32[4,2,4,8,512]{4,3,2,1,0:T(8,128)S(1)} %get-tuple-element.26), channel_id=1, source_target_pairs={{0,16},{8,24},{16,0},{24,8},{1,17},{9,25},{17,1},{25,9},{2,18},{10... | collective-permute-start | bytes 1572872 | tf_op jit(solution)/shard_map/gather_across/ppermute | solution.py:135
  93.4 3.3 %collective-permute-start.1 = (f32[32,1024]{1,0:T(8,128)S(1)}, f32[32,1024]{1,0:T(8,128)S(1)}, u32[]{:S(2)}, u32[]{:S(2)}) collective-permute-start(f32[32,1024]{1,0:T(8,128)S(1)} %get-tuple-element.19), channel_id=1, source_target_pairs={{0,4},{2,6},{4,0},{6,2},{1,5},{3,7},{5,1},{7,3},{8,12},{10,14},{12... | collective-permute-start | bytes 393224 | tf_op jit(solution)/shard_map/own_y/ppermute | solution.py:135
  96.7 4.0 %collective-permute-start.2 = (f32[32,1024]{1,0:T(8,128)S(1)}, f32[32,1024]{1,0:T(8,128)S(1)}, u32[]{:S(2)}, u32[]{:S(2)}) collective-permute-start(f32[32,1024]{1,0:T(8,128)S(1)} %get-tuple-element.20), channel_id=1, source_target_pairs={{0,2},{2,4},{4,6},{6,0},{1,3},{3,5},{5,7},{7,1},{8,10},{10,12},{12... | collective-permute-start | bytes 393224 | tf_op jit(solution)/shard_map/own_y/ppermute | solution.py:135
  100.7 0.0 collective-permute-done.5.refs_1_
  100.7 1.9 %collective-permute-start.3 = (f32[32,1024]{1,0:T(8,128)S(1)}, f32[32,1024]{1,0:T(8,128)S(1)}, u32[]{:S(2)}, u32[]{:S(2)}) collective-permute-start(f32[32,1024]{1,0:T(8,128)S(1)} %get-tuple-element.21), channel_id=1, source_target_pairs={{0,6},{2,0},{4,2},{6,4},{1,7},{3,1},{5,3},{7,5},{8,14},{10,8},{12,... | collective-permute-start | bytes 393224 | tf_op jit(solution)/shard_map/own_y/ppermute | solution.py:135
  102.6 7.9 %collective-permute-done.4.refs_0_ = f32[4,2,4,8,512]{4,3,2,1,0:T(8,128)S(1)} collective-permute-done((f32[4,2,4,8,512]{4,3,2,1,0:T(8,128)S(1)}, f32[4,2,4,8,512]{4,3,2,1,0:T(8,128)S(1)}, u32[]{:S(2)}, u32[]{:S(2)}) %collective-permute-start.4) | collective-permute-done | bytes 524320 | tf_op jit(solution)/shard_map/gather_sides/ppermute | solution.py:135
  110.5 5.4 %sides_y.1 = (f32[64,1024]{1,0:T(8,128)S(1)}, f32[64,1024]{1,0:T(8,128)}, f32[64,1024]{1,0:T(8,128)}, f32[64,1024]{1,0:T(8,128)S(1)}) custom-call(s32[2]{0:T(128)S(1)} %pad_add_fusion.where_ref, f32[4,2,4,8,512]{4,3,2,1,0:T(8,128)S(1)} %collective-permute-done.4.refs_0_, f32[4,2,4,8,512]{4,3,2,1,0:T(8,128)S(1)} %collective-permute-done.5.refs_1_, ...), custom_call_target="tpu_custom_call" | custom-call | flops 1610612736 | bytes 16777216 | tf_op jit(solution)/shard_map/sides_y/pallas_call | solution.py:84
  115.9 0.0 collective-permute-done.1.refs_4_
  115.9 0.0 collective-permute-done.2.refs_5_
  115.9 0.0 collective-permute-done.3.refs_6_
  116.0 0.0 collective-permute-done.9.refs_0_
  116.0 5.0 %across_y.1 = (f32[32,1024]{1,0:T(8,128)S(1)}, f32[32,1024]{1,0:T(8,128)}, f32[32,1024]{1,0:T(8,128)S(1)}, f32[32,1024]{1,0:T(8,128)}) custom-call(s32[2]{0:T(128)S(1)} %pad_add_fusion.where_ref, f32[4,2,4,8,512]{4,3,2,1,0:T(8,128)S(1)} %collective-permute-done.9.refs_0_, f32[1024,512]{1,0:T(8,128)S(1)} %slab.1.refs_1_.refs_2_, ...), custom_call_target="tpu_custom_call" | custom-call | flops 805306368 | bytes 16777216 | tf_op jit(solution)/shard_map/across_y/pallas_call | solution.py:84
  120.9 3.3 %collective-permute-start.10 = (f32[32,1024]{1,0:T(8,128)S(1)}, f32[32,1024]{1,0:T(8,128)S(1)}, u32[]{:S(2)}, u32[]{:S(2)}) collective-permute-start(f32[32,1024]{1,0:T(8,128)S(1)} %get-tuple-element.28), channel_id=1, source_target_pairs={{0,4},{2,6},{4,0},{6,2},{1,5},{3,7},{5,1},{7,3},{8,12},{10,14},{12... | collective-permute-start | bytes 393224 | tf_op jit(solution)/shard_map/across_y/ppermute | solution.py:135
  124.2 4.0 %collective-permute-start.6 = (f32[64,1024]{1,0:T(8,128)}, f32[64,1024]{1,0:T(8,128)S(1)}, u32[]{:S(2)}, u32[]{:S(2)}) collective-permute-start(f32[64,1024]{1,0:T(8,128)} %get-tuple-element.23), channel_id=1, source_target_pairs={{0,4},{2,6},{4,0},{6,2},{1,5},{3,7},{5,1},{7,3},{8,12},{10,14},{12... | collective-permute-start | bytes 786440 | tf_op jit(solution)/shard_map/sides_y/ppermute | solution.py:135
  128.3 2.4 %collective-permute-start.7 = (f32[64,1024]{1,0:T(8,128)}, f32[64,1024]{1,0:T(8,128)S(1)}, u32[]{:S(2)}, u32[]{:S(2)}) collective-permute-start(f32[64,1024]{1,0:T(8,128)} %get-tuple-element.24), channel_id=1, source_target_pairs={{0,2},{2,4},{4,6},{6,0},{1,3},{3,5},{5,7},{7,1},{8,10},{10,12},{12... | collective-permute-start | bytes 786440 | tf_op jit(solution)/shard_map/sides_y/ppermute | solution.py:135
  130.7 3.5 %collective-permute-start.8 = (f32[64,1024]{1,0:T(8,128)S(1)}, f32[64,1024]{1,0:T(8,128)S(1)}, u32[]{:S(2)}, u32[]{:S(2)}) collective-permute-start(f32[64,1024]{1,0:T(8,128)S(1)} %get-tuple-element.25), channel_id=1, source_target_pairs={{0,6},{2,0},{4,2},{6,4},{1,7},{3,1},{5,3},{7,5},{8,14},{10,8},{12,... | collective-permute-start | bytes 786440 | tf_op jit(solution)/shard_map/sides_y/ppermute | solution.py:135
  134.1 3.6 %collective-permute-start.11 = (f32[32,1024]{1,0:T(8,128)}, f32[32,1024]{1,0:T(8,128)S(1)}, u32[]{:S(2)}, u32[]{:S(2)}) collective-permute-start(f32[32,1024]{1,0:T(8,128)} %get-tuple-element.29), channel_id=1, source_target_pairs={{0,2},{2,4},{4,6},{6,0},{1,3},{3,5},{5,7},{7,1},{8,10},{10,12},{12... | collective-permute-start | bytes 393224 | tf_op jit(solution)/shard_map/across_y/ppermute | solution.py:135
  137.7 0.0 collective-permute-done.10
  137.7 2.3 %collective-permute-start.12 = (f32[32,1024]{1,0:T(8,128)}, f32[32,1024]{1,0:T(8,128)S(1)}, u32[]{:S(2)}, u32[]{:S(2)}) collective-permute-start(f32[32,1024]{1,0:T(8,128)} %get-tuple-element.30), channel_id=1, source_target_pairs={{0,6},{2,0},{4,2},{6,4},{1,7},{3,1},{5,3},{7,5},{8,14},{10,8},{12,... | collective-permute-start | bytes 393224 | tf_op jit(solution)/shard_map/across_y/ppermute | solution.py:135
  140.0 1.2 collective-permute-done.11
  141.2 4.8 %collective-permute-done.12 = f32[32,1024]{1,0:T(8,128)S(1)} collective-permute-done((f32[32,1024]{1,0:T(8,128)}, f32[32,1024]{1,0:T(8,128)S(1)}, u32[]{:S(2)}, u32[]{:S(2)}) %collective-permute-start.12) | collective-permute-done | bytes 131104 | tf_op jit(solution)/shard_map/across_y/ppermute | solution.py:135
  146.0 0.0 collective-permute-done.6
  146.0 0.0 collective-permute-done.7
  146.0 0.0 collective-permute-done.8
  146.0 1.5 finish.1
  (1 shorter events, 0.0 us)
Async XLA Ops:
  0.0 62.7 %copy-start.1 = (s32[8,4]{0,1:T(4,128)S(1)}, s32[8,4]{0,1:T(4,128)}, u32[]{:S(2)}) copy-start(s32[8,4]{0,1:T(4,128)} %param.5) | copy-start | bytes 388
  57.5 20.5 %all-to-all-start.1 = ((f32[8,4,8,512]{3,2,1,0:T(8,128)}), f32[8,4,8,512]{3,2,1,0:T(8,128)S(1)}, u32[]{:S(2)}, u32[]{:S(2)}) async-start(f32[8,4,8,512]{3,2,1,0:T(8,128)} %bitcast.6), calls=%async_computation.1 | async-start | bytes 1048576 | tf_op jit(solution)/shard_map/gather_near/all_to_all | solution.py:153
  62.8 1.6 %copy-start = (f32[1024,512]{1,0:T(8,128)S(1)}, f32[1024,512]{1,0:T(8,128)}, u32[]{:S(2)}) copy-start(f32[1024,512]{1,0:T(8,128)} %v_ref.1) | copy-start | bytes 6291460
  65.3 19.8 %collective-permute-start = (f32[1024,512]{1,0:T(8,128)S(1)}, f32[1024,512]{1,0:T(8,128)}, u32[]{:S(2)}, u32[]{:S(2)}) collective-permute-start(f32[1024,512]{1,0:T(8,128)S(1)} %slab.1.refs_1_.refs_2_), channel_id=1, source_target_pairs={{0,1},{1,0},{2,3},{3,2},{4,5},{5,4},{6,7},{7,6},{8,9},{9,8},{10,11... | collective-permute-start | bytes 6291464 | tf_op jit(solution)/shard_map/slab/ppermute | solution.py:147
  78.1 22.6 %collective-permute-start.5 = (f32[4,2,4,8,512]{4,3,2,1,0:T(8,128)S(1)}, f32[4,2,4,8,512]{4,3,2,1,0:T(8,128)S(1)}, u32[]{:S(2)}, u32[]{:S(2)}) collective-permute-start(f32[4,2,4,8,512]{4,3,2,1,0:T(8,128)S(1)} %bitcast.23), channel_id=1, source_target_pairs={{0,24},{8,0},{16,8},{24,16},{1,25},{9,1},{17,9},{25,17},{2,26},{10... | collective-permute-start | bytes 1572872 | tf_op jit(solution)/shard_map/gather_sides/ppermute | solution.py:135
  83.0 27.5 %collective-permute-start.4 = (f32[4,2,4,8,512]{4,3,2,1,0:T(8,128)S(1)}, f32[4,2,4,8,512]{4,3,2,1,0:T(8,128)S(1)}, u32[]{:S(2)}, u32[]{:S(2)}) collective-permute-start(f32[4,2,4,8,512]{4,3,2,1,0:T(8,128)S(1)} %bitcast.24), channel_id=1, source_target_pairs={{0,8},{8,16},{16,24},{24,0},{1,9},{9,17},{17,25},{25,1},{2,10},{10... | collective-permute-start | bytes 1572872 | tf_op jit(solution)/shard_map/gather_sides/ppermute | solution.py:135
  89.3 26.7 %collective-permute-start.9 = (f32[4,2,4,8,512]{4,3,2,1,0:T(8,128)S(1)}, f32[4,2,4,8,512]{4,3,2,1,0:T(8,128)S(1)}, u32[]{:S(2)}, u32[]{:S(2)}) collective-permute-start(f32[4,2,4,8,512]{4,3,2,1,0:T(8,128)S(1)} %get-tuple-element.26), channel_id=1, source_target_pairs={{0,16},{8,24},{16,0},{24,8},{1,17},{9,25},{17,1},{25,9},{2,18},{10... | collective-permute-start | bytes 1572872 | tf_op jit(solution)/shard_map/gather_across/ppermute | solution.py:135
  93.4 22.6 %collective-permute-start.1 = (f32[32,1024]{1,0:T(8,128)S(1)}, f32[32,1024]{1,0:T(8,128)S(1)}, u32[]{:S(2)}, u32[]{:S(2)}) collective-permute-start(f32[32,1024]{1,0:T(8,128)S(1)} %get-tuple-element.19), channel_id=1, source_target_pairs={{0,4},{2,6},{4,0},{6,2},{1,5},{3,7},{5,1},{7,3},{8,12},{10,14},{12... | collective-permute-start | bytes 393224 | tf_op jit(solution)/shard_map/own_y/ppermute | solution.py:135
  96.7 19.2 %collective-permute-start.2 = (f32[32,1024]{1,0:T(8,128)S(1)}, f32[32,1024]{1,0:T(8,128)S(1)}, u32[]{:S(2)}, u32[]{:S(2)}) collective-permute-start(f32[32,1024]{1,0:T(8,128)S(1)} %get-tuple-element.20), channel_id=1, source_target_pairs={{0,2},{2,4},{4,6},{6,0},{1,3},{3,5},{5,7},{7,1},{8,10},{10,12},{12... | collective-permute-start | bytes 393224 | tf_op jit(solution)/shard_map/own_y/ppermute | solution.py:135
  100.7 15.2 %collective-permute-start.3 = (f32[32,1024]{1,0:T(8,128)S(1)}, f32[32,1024]{1,0:T(8,128)S(1)}, u32[]{:S(2)}, u32[]{:S(2)}) collective-permute-start(f32[32,1024]{1,0:T(8,128)S(1)} %get-tuple-element.21), channel_id=1, source_target_pairs={{0,6},{2,0},{4,2},{6,4},{1,7},{3,1},{5,3},{7,5},{8,14},{10,8},{12,... | collective-permute-start | bytes 393224 | tf_op jit(solution)/shard_map/own_y/ppermute | solution.py:135
  120.9 16.8 %collective-permute-start.10 = (f32[32,1024]{1,0:T(8,128)S(1)}, f32[32,1024]{1,0:T(8,128)S(1)}, u32[]{:S(2)}, u32[]{:S(2)}) collective-permute-start(f32[32,1024]{1,0:T(8,128)S(1)} %get-tuple-element.28), channel_id=1, source_target_pairs={{0,4},{2,6},{4,0},{6,2},{1,5},{3,7},{5,1},{7,3},{8,12},{10,14},{12... | collective-permute-start | bytes 393224 | tf_op jit(solution)/shard_map/across_y/ppermute | solution.py:135
  124.2 21.8 %collective-permute-start.6 = (f32[64,1024]{1,0:T(8,128)}, f32[64,1024]{1,0:T(8,128)S(1)}, u32[]{:S(2)}, u32[]{:S(2)}) collective-permute-start(f32[64,1024]{1,0:T(8,128)} %get-tuple-element.23), channel_id=1, source_target_pairs={{0,4},{2,6},{4,0},{6,2},{1,5},{3,7},{5,1},{7,3},{8,12},{10,14},{12... | collective-permute-start | bytes 786440 | tf_op jit(solution)/shard_map/sides_y/ppermute | solution.py:135
  128.3 17.8 %collective-permute-start.7 = (f32[64,1024]{1,0:T(8,128)}, f32[64,1024]{1,0:T(8,128)S(1)}, u32[]{:S(2)}, u32[]{:S(2)}) collective-permute-start(f32[64,1024]{1,0:T(8,128)} %get-tuple-element.24), channel_id=1, source_target_pairs={{0,2},{2,4},{4,6},{6,0},{1,3},{3,5},{5,7},{7,1},{8,10},{10,12},{12... | collective-permute-start | bytes 786440 | tf_op jit(solution)/shard_map/sides_y/ppermute | solution.py:135
  130.7 15.4 %collective-permute-start.8 = (f32[64,1024]{1,0:T(8,128)S(1)}, f32[64,1024]{1,0:T(8,128)S(1)}, u32[]{:S(2)}, u32[]{:S(2)}) collective-permute-start(f32[64,1024]{1,0:T(8,128)S(1)} %get-tuple-element.25), channel_id=1, source_target_pairs={{0,6},{2,0},{4,2},{6,4},{1,7},{3,1},{5,3},{7,5},{8,14},{10,8},{12,... | collective-permute-start | bytes 786440 | tf_op jit(solution)/shard_map/sides_y/ppermute | solution.py:135
  134.1 7.1 %collective-permute-start.11 = (f32[32,1024]{1,0:T(8,128)}, f32[32,1024]{1,0:T(8,128)S(1)}, u32[]{:S(2)}, u32[]{:S(2)}) collective-permute-start(f32[32,1024]{1,0:T(8,128)} %get-tuple-element.29), channel_id=1, source_target_pairs={{0,2},{2,4},{4,6},{6,0},{1,3},{3,5},{5,7},{7,1},{8,10},{10,12},{12... | collective-permute-start | bytes 393224 | tf_op jit(solution)/shard_map/across_y/ppermute | solution.py:135
  137.7 8.3 %collective-permute-start.12 = (f32[32,1024]{1,0:T(8,128)}, f32[32,1024]{1,0:T(8,128)S(1)}, u32[]{:S(2)}, u32[]{:S(2)}) collective-permute-start(f32[32,1024]{1,0:T(8,128)} %get-tuple-element.30), channel_id=1, source_target_pairs={{0,6},{2,0},{4,2},{6,4},{1,7},{3,1},{5,3},{7,5},{8,14},{10,8},{12,... | collective-permute-start | bytes 393224 | tf_op jit(solution)/shard_map/across_y/ppermute | solution.py:135

commit v7 on v3

--- a/solution.py
+++ b/solution.py
@@ -44,47 +44,75 @@
 
 
 def ladder_body(count, core_ref, *refs):
-    t_refs, (own_ref, got_ref, out_ref, t_parts) = refs[:count], refs[count:]
+    t_hbm, (own_hbm, got_hbm, out_hbm) = refs[:count], refs[count : count + 3]
+    t_buf, v_buf, o_buf, t_parts, t_sem, v_sem, o_sem = refs[count + 3 :]
     core = core_ref[0]
     size = 32 * count
     rows = 4 * size
+    blocks = own_hbm.shape[0] // COLS
 
-    @pl.when(pl.program_id(0) == 0)
-    def _():
-        for side in range(2):
-            source = core if side == 0 else 1 - core
-            for xx in range(4):
-                wide = jnp.concatenate([t[low, source, xx] for low in range(4) for t in t_refs], axis=0)
-                high, low_part = split(wide)
-                t_parts[side, pl.ds(xx * size, size), :] = high
-                t_parts[side, pl.ds(rows + xx * size, size), :] = low_part
+    t_copies = [pltpu.make_async_copy(t_hbm[y], t_buf.at[y], t_sem.at[y]) for y in range(count)]
+    for copy in t_copies:
+        copy.start()
+    v_copies = []
+    for j in range(blocks):
+        for side, v_hbm in enumerate((own_hbm, got_hbm)):
+            at = pl.ds(j * COLS, COLS)
+            copy = pltpu.make_async_copy(v_hbm.at[at, :], v_buf.at[side, at, :], v_sem.at[j, side])
+            copy.start()
+            v_copies.append(copy)
+
+    for copy in t_copies:
+        copy.wait()
+    for side in range(2):
+        source = core if side == 0 else 1 - core
+        for xx in range(4):
+            wide = jnp.concatenate([t_buf[y, low, source, xx] for low in range(4) for y in range(count)], axis=0)
+            high, low_part = split(wide)
+            t_parts[side, pl.ds(xx * size, size), :] = high
+            t_parts[side, pl.ds(rows + xx * size, size), :] = low_part
 
     def dot(left, right):
         return lax.dot_general(left, right, NT, preferred_element_type=jnp.float32)
 
-    total = None
-    for side, v_ref in enumerate((own_ref, got_ref)):
-        high, low_part = split(v_ref[...])
-        both = dot(t_parts[side], high)
-        term = (both[rows:] + dot(t_parts[side, :rows], low_part)) + both[:rows]
-        total = term if total is None else total + term
-    out_ref[...] = total
+    o_copies = []
+    for j in range(blocks):
+        at = pl.ds(j * COLS, COLS)
+        total = None
+        for side in range(2):
+            v_copies[2 * j + side].wait()
+            high, low_part = split(v_buf[side, at, :])
+            both = dot(t_parts[side], high)
+            term = (both[rows:] + dot(t_parts[side, :rows], low_part)) + both[:rows]
+            total = term if total is None else total + term
+        o_buf[:, at] = total
+        copy = pltpu.make_async_copy(o_buf.at[:, at], out_hbm.at[:, at], o_sem.at[j])
+        copy.start()
+        o_copies.append(copy)
+    for copy in o_copies:
+        copy.wait()
 
 
 def ladder(core, chunks, slabs):
     width, depth = slabs[0].shape
-    rows = 128 * len(chunks)
+    count = len(chunks)
+    rows = 128 * count
+    blocks = width // COLS
+    hbm = pl.BlockSpec(memory_space=pltpu.HBM)
     return pl.pallas_call(
-        functools.partial(ladder_body, len(chunks)),
+        functools.partial(ladder_body, count),
         out_shape=jax.ShapeDtypeStruct((rows, width), jnp.float32),
-        grid_spec=pltpu.PrefetchScalarGridSpec(
-            num_scalar_prefetch=1,
-            grid=(width // COLS,),
-            in_specs=[pl.BlockSpec((4, 2, 4, 8, depth), lambda i, core: (0, 0, 0, 0, 0))] * len(chunks)
-            + [pl.BlockSpec((COLS, depth), lambda i, core: (i, 0))] * 2,
-            out_specs=pl.BlockSpec((rows, COLS), lambda i, core: (0, i)),
-            scratch_shapes=[pltpu.VMEM((2, 2 * rows, depth), jnp.bfloat16)],
-        ),
+        in_specs=[pl.BlockSpec(memory_space=pltpu.SMEM)] + [hbm] * (count + 2),
+        out_specs=hbm,
+        scratch_shapes=[
+            pltpu.VMEM((count, 4, 2, 4, 8, depth), jnp.float32),
+            pltpu.VMEM((2, width, depth), jnp.float32),
+            pltpu.VMEM((rows, width), jnp.float32),
+            pltpu.VMEM((2, 2 * rows, depth), jnp.bfloat16),
+            pltpu.SemaphoreType.DMA((count,)),
+            pltpu.SemaphoreType.DMA((blocks, 2)),
+            pltpu.SemaphoreType.DMA((blocks,)),
+        ],
         compiler_params=PARAMS,
         cost_estimate=COST,
     )(core, *chunks, *slabs)

time: 135 us -> 137 us (1.015)
  Pallas kernels: 15.9 us -> 17.6 us
    pallas_call x3, Pallas kernels: 13.5 us -> 15.2 us  [ladder(): pl.pallas_call(functools.partial(ladder_body, count), out_shape=jax.Shape...]
  transfers between devices with their start and end apart: 8 -> 8, of which waited for: 3 -> 3; matrix products, arithmetic and copies ran while one was open for 0% -> 0% of each run, Pallas kernels for 11% -> 12%
where the time goes in v7:
time: 137 us; the launch traced here: 136 us
  blocking collectives  55.9 us (41%)
  starting transfers between devices  30.4 us (22%)
  waiting for transfers between devices  27.9 us (20%)
  Pallas kernels  17.6 us (13%)
  local copies, waits for them, and re-layouts  4.07 us (3%)
    all_to_all x1, blocking collectives, per_device(): lax.all_to_all(jnp.broadcast_to(amplitudes[None], (8, 8, 512)), 'zh', 0, 0)  55.9 us
    pallas_call x3, Pallas kernels, ladder(): pl.pallas_call(functools.partial(ladder_body, count), out_shape=jax.Shape...  15.2 us
    all_to_all x3, starting transfers between devices, over_x(): return lax.all_to_all(partial.reshape(4, 4, -1, 8, 1024), 'x', 0, 0)  13.6 us
    all_to_all x3, waiting for transfers between devices, over_x(): return lax.all_to_all(partial.reshape(4, 4, -1, 8, 1024), 'x', 0, 0)  12.9 us
    all_to_all x1, waiting for transfers between devices, per_device(): near = lax.all_to_all(spread, ('zl', 'core'), 0, 0).reshape(4, 2, 4, 8, 512)  10.5 us
    ppermute x3, starting transfers between devices, around(): return lax.ppermute(value, 'y', [(i, (i + hops) % 4) for i in range(4)])  9.13 us
    all_to_all x1, starting transfers between devices, per_device(): near = lax.all_to_all(spread, ('zl', 'core'), 0, 0).reshape(4, 2, 4, 8, 512)  5.19 us
    ppermute x3, waiting for transfers between devices, around(): return lax.ppermute(value, 'y', [(i, (i + hops) % 4) for i in range(4)])  4.56 us
  transfers between devices with their start and end apart: 8, of which 3 were waited for; matrix products, arithmetic and copies ran while one was open for 0% of the time, Pallas kernels for 12%

profile of v7, /device:TPU:24, one launch (start us, length us, event | category | flops | bytes accessed | tf_op | source)
XLA Modules:
  0.0 136.0 jit_solution(9856015834967104539)
XLA Ops:
  0.0 0.0 copy-start.2
  0.0 0.7 broadcast_in_dim.21
  0.7 55.9 %all_to_all.25 = f32[8,8,512]{2,1,0:T(8,128)S(1)} all-to-all(f32[8,8,512]{2,1,0:T(8,128)S(1)} %broadcast_in_dim.21), channel_id=1, replica_groups=mesh['zh'=8,'zl'=4,'y'=4,'x'=4,'core'=2] {'zh'}, dimensions={0} | all-to-all | bytes 262144 | tf_op jit(solution)/shard_map/gather_far/all_to_all | solution.py:167
  56.7 0.9 broadcast_in_dim.23
  57.5 5.2 %all-to-all-start.1 = ((f32[8,4,8,512]{3,2,1,0:T(8,128)}), f32[8,4,8,512]{3,2,1,0:T(8,128)}, u32[]{:S(2)}, u32[]{:S(2)}) async-start(f32[8,4,8,512]{3,2,1,0:T(8,128)} %bitcast.5), calls=%async_computation.1 | async-start | bytes 1048576 | tf_op jit(solution)/shard_map/gather_near/all_to_all | solution.py:171
  62.7 0.0 copy-done.2
  62.7 0.1 copy.6.allowed_ref
  62.8 0.0 copy-start
  62.8 1.6 %copy-done = f32[1024,512]{1,0:T(8,128)S(1)} copy-done((f32[1024,512]{1,0:T(8,128)S(1)}, f32[1024,512]{1,0:T(8,128)}, u32[]{:S(2)}) %copy-start) | copy-done | bytes 2097176
  64.4 0.8 slab.1.refs_1_.refs_2_
  65.3 2.4 %collective-permute-start = (f32[1024,512]{1,0:T(8,128)S(1)}, f32[1024,512]{1,0:T(8,128)}, u32[]{:S(2)}, u32[]{:S(2)}) collective-permute-start(f32[1024,512]{1,0:T(8,128)S(1)} %slab.1.refs_1_.refs_2_), channel_id=1, source_target_pairs={{0,1},{1,0},{2,3},{3,2},{4,5},{5,4},{6,7},{7,6},{8,9},{9,8},{10,11... | collective-permute-start | bytes 6291464 | tf_op jit(solution)/shard_map/slab/ppermute | solution.py:165
  67.7 10.5 %all-to-all-done.1 = f32[8,4,8,512]{3,2,1,0:T(8,128)} async-done(((f32[8,4,8,512]{3,2,1,0:T(8,128)}), f32[8,4,8,512]{3,2,1,0:T(8,128)}, u32[]{:S(2)}, u32[]{:S(2)}) %all-to-all-start.1) | async-done | bytes 524320 | tf_op jit(solution)/shard_map/gather_near/all_to_all | solution.py:171
  78.2 3.1 %collective-permute-start.3 = (f32[4,2,4,8,512]{4,3,2,1,0:T(8,128)}, f32[4,2,4,8,512]{4,3,2,1,0:T(8,128)S(1)}, u32[]{:S(2)}, u32[]{:S(2)}) collective-permute-start(f32[4,2,4,8,512]{4,3,2,1,0:T(8,128)} %bitcast.6.refs_0_), channel_id=1, source_target_pairs={{0,16},{8,24},{16,0},{24,8},{1,17},{9,25},{17,1},{25,9},{2,18},{10... | collective-permute-start | bytes 1572872 | tf_op jit(solution)/shard_map/gather_y/ppermute | solution.py:153
  81.3 0.0 collective-permute-done.refs_2_.refs_3_
  81.3 4.8 %own_y.1 = f32[128,1024]{1,0:T(8,128)} custom-call(s32[1]{0:T(128)} %bitcast.1.core_ref, f32[4,2,4,8,512]{4,3,2,1,0:T(8,128)} %bitcast.6.refs_0_, f32[1024,512]{1,0:T(8,128)S(1)} %slab.1.refs_1_.refs_2_, f32[1024,512]{1,0:T(8,128)} %collective-permute-done.refs_2_.refs_3_), custom_call_target="tpu_custom_call" | custom-call | flops 1 | bytes 1 | tf_op jit(solution)/shard_map/own_y/pallas_call | solution.py:102
  86.2 4.3 %all-to-all-start.2 = ((f32[4,4,1,8,1024]{4,3,2,1,0:T(8,128)}), f32[4,4,1,8,1024]{4,3,2,1,0:T(8,128)S(1)}, u32[]{:S(2)}, u32[]{:S(2)}) async-start(f32[4,4,1,8,1024]{4,3,2,1,0:T(8,128)} %bitcast.7), calls=%async_computation.2 | async-start | bytes 1048576 | tf_op jit(solution)/shard_map/own_y/all_to_all | solution.py:157
  90.5 4.1 %collective-permute-start.1 = (f32[4,2,4,8,512]{4,3,2,1,0:T(8,128)}, f32[4,2,4,8,512]{4,3,2,1,0:T(8,128)}, u32[]{:S(2)}, u32[]{:S(2)}) collective-permute-start(f32[4,2,4,8,512]{4,3,2,1,0:T(8,128)} %bitcast.6.refs_0_), channel_id=1, source_target_pairs={{0,8},{8,16},{16,24},{24,0},{1,9},{9,17},{17,25},{25,1},{2,10},{10... | collective-permute-start | bytes 1572872 | tf_op jit(solution)/shard_map/gather_y/ppermute | solution.py:153
  94.6 1.9 %collective-permute-start.2 = (f32[4,2,4,8,512]{4,3,2,1,0:T(8,128)}, f32[4,2,4,8,512]{4,3,2,1,0:T(8,128)}, u32[]{:S(2)}, u32[]{:S(2)}) collective-permute-start(f32[4,2,4,8,512]{4,3,2,1,0:T(8,128)} %bitcast.6.refs_0_), channel_id=1, source_target_pairs={{0,24},{8,0},{16,8},{24,16},{1,25},{9,1},{17,9},{25,17},{2,26},{10... | collective-permute-start | bytes 1572872 | tf_op jit(solution)/shard_map/gather_y/ppermute | solution.py:153
  96.5 0.0 collective-permute-done.3.refs_0_
  96.5 3.9 %across_y.1 = f32[128,1024]{1,0:T(8,128)S(1)} custom-call(s32[1]{0:T(128)} %bitcast.1.core_ref, f32[4,2,4,8,512]{4,3,2,1,0:T(8,128)S(1)} %collective-permute-done.3.refs_0_, f32[1024,512]{1,0:T(8,128)S(1)} %slab.1.refs_1_.refs_2_, f32[1024,512]{1,0:T(8,128)} %collective-permute-done.refs_2_.refs_3_), custom_call_target="tpu_custom_call" | custom-call | flops 1 | bytes 1 | tf_op jit(solution)/shard_map/across_y/pallas_call | solution.py:102
  100.5 0.0 copy-start.1
  100.5 0.8 copy-done.1
  101.3 0.0 all-to-all-done.2.own_ref
  101.3 4.8 %all-to-all-start.4 = ((f32[4,4,1,8,1024]{4,3,2,1,0:T(8,128)}), f32[4,4,1,8,1024]{4,3,2,1,0:T(8,128)S(1)}, u32[]{:S(2)}, u32[]{:S(2)}) async-start(f32[4,4,1,8,1024]{4,3,2,1,0:T(8,128)} %bitcast.13), calls=%async_computation.4 | async-start | bytes 1048576 | tf_op jit(solution)/shard_map/across_y/all_to_all | solution.py:157
  106.1 0.0 collective-permute-done.1.refs_0_
  106.1 4.5 %collective-permute-done.2.refs_1_ = f32[4,2,4,8,512]{4,3,2,1,0:T(8,128)} collective-permute-done((f32[4,2,4,8,512]{4,3,2,1,0:T(8,128)}, f32[4,2,4,8,512]{4,3,2,1,0:T(8,128)}, u32[]{:S(2)}, u32[]{:S(2)}) %collective-permute-start.2) | collective-permute-done | bytes 524320 | tf_op jit(solution)/shard_map/gather_y/ppermute | solution.py:153
  110.6 6.5 %sides_y.1 = f32[256,1024]{1,0:T(8,128)} custom-call(s32[1]{0:T(128)} %bitcast.1.core_ref, f32[4,2,4,8,512]{4,3,2,1,0:T(8,128)} %collective-permute-done.1.refs_0_, f32[4,2,4,8,512]{4,3,2,1,0:T(8,128)} %collective-permute-done.2.refs_1_, f32[1024,512]{1,0:T(8,128)S(1)} %slab.1.refs_1_.refs_2_, f32[1024,512]{1,0:T(8,128)} %collective-permute-done.refs_2_.refs_3_), custom_call_target="tpu_custom_call" | custom-call | flops 1 | bytes 1 | tf_op jit(solution)/shard_map/sides_y/pallas_call | solution.py:102
  117.1 0.0 all-to-all-done.4.across_ref
  117.1 4.5 %all-to-all-start.3 = ((f32[4,4,2,8,1024]{4,3,2,1,0:T(8,128)}), f32[4,4,2,8,1024]{4,3,2,1,0:T(8,128)S(1)}, u32[]{:S(2)}, u32[]{:S(2)}) async-start(f32[4,4,2,8,1024]{4,3,2,1,0:T(8,128)} %bitcast.8), calls=%async_computation.3 | async-start | bytes 2097152 | tf_op jit(solution)/shard_map/sides_y/all_to_all | solution.py:157
  121.6 12.9 %all-to-all-done.3.sides_ref = f32[4,4,2,8,1024]{4,3,2,1,0:T(8,128)S(1)} async-done(((f32[4,4,2,8,1024]{4,3,2,1,0:T(8,128)}), f32[4,4,2,8,1024]{4,3,2,1,0:T(8,128)S(1)}, u32[]{:S(2)}, u32[]{:S(2)}) %all-to-all-start.3) | async-done | bytes 1048608 | tf_op jit(solution)/shard_map/sides_y/all_to_all | solution.py:157
  134.5 1.5 %shard_map.37 = f32[4,4,8,1024]{3,2,1,0:T(8,128)} custom-call(s32[1]{0:T(128)} %bitcast.y_ref, f32[4,4,1,8,1024]{4,3,2,1,0:T(8,128)S(1)} %all-to-all-done.2.own_ref, f32[4,4,2,8,1024]{4,3,2,1,0:T(8,128)S(1)} %all-to-all-done.3.sides_ref, f32[4,4,1,8,1024]{4,3,2,1,0:T(8,128)S(1)} %all-to-all-done.4.across_ref), custom_call_target="tpu_custom_call" | custom-call | flops 1 | bytes 1 | tf_op jit(solution)/shard_map/pallas_call | solution.py:138
  (1 shorter events, 0.0 us)
Async XLA Ops:
  0.0 62.7 %copy-start.2 = (s32[8,4]{0,1:T(4,128)S(1)}, s32[8,4]{0,1:T(4,128)}, u32[]{:S(2)}) copy-start(s32[8,4]{0,1:T(4,128)} %param.5) | copy-start | bytes 388
  57.5 20.7 %all-to-all-start.1 = ((f32[8,4,8,512]{3,2,1,0:T(8,128)}), f32[8,4,8,512]{3,2,1,0:T(8,128)}, u32[]{:S(2)}, u32[]{:S(2)}) async-start(f32[8,4,8,512]{3,2,1,0:T(8,128)} %bitcast.5), calls=%async_computation.1 | async-start | bytes 1048576 | tf_op jit(solution)/shard_map/gather_near/all_to_all | solution.py:171
  62.8 1.6 %copy-start = (f32[1024,512]{1,0:T(8,128)S(1)}, f32[1024,512]{1,0:T(8,128)}, u32[]{:S(2)}) copy-start(f32[1024,512]{1,0:T(8,128)} %v_ref.1) | copy-start | bytes 6291460
  65.3 16.1 %collective-permute-start = (f32[1024,512]{1,0:T(8,128)S(1)}, f32[1024,512]{1,0:T(8,128)}, u32[]{:S(2)}, u32[]{:S(2)}) collective-permute-start(f32[1024,512]{1,0:T(8,128)S(1)} %slab.1.refs_1_.refs_2_), channel_id=1, source_target_pairs={{0,1},{1,0},{2,3},{3,2},{4,5},{5,4},{6,7},{7,6},{8,9},{9,8},{10,11... | collective-permute-start | bytes 6291464 | tf_op jit(solution)/shard_map/slab/ppermute | solution.py:165
  78.2 18.3 %collective-permute-start.3 = (f32[4,2,4,8,512]{4,3,2,1,0:T(8,128)}, f32[4,2,4,8,512]{4,3,2,1,0:T(8,128)S(1)}, u32[]{:S(2)}, u32[]{:S(2)}) collective-permute-start(f32[4,2,4,8,512]{4,3,2,1,0:T(8,128)} %bitcast.6.refs_0_), channel_id=1, source_target_pairs={{0,16},{8,24},{16,0},{24,8},{1,17},{9,25},{17,1},{25,9},{2,18},{10... | collective-permute-start | bytes 1572872 | tf_op jit(solution)/shard_map/gather_y/ppermute | solution.py:153
  86.2 15.1 %all-to-all-start.2 = ((f32[4,4,1,8,1024]{4,3,2,1,0:T(8,128)}), f32[4,4,1,8,1024]{4,3,2,1,0:T(8,128)S(1)}, u32[]{:S(2)}, u32[]{:S(2)}) async-start(f32[4,4,1,8,1024]{4,3,2,1,0:T(8,128)} %bitcast.7), calls=%async_computation.2 | async-start | bytes 1048576 | tf_op jit(solution)/shard_map/own_y/all_to_all | solution.py:157
  90.5 15.6 %collective-permute-start.1 = (f32[4,2,4,8,512]{4,3,2,1,0:T(8,128)}, f32[4,2,4,8,512]{4,3,2,1,0:T(8,128)}, u32[]{:S(2)}, u32[]{:S(2)}) collective-permute-start(f32[4,2,4,8,512]{4,3,2,1,0:T(8,128)} %bitcast.6.refs_0_), channel_id=1, source_target_pairs={{0,8},{8,16},{16,24},{24,0},{1,9},{9,17},{17,25},{25,1},{2,10},{10... | collective-permute-start | bytes 1572872 | tf_op jit(solution)/shard_map/gather_y/ppermute | solution.py:153
  94.6 16.1 %collective-permute-start.2 = (f32[4,2,4,8,512]{4,3,2,1,0:T(8,128)}, f32[4,2,4,8,512]{4,3,2,1,0:T(8,128)}, u32[]{:S(2)}, u32[]{:S(2)}) collective-permute-start(f32[4,2,4,8,512]{4,3,2,1,0:T(8,128)} %bitcast.6.refs_0_), channel_id=1, source_target_pairs={{0,24},{8,0},{16,8},{24,16},{1,25},{9,1},{17,9},{25,17},{2,26},{10... | collective-permute-start | bytes 1572872 | tf_op jit(solution)/shard_map/gather_y/ppermute | solution.py:153
  100.5 0.8 copy-start.1
  101.3 15.8 %all-to-all-start.4 = ((f32[4,4,1,8,1024]{4,3,2,1,0:T(8,128)}), f32[4,4,1,8,1024]{4,3,2,1,0:T(8,128)S(1)}, u32[]{:S(2)}, u32[]{:S(2)}) async-start(f32[4,4,1,8,1024]{4,3,2,1,0:T(8,128)} %bitcast.13), calls=%async_computation.4 | async-start | bytes 1048576 | tf_op jit(solution)/shard_map/across_y/all_to_all | solution.py:157
  117.1 17.4 %all-to-all-start.3 = ((f32[4,4,2,8,1024]{4,3,2,1,0:T(8,128)}), f32[4,4,2,8,1024]{4,3,2,1,0:T(8,128)S(1)}, u32[]{:S(2)}, u32[]{:S(2)}) async-start(f32[4,4,2,8,1024]{4,3,2,1,0:T(8,128)} %bitcast.8), calls=%async_computation.3 | async-start | bytes 2097152 | tf_op jit(solution)/shard_map/sides_y/all_to_all | solution.py:157

commit v8 on v7

v8 whole, which is shorter than its diff:
```python
import functools

import jax
import jax.numpy as jnp
from jax import lax
from jax.experimental import pallas as pl
from jax.experimental.pallas import tpu as pltpu
from jax.sharding import Mesh, PartitionSpec as P

BLK = 128
NT = (((1,), (1,)), ((), ()))
COLS = 256
PARAMS = pltpu.CompilerParams(vmem_limit_bytes=48 * 2**20)
COST = pl.CostEstimate(flops=1, bytes_accessed=1, transcendentals=0)


def split(wide):
    high = wide.astype(jnp.bfloat16)
    return high, (wide - high.astype(jnp.float32)).astype(jnp.bfloat16)


def mask_body(allowed_ref, v_ref, kept_ref, high_ref, low_ref):
    step = pl.program_id(0)
    for a in range(COLS // BLK):
        rows = pl.ds(a * BLK, BLK)
        for c in range(v_ref.shape[1] // BLK):
            cols = pl.ds(c * BLK, BLK)
            weight = allowed_ref[step * (COLS // BLK) + a, c].astype(jnp.float32)
            kept = v_ref[rows, cols] * weight
            kept_ref[rows, cols] = kept
            high_ref[rows, cols], low_ref[rows, cols] = split(kept)


def masked(integrals, allowed):
    rows, depth = integrals.shape
    block = pl.BlockSpec((COLS, depth), lambda i, allowed: (i, 0))
    return pl.pallas_call(
        mask_body,
        out_shape=[jax.ShapeDtypeStruct((rows, depth), t) for t in (jnp.float32, jnp.bfloat16, jnp.bfloat16)],
        grid_spec=pltpu.PrefetchScalarGridSpec(
            num_scalar_prefetch=1, grid=(rows // COLS,), in_specs=[block], out_specs=[block] * 3
        ),
        compiler_params=PARAMS,
        cost_estimate=COST,
    )(allowed, integrals)


def ladder_body(count, first, core_ref, *refs):
    t_hbm, (own_high, own_low), refs = refs[:count], refs[count : count + 2], refs[count + 2 :]
    if first:
        got_hbm, out_hbm, got_high, got_low, *refs = refs
    else:
        got_high, got_low, out_hbm, *refs = refs
    t_buf, high_buf, low_buf, o_buf, t_parts, t_sem, v_sem, o_sem, *rest = refs
    core = core_ref[0]
    size = 32 * count
    rows = 4 * size
    width, depth = own_high.shape
    blocks = width // COLS
    near_cols, far_cols = pl.ds(0, depth), pl.ds(depth, depth)

    def started(source, target, sem):
        copy = pltpu.make_async_copy(source, target, sem)
        copy.start()
        return copy

    t_copies = [started(t_hbm[y], t_buf.at[y], t_sem.at[y]) for y in range(count)]
    v_copies = []
    for j in range(blocks):
        at = pl.ds(j * COLS, COLS)
        block = [
            started(own_high.at[at, :], high_buf.at[at, near_cols], v_sem.at[j, 0]),
            started(own_low.at[at, :], low_buf.at[at, near_cols], v_sem.at[j, 1]),
        ]
        if first:
            block.append(started(got_hbm.at[at, :], rest[0].at[at, :], v_sem.at[j, 2]))
        else:
            block.append(started(got_high.at[at, :], high_buf.at[at, far_cols], v_sem.at[j, 2]))
            block.append(started(got_low.at[at, :], low_buf.at[at, far_cols], v_sem.at[j, 3]))
        v_copies.append(block)

    for copy in t_copies:
        copy.wait()
    for side, cols in enumerate((near_cols, far_cols)):
        source = core if side == 0 else 1 - core
        for xx in range(4):
            wide = jnp.concatenate([t_buf[y, low, source, xx] for low in range(4) for y in range(count)], axis=0)
            high, low_part = split(wide)
            t_parts[pl.ds(xx * size, size), cols] = high
            t_parts[pl.ds(rows + xx * size, size), cols] = low_part

    def dot(left, right):
        return lax.dot_general(left, right, NT, preferred_element_type=jnp.float32)

    o_copies = []
    for j in range(blocks):
        at = pl.ds(j * COLS, COLS)
        for copy in v_copies[j]:
            copy.wait()
        if first:
            high_buf[at, far_cols], low_buf[at, far_cols] = split(rest[0][at, :])
            o_copies.append(started(high_buf.at[at, far_cols], got_high.at[at, :], rest[1].at[j, 0]))
            o_copies.append(started(low_buf.at[at, far_cols], got_low.at[at, :], rest[1].at[j, 1]))
        both = dot(t_parts[...], high_buf[at, :])
        o_buf[:, at] = (both[rows:] + dot(t_parts[:rows, :], low_buf[at, :])) + both[:rows]
        o_copies.append(started(o_buf.at[:, at], out_hbm.at[:, at], o_sem.at[j]))
    for copy in o_copies:
        copy.wait()


def ladder(core, chunks, own_parts, got):
    width, depth = own_parts[0].shape
    first = len(got) == 1
    count = len(chunks)
    rows = 128 * count
    blocks = width // COLS
    hbm = pl.BlockSpec(memory_space=pltpu.HBM)
    part = jax.ShapeDtypeStruct((width, depth), jnp.bfloat16)
    return pl.pallas_call(
        functools.partial(ladder_body, count, first),
        out_shape=[jax.ShapeDtypeStruct((rows, width), jnp.float32)] + [part] * (2 * first),
        in_specs=[pl.BlockSpec(memory_space=pltpu.SMEM)] + [hbm] * (count + 2 + len(got)),
        out_specs=[hbm] * (1 + 2 * first),
        scratch_shapes=[
            pltpu.VMEM((count, 4, 2, 4, 8, depth), jnp.float32),
            pltpu.VMEM((width, 2 * depth), jnp.bfloat16),
            pltpu.VMEM((width, 2 * depth), jnp.bfloat16),
            pltpu.VMEM((rows, width), jnp.float32),
            pltpu.VMEM((2 * rows, 2 * depth), jnp.bfloat16),
            pltpu.SemaphoreType.DMA((count,)),
            pltpu.SemaphoreType.DMA((blocks, 4)),
            pltpu.SemaphoreType.DMA((blocks,)),
        ]
        + [pltpu.VMEM((width, depth), jnp.float32), pltpu.SemaphoreType.DMA((blocks, 2))] * first,
        compiler_params=PARAMS,
        cost_estimate=COST,
    )(core, *chunks, *own_parts, *got)


def finish_body(y_ref, own_ref, sides_ref, across_ref, out_ref):
    me = y_ref[0]

    def put(offset, part_ref, k):
        place = lax.rem(me + offset, 4)
        out_ref[0, place] = (part_ref[0, 0, k] + part_ref[1, 0, k]) + (part_ref[2, 0, k] + part_ref[3, 0, k])

    put(0, own_ref, 0)
    put(3, sides_ref, 0)
    put(1, sides_ref, 1)
    put(2, across_ref, 0)


def finish(y, own, sides, across):
    def part(count):
        return pl.BlockSpec((4, 1, count, 8, 1024), lambda low, y: (0, low, 0, 0, 0))

    return pl.pallas_call(
        finish_body,
        out_shape=jax.ShapeDtypeStruct((4, 4, 8, 1024), jnp.float32),
        grid_spec=pltpu.PrefetchScalarGridSpec(
            num_scalar_prefetch=1,
            grid=(4,),
            in_specs=[part(1), part(2), part(1)],
            out_specs=pl.BlockSpec((1, 4, 8, 1024), lambda low, y: (low, 0, 0, 0)),
        ),
        compiler_params=PARAMS,
        cost_estimate=COST,
    )(y, own, sides, across)


def around(value, hops):
    return lax.ppermute(value, "y", [(i, (i + hops) % 4) for i in range(4)])


def over_x(partial):
    return lax.all_to_all(partial.reshape(4, 4, -1, 8, 1024), "x", 0, 0)


def per_device(integrals, amplitudes, allowed):
    core = lax.axis_index("core").astype(jnp.int32)[None]
    me = lax.axis_index("y").astype(jnp.int32)[None]
    with jax.named_scope("slab"):
        kept, *own_parts = masked(integrals, allowed)
        got = lax.ppermute(kept, "core", [(0, 1), (1, 0)])
    with jax.named_scope("gather_far"):
        far = lax.all_to_all(jnp.broadcast_to(amplitudes[None], (8, 8, 512)), "zh", 0, 0)
    with jax.named_scope("gather_near"):
        by_core = far.reshape(1, 4, 2, 8, 512).swapaxes(1, 2)
        spread = jnp.broadcast_to(by_core, (4, 2, 4, 8, 512)).reshape(8, 4, 8, 512)
        near = lax.all_to_all(spread, ("zl", "core"), 0, 0).reshape(4, 2, 4, 8, 512)
    with jax.named_scope("gather_y"):
        below, above = around(near, 1), around(near, 3)
        across = around(near, 2)
    with jax.named_scope("own_y"):
        own, *got_parts = ladder(core, [near], own_parts, [got])
        own = over_x(own)
    with jax.named_scope("sides_y"):
        sides = over_x(*ladder(core, [below, above], own_parts, got_parts))
    with jax.named_scope("across_y"):
        opposite = over_x(*ladder(core, [across], own_parts, got_parts))
    return finish(me, own, sides, opposite).reshape(128, 1024)


def solution(mesh):
    fine = Mesh(mesh.devices.reshape(8, 4, 4, 4, 2), ("zh", "zl", "y", "x", "core"))
    rows, cols = ("zh", "zl", "y"), ("x", "core")
    return jax.shard_map(
        per_device, mesh=fine, in_specs=(P(rows, cols),) * 3, out_specs=P(cols, rows), check_vma=False
    )
```

time: 137 us -> 140 us (1.022)
  Pallas kernels: 17.6 us -> 23.1 us
  waiting for transfers between devices: 27.9 us -> 24.6 us
    pallas_call x4, Pallas kernels: 16.1 us -> 19.8 us  [the longest x3 15.2 us: ladder(): pl.pallas_call(functools.partial(ladder_body, count, first), out_shape=[j...]
    all_to_all x1, waiting for transfers between devices: 10.5 us -> 8.44 us  [per_device(): near = lax.all_to_all(spread, ('zl', 'core'), 0, 0).reshape(4, 2, 4, 8, 512)]
    pallas_call x1, Pallas kernels: 1.54 us -> 3.33 us  [finish(): pl.pallas_call(finish_body, out_shape=jax.ShapeDtypeStruct((4, 4, 8, 1024...]
    unnamed x7 -> x11, local copies, waits for them, and re-layouts: 2.47 us -> 3.87 us
  transfers between devices with their start and end apart: 8 -> 8, of which waited for: 3 -> 3; matrix products, arithmetic and copies ran while one was open for 0% -> 0% of each run, Pallas kernels for 12% -> 14%
where the time goes in v8:
time: 140 us
  blocking collectives  55.9 us (40%)
  starting transfers between devices  30.3 us (22%)
  waiting for transfers between devices  24.6 us (18%)
  Pallas kernels  23.1 us (16%)
  local copies, waits for them, and re-layouts  5.47 us (4%)
    all_to_all x1, blocking collectives, per_device(): lax.all_to_all(jnp.broadcast_to(amplitudes[None], (8, 8, 512)), 'zh', 0, 0)  55.9 us
    pallas_call x3, Pallas kernels, ladder(): pl.pallas_call(functools.partial(ladder_body, count, first), out_shape=[j...  15.2 us
    all_to_all x3, starting transfers between devices, over_x(): return lax.all_to_all(partial.reshape(4, 4, -1, 8, 1024), 'x', 0, 0)  13.6 us
    all_to_all x3, waiting for transfers between devices, over_x(): return lax.all_to_all(partial.reshape(4, 4, -1, 8, 1024), 'x', 0, 0)  12.9 us
    ppermute x3, starting transfers between devices, around(): return lax.ppermute(value, 'y', [(i, (i + hops) % 4) for i in range(4)])  9.13 us
    all_to_all x1, waiting for transfers between devices, per_device(): near = lax.all_to_all(spread, ('zl', 'core'), 0, 0).reshape(4, 2, 4, 8, 512)  8.44 us
    all_to_all x1, starting transfers between devices, per_device(): near = lax.all_to_all(spread, ('zl', 'core'), 0, 0).reshape(4, 2, 4, 8, 512)  5.19 us
    pallas_call x1, Pallas kernels, masked(): pl.pallas_call(mask_body, out_shape=[jax.ShapeDtypeStruct((rows, depth),...  4.53 us
  transfers between devices with their start and end apart: 8, of which 3 were waited for; matrix products, arithmetic and copies ran while one was open for 0% of the time, Pallas kernels for 14%

profile of v8, /device:TPU:24, one launch (start us, length us, event | category | flops | bytes accessed | tf_op | source)
XLA Modules:
  0.0 139.5 jit_solution(6545293786410577131)
XLA Ops:
  0.0 0.0 copy-start.4
  0.0 0.7 broadcast_in_dim.21
  0.7 55.9 %all_to_all.25 = f32[8,8,512]{2,1,0:T(8,128)S(1)} all-to-all(f32[8,8,512]{2,1,0:T(8,128)S(1)} %broadcast_in_dim.21), channel_id=1, replica_groups=mesh['zh'=8,'zl'=4,'y'=4,'x'=4,'core'=2] {'zh'}, dimensions={0} | all-to-all | bytes 262144 | tf_op jit(solution)/shard_map/gather_far/all_to_all | solution.py:186
  56.7 0.9 broadcast_in_dim.23
  57.5 5.2 %all-to-all-start.1 = ((f32[8,4,8,512]{3,2,1,0:T(8,128)}), f32[8,4,8,512]{3,2,1,0:T(8,128)}, u32[]{:S(2)}, u32[]{:S(2)}) async-start(f32[8,4,8,512]{3,2,1,0:T(8,128)} %bitcast.5), calls=%async_computation.1 | async-start | bytes 1048576 | tf_op jit(solution)/shard_map/gather_near/all_to_all | solution.py:190
  62.7 0.0 copy-done.4
  62.7 0.1 copy.6.allowed_ref
  62.8 4.5 %slab.1 = (f32[1024,512]{1,0:T(8,128)}, bf16[1024,512]{1,0:T(8,128)(2,1)S(1)}, bf16[1024,512]{1,0:T(8,128)(2,1)S(1)}) custom-call(s32[8,4]{1,0:T(8,128)S(1)} %copy.6.allowed_ref, f32[1024,512]{1,0:T(8,128)} %v_ref.1), custom_call_target="tpu_custom_call" | custom-call | flops 1 | bytes 1 | tf_op jit(solution)/shard_map/slab/pallas_call | solution.py:37
  67.3 2.4 %collective-permute-start = (f32[1024,512]{1,0:T(8,128)}, f32[1024,512]{1,0:T(8,128)}, u32[]{:S(2)}, u32[]{:S(2)}) collective-permute-start(f32[1024,512]{1,0:T(8,128)} %get-tuple-element.13), channel_id=1, source_target_pairs={{0,1},{1,0},{2,3},{3,2},{4,5},{5,4},{6,7},{7,6},{8,9},{9,8},{10,11... | collective-permute-start | bytes 6291464 | tf_op jit(solution)/shard_map/slab/ppermute | solution.py:184
  69.7 8.4 %all-to-all-done.1 = f32[8,4,8,512]{3,2,1,0:T(8,128)} async-done(((f32[8,4,8,512]{3,2,1,0:T(8,128)}), f32[8,4,8,512]{3,2,1,0:T(8,128)}, u32[]{:S(2)}, u32[]{:S(2)}) %all-to-all-start.1) | async-done | bytes 524320 | tf_op jit(solution)/shard_map/gather_near/all_to_all | solution.py:190
  78.2 3.1 %collective-permute-start.3 = (f32[4,2,4,8,512]{4,3,2,1,0:T(8,128)}, f32[4,2,4,8,512]{4,3,2,1,0:T(8,128)}, u32[]{:S(2)}, u32[]{:S(2)}) collective-permute-start(f32[4,2,4,8,512]{4,3,2,1,0:T(8,128)} %bitcast.6.refs_0_), channel_id=1, source_target_pairs={{0,16},{8,24},{16,0},{24,8},{1,17},{9,25},{17,1},{25,9},{2,18},{10... | collective-permute-start | bytes 1572872 | tf_op jit(solution)/shard_map/gather_y/ppermute | solution.py:172
  81.3 0.0 collective-permute-done.refs_3_
  81.3 4.8 %own_y.1 = (f32[128,1024]{1,0:T(8,128)S(1)}, bf16[1024,512]{1,0:T(8,128)(2,1)S(1)}, bf16[1024,512]{1,0:T(8,128)(2,1)S(1)}) custom-call(s32[1]{0:T(128)} %bitcast.1.core_ref, f32[4,2,4,8,512]{4,3,2,1,0:T(8,128)} %bitcast.6.refs_0_, bf16[1024,512]{1,0:T(8,128)(2,1)S(1)} %get-tuple-element.11.refs_1_.refs_2_, ...), custom_call_target="tpu_custom_call" | custom-call | flops 1 | bytes 1 | tf_op jit(solution)/shard_map/own_y/pallas_call | solution.py:119
  86.1 0.0 copy-start
  86.1 1.0 copy-done
  87.1 0.0 copy-start.3
  87.1 0.8 copy-done.3
  87.9 4.3 %all-to-all-start.2 = ((f32[4,4,1,8,1024]{4,3,2,1,0:T(8,128)}), f32[4,4,1,8,1024]{4,3,2,1,0:T(8,128)}, u32[]{:S(2)}, u32[]{:S(2)}) async-start(f32[4,4,1,8,1024]{4,3,2,1,0:T(8,128)} %bitcast.14), calls=%async_computation.2 | async-start | bytes 1048576 | tf_op jit(solution)/shard_map/own_y/all_to_all | solution.py:176
  92.2 4.1 %collective-permute-start.1 = (f32[4,2,4,8,512]{4,3,2,1,0:T(8,128)}, f32[4,2,4,8,512]{4,3,2,1,0:T(8,128)}, u32[]{:S(2)}, u32[]{:S(2)}) collective-permute-start(f32[4,2,4,8,512]{4,3,2,1,0:T(8,128)} %bitcast.6.refs_0_), channel_id=1, source_target_pairs={{0,8},{8,16},{16,24},{24,0},{1,9},{9,17},{17,25},{25,1},{2,10},{10... | collective-permute-start | bytes 1572872 | tf_op jit(solution)/shard_map/gather_y/ppermute | solution.py:172
  96.3 1.9 %collective-permute-start.2 = (f32[4,2,4,8,512]{4,3,2,1,0:T(8,128)}, f32[4,2,4,8,512]{4,3,2,1,0:T(8,128)}, u32[]{:S(2)}, u32[]{:S(2)}) collective-permute-start(f32[4,2,4,8,512]{4,3,2,1,0:T(8,128)} %bitcast.6.refs_0_), channel_id=1, source_target_pairs={{0,24},{8,0},{16,8},{24,16},{1,25},{9,1},{17,9},{25,17},{2,26},{10... | collective-permute-start | bytes 1572872 | tf_op jit(solution)/shard_map/gather_y/ppermute | solution.py:172
  98.2 0.0 collective-permute-done.3.refs_0_
  98.2 0.0 copy-start.1
  98.2 1.2 copy-done.1
  99.5 4.2 %across_y.1 = f32[128,1024]{1,0:T(8,128)S(1)} custom-call(s32[1]{0:T(128)} %bitcast.1.core_ref, f32[4,2,4,8,512]{4,3,2,1,0:T(8,128)} %collective-permute-done.3.refs_0_, bf16[1024,512]{1,0:T(8,128)(2,1)S(1)} %get-tuple-element.11.refs_1_.refs_2_, bf16[1024,512]{1,0:T(8,128)(2,1)S(1)} %get-tuple-element.12.refs_2_.refs_3_, ...), custom_call_target="tpu_custom_call" | custom-call | flops 1 | bytes 1 | tf_op jit(solution)/shard_map/across_y/pallas_call | solution.py:119
  103.7 0.0 copy-start.2
  103.7 0.8 copy-done.2
  104.5 0.0 all-to-all-done.2.own_ref
  104.5 4.8 %all-to-all-start.4 = ((f32[4,4,1,8,1024]{4,3,2,1,0:T(8,128)}), f32[4,4,1,8,1024]{4,3,2,1,0:T(8,128)}, u32[]{:S(2)}, u32[]{:S(2)}) async-start(f32[4,4,1,8,1024]{4,3,2,1,0:T(8,128)} %bitcast.13), calls=%async_computation.4 | async-start | bytes 1048576 | tf_op jit(solution)/shard_map/across_y/all_to_all | solution.py:176
  109.3 0.0 collective-permute-done.1.refs_0_
  109.3 3.2 %collective-permute-done.2.refs_1_ = f32[4,2,4,8,512]{4,3,2,1,0:T(8,128)} collective-permute-done((f32[4,2,4,8,512]{4,3,2,1,0:T(8,128)}, f32[4,2,4,8,512]{4,3,2,1,0:T(8,128)}, u32[]{:S(2)}, u32[]{:S(2)}) %collective-permute-start.2) | collective-permute-done | bytes 524320 | tf_op jit(solution)/shard_map/gather_y/ppermute | solution.py:172
  112.5 6.3 %sides_y.1 = f32[256,1024]{1,0:T(8,128)} custom-call(s32[1]{0:T(128)} %bitcast.1.core_ref, f32[4,2,4,8,512]{4,3,2,1,0:T(8,128)} %collective-permute-done.1.refs_0_, f32[4,2,4,8,512]{4,3,2,1,0:T(8,128)} %collective-permute-done.2.refs_1_, bf16[1024,512]{1,0:T(8,128)(2,1)S(1)} %get-tuple-element.11.refs_1_.refs_2_, ...), custom_call_target="tpu_custom_call" | custom-call | flops 1 | bytes 1 | tf_op jit(solution)/shard_map/sides_y/pallas_call | solution.py:119
  118.8 0.0 all-to-all-done.4.across_ref
  118.8 4.5 %all-to-all-start.3 = ((f32[4,4,2,8,1024]{4,3,2,1,0:T(8,128)}), f32[4,4,2,8,1024]{4,3,2,1,0:T(8,128)S(1)}, u32[]{:S(2)}, u32[]{:S(2)}) async-start(f32[4,4,2,8,1024]{4,3,2,1,0:T(8,128)} %bitcast.8), calls=%async_computation.3 | async-start | bytes 2097152 | tf_op jit(solution)/shard_map/sides_y/all_to_all | solution.py:176
  123.2 12.9 %all-to-all-done.3.sides_ref = f32[4,4,2,8,1024]{4,3,2,1,0:T(8,128)S(1)} async-done(((f32[4,4,2,8,1024]{4,3,2,1,0:T(8,128)}), f32[4,4,2,8,1024]{4,3,2,1,0:T(8,128)S(1)}, u32[]{:S(2)}, u32[]{:S(2)}) %all-to-all-start.3) | async-done | bytes 1048608 | tf_op jit(solution)/shard_map/sides_y/all_to_all | solution.py:176
  136.2 3.3 %shard_map.37 = f32[4,4,8,1024]{3,2,1,0:T(8,128)} custom-call(s32[1]{0:T(128)} %bitcast.y_ref, f32[4,4,1,8,1024]{4,3,2,1,0:T(8,128)} %all-to-all-done.2.own_ref, f32[4,4,2,8,1024]{4,3,2,1,0:T(8,128)S(1)} %all-to-all-done.3.sides_ref, f32[4,4,1,8,1024]{4,3,2,1,0:T(8,128)} %all-to-all-done.4.across_ref), custom_call_target="tpu_custom_call" | custom-call | flops 1 | bytes 1 | tf_op jit(solution)/shard_map/pallas_call | solution.py:157
  (1 shorter events, 0.0 us)
Async XLA Ops:
  0.0 62.7 %copy-start.4 = (s32[8,4]{0,1:T(4,128)S(1)}, s32[8,4]{0,1:T(4,128)}, u32[]{:S(2)}) copy-start(s32[8,4]{0,1:T(4,128)} %param.5) | copy-start | bytes 388
  57.5 20.7 %all-to-all-start.1 = ((f32[8,4,8,512]{3,2,1,0:T(8,128)}), f32[8,4,8,512]{3,2,1,0:T(8,128)}, u32[]{:S(2)}, u32[]{:S(2)}) async-start(f32[8,4,8,512]{3,2,1,0:T(8,128)} %bitcast.5), calls=%async_computation.1 | async-start | bytes 1048576 | tf_op jit(solution)/shard_map/gather_near/all_to_all | solution.py:190
  67.3 14.0 %collective-permute-start = (f32[1024,512]{1,0:T(8,128)}, f32[1024,512]{1,0:T(8,128)}, u32[]{:S(2)}, u32[]{:S(2)}) collective-permute-start(f32[1024,512]{1,0:T(8,128)} %get-tuple-element.13), channel_id=1, source_target_pairs={{0,1},{1,0},{2,3},{3,2},{4,5},{5,4},{6,7},{7,6},{8,9},{9,8},{10,11... | collective-permute-start | bytes 6291464 | tf_op jit(solution)/shard_map/slab/ppermute | solution.py:184
  78.2 20.0 %collective-permute-start.3 = (f32[4,2,4,8,512]{4,3,2,1,0:T(8,128)}, f32[4,2,4,8,512]{4,3,2,1,0:T(8,128)}, u32[]{:S(2)}, u32[]{:S(2)}) collective-permute-start(f32[4,2,4,8,512]{4,3,2,1,0:T(8,128)} %bitcast.6.refs_0_), channel_id=1, source_target_pairs={{0,16},{8,24},{16,0},{24,8},{1,17},{9,25},{17,1},{25,9},{2,18},{10... | collective-permute-start | bytes 1572872 | tf_op jit(solution)/shard_map/gather_y/ppermute | solution.py:172
  86.1 1.0 copy-start
  87.1 0.8 copy-start.3
  87.9 16.6 %all-to-all-start.2 = ((f32[4,4,1,8,1024]{4,3,2,1,0:T(8,128)}), f32[4,4,1,8,1024]{4,3,2,1,0:T(8,128)}, u32[]{:S(2)}, u32[]{:S(2)}) async-start(f32[4,4,1,8,1024]{4,3,2,1,0:T(8,128)} %bitcast.14), calls=%async_computation.2 | async-start | bytes 1048576 | tf_op jit(solution)/shard_map/own_y/all_to_all | solution.py:176
  92.2 17.1 %collective-permute-start.1 = (f32[4,2,4,8,512]{4,3,2,1,0:T(8,128)}, f32[4,2,4,8,512]{4,3,2,1,0:T(8,128)}, u32[]{:S(2)}, u32[]{:S(2)}) collective-permute-start(f32[4,2,4,8,512]{4,3,2,1,0:T(8,128)} %bitcast.6.refs_0_), channel_id=1, source_target_pairs={{0,8},{8,16},{16,24},{24,0},{1,9},{9,17},{17,25},{25,1},{2,10},{10... | collective-permute-start | bytes 1572872 | tf_op jit(solution)/shard_map/gather_y/ppermute | solution.py:172
  96.3 16.2 %collective-permute-start.2 = (f32[4,2,4,8,512]{4,3,2,1,0:T(8,128)}, f32[4,2,4,8,512]{4,3,2,1,0:T(8,128)}, u32[]{:S(2)}, u32[]{:S(2)}) collective-permute-start(f32[4,2,4,8,512]{4,3,2,1,0:T(8,128)} %bitcast.6.refs_0_), channel_id=1, source_target_pairs={{0,24},{8,0},{16,8},{24,16},{1,25},{9,1},{17,9},{25,17},{2,26},{10... | collective-permute-start | bytes 1572872 | tf_op jit(solution)/shard_map/gather_y/ppermute | solution.py:172
  98.2 1.2 copy-start.1
  103.7 0.8 copy-start.2
  104.5 14.3 %all-to-all-start.4 = ((f32[4,4,1,8,1024]{4,3,2,1,0:T(8,128)}), f32[4,4,1,8,1024]{4,3,2,1,0:T(8,128)}, u32[]{:S(2)}, u32[]{:S(2)}) async-start(f32[4,4,1,8,1024]{4,3,2,1,0:T(8,128)} %bitcast.13), calls=%async_computation.4 | async-start | bytes 1048576 | tf_op jit(solution)/shard_map/across_y/all_to_all | solution.py:176
  118.8 17.4 %all-to-all-start.3 = ((f32[4,4,2,8,1024]{4,3,2,1,0:T(8,128)}), f32[4,4,2,8,1024]{4,3,2,1,0:T(8,128)S(1)}, u32[]{:S(2)}, u32[]{:S(2)}) async-start(f32[4,4,2,8,1024]{4,3,2,1,0:T(8,128)} %bitcast.8), calls=%async_computation.3 | async-start | bytes 2097152 | tf_op jit(solution)/shard_map/sides_y/all_to_all | solution.py:176

commit v9 on v3

--- a/solution.py
+++ b/solution.py
@@ -136,7 +136,7 @@
         kept = masked(integrals, allowed)
         slabs = (kept, lax.ppermute(kept, "core", [(0, 1), (1, 0)]))
     with jax.named_scope("gather_far"):
-        far = lax.all_to_all(jnp.broadcast_to(amplitudes[None], (8, 8, 512)), "zh", 0, 0)
+        far = lax.all_gather(amplitudes, "zh")
     with jax.named_scope("gather_near"):
         by_core = far.reshape(1, 4, 2, 8, 512).swapaxes(1, 2)
         spread = jnp.broadcast_to(by_core, (4, 2, 4, 8, 512)).reshape(8, 4, 8, 512)

time: 135 us -> 130 us (0.963)
  blocking collectives: 55.9 us -> 52.8 us
    all_to_all x1 -> x0, blocking collectives: 55.9 us -> none  [per_device(): lax.all_to_all(jnp.broadcast_to(amplitudes[None], (8, 8, 512)), 'zh', 0, 0)]
    all_gather x0 -> x1, blocking collectives: none -> 52.8 us  [per_device(): far = lax.all_gather(amplitudes, 'zh')]
where the time goes in v9:
time: 130 us
  blocking collectives  52.8 us (41%)
  starting transfers between devices  29.2 us (22%)
  waiting for transfers between devices  28.2 us (22%)
  Pallas kernels  15.9 us (12%)
  local copies, waits for them, and re-layouts  3.33 us (3%)
    all_gather x1, blocking collectives, per_device(): far = lax.all_gather(amplitudes, 'zh')  52.8 us
    all_to_all x3, starting transfers between devices, over_x(): return lax.all_to_all(partial.reshape(4, 4, -1, 8, 1024), 'x', 0, 0)  13.6 us
    pallas_call x3, Pallas kernels, ladder(): pl.pallas_call(functools.partial(ladder_body, len(chunks)), out_shape=jax...  13.5 us
    all_to_all x3, waiting for transfers between devices, over_x(): return lax.all_to_all(partial.reshape(4, 4, -1, 8, 1024), 'x', 0, 0)  12.8 us
    all_to_all x1, waiting for transfers between devices, per_device(): near = lax.all_to_all(spread, ('zl', 'core'), 0, 0).reshape(4, 2, 4, 8, 512)  10.5 us
    ppermute x3, starting transfers between devices, around(): return lax.ppermute(value, 'y', [(i, (i + hops) % 4) for i in range(4)])  9.14 us
    ppermute x3, waiting for transfers between devices, around(): return lax.ppermute(value, 'y', [(i, (i + hops) % 4) for i in range(4)])  4.84 us
    all_to_all x1, starting transfers between devices, per_device(): near = lax.all_to_all(spread, ('zl', 'core'), 0, 0).reshape(4, 2, 4, 8, 512)  4.15 us
  transfers between devices with their start and end apart: 8, of which 3 were waited for; matrix products, arithmetic and copies ran while one was open for 0% of the time, Pallas kernels for 11%

profile of v9, /device:TPU:24, one launch (start us, length us, event | category | flops | bytes accessed | tf_op | source)
XLA Modules:
  0.0 129.5 jit_solution(3861119182566929232)
XLA Ops:
  0.0 0.0 copy-start.2
  0.0 52.8 %all-gather = f32[64,512]{1,0:T(8,128)S(1)} all-gather(f32[8,512]{1,0:T(8,128)} %param.4), channel_id=2, replica_groups=mesh['zh'=8,'zl'=4,'y'=4,'x'=4,'core'=2] {'zh'}, dimensions={0}, use_global_device_ids=true | all-gather | bytes 147456 | tf_op jit(solution)/shard_map/gather_far/all_gather | solution.py:139
  52.8 0.9 broadcast_in_dim.16
  53.6 4.2 %all-to-all-start = ((f32[8,4,8,512]{3,2,1,0:T(8,128)}), f32[8,4,8,512]{3,2,1,0:T(8,128)}, u32[]{:S(2)}, u32[]{:S(2)}) async-start(f32[8,4,8,512]{3,2,1,0:T(8,128)} %bitcast.5), calls=%async_computation | async-start | bytes 1048576 | tf_op jit(solution)/shard_map/gather_near/all_to_all | solution.py:143
  57.8 0.0 copy-done.2
  57.8 0.1 copy.5.allowed_ref
  57.9 0.0 copy-start
  57.9 1.6 %copy-done = f32[1024,512]{1,0:T(8,128)S(1)} copy-done((f32[1024,512]{1,0:T(8,128)S(1)}, f32[1024,512]{1,0:T(8,128)}, u32[]{:S(2)}) %copy-start) | copy-done | bytes 2097176
  59.5 0.8 slab.1.refs_1_.refs_2_
  60.3 2.3 %collective-permute-start = (f32[1024,512]{1,0:T(8,128)S(1)}, f32[1024,512]{1,0:T(8,128)}, u32[]{:S(2)}, u32[]{:S(2)}) collective-permute-start(f32[1024,512]{1,0:T(8,128)S(1)} %slab.1.refs_1_.refs_2_), channel_id=1, source_target_pairs={{0,1},{1,0},{2,3},{3,2},{4,5},{5,4},{6,7},{7,6},{8,9},{9,8},{10,11... | collective-permute-start | bytes 6291464 | tf_op jit(solution)/shard_map/slab/ppermute | solution.py:137
  62.6 10.5 %all-to-all-done = f32[8,4,8,512]{3,2,1,0:T(8,128)} async-done(((f32[8,4,8,512]{3,2,1,0:T(8,128)}), f32[8,4,8,512]{3,2,1,0:T(8,128)}, u32[]{:S(2)}, u32[]{:S(2)}) %all-to-all-start) | async-done | bytes 524320 | tf_op jit(solution)/shard_map/gather_near/all_to_all | solution.py:143
  73.2 3.1 %collective-permute-start.3 = (f32[4,2,4,8,512]{4,3,2,1,0:T(8,128)}, f32[4,2,4,8,512]{4,3,2,1,0:T(8,128)S(1)}, u32[]{:S(2)}, u32[]{:S(2)}) collective-permute-start(f32[4,2,4,8,512]{4,3,2,1,0:T(8,128)} %bitcast.6.refs_0_), channel_id=1, source_target_pairs={{0,16},{8,24},{16,0},{24,8},{1,17},{9,25},{17,1},{25,9},{2,18},{10... | collective-permute-start | bytes 1572872 | tf_op jit(solution)/shard_map/gather_y/ppermute | solution.py:125
  76.3 0.0 collective-permute-done.refs_2_.refs_3_
  76.3 4.6 %own_y.1 = f32[128,1024]{1,0:T(8,128)} custom-call(s32[1]{0:T(128)} %bitcast.1.core_ref, f32[4,2,4,8,512]{4,3,2,1,0:T(8,128)} %bitcast.6.refs_0_, f32[1024,512]{1,0:T(8,128)S(1)} %slab.1.refs_1_.refs_2_, f32[1024,512]{1,0:T(8,128)} %collective-permute-done.refs_2_.refs_3_), custom_call_target="tpu_custom_call" | custom-call | flops 1 | bytes 1 | tf_op jit(solution)/shard_map/own_y/pallas_call | solution.py:77
  80.9 4.3 %all-to-all-start.1 = ((f32[4,4,1,8,1024]{4,3,2,1,0:T(8,128)}), f32[4,4,1,8,1024]{4,3,2,1,0:T(8,128)S(1)}, u32[]{:S(2)}, u32[]{:S(2)}) async-start(f32[4,4,1,8,1024]{4,3,2,1,0:T(8,128)} %bitcast.7), calls=%async_computation.1 | async-start | bytes 1048576 | tf_op jit(solution)/shard_map/own_y/all_to_all | solution.py:129
  85.2 4.1 %collective-permute-start.1 = (f32[4,2,4,8,512]{4,3,2,1,0:T(8,128)}, f32[4,2,4,8,512]{4,3,2,1,0:T(8,128)}, u32[]{:S(2)}, u32[]{:S(2)}) collective-permute-start(f32[4,2,4,8,512]{4,3,2,1,0:T(8,128)} %bitcast.6.refs_0_), channel_id=1, source_target_pairs={{0,8},{8,16},{16,24},{24,0},{1,9},{9,17},{17,25},{25,1},{2,10},{10... | collective-permute-start | bytes 1572872 | tf_op jit(solution)/shard_map/gather_y/ppermute | solution.py:125
  89.3 1.9 %collective-permute-start.2 = (f32[4,2,4,8,512]{4,3,2,1,0:T(8,128)}, f32[4,2,4,8,512]{4,3,2,1,0:T(8,128)}, u32[]{:S(2)}, u32[]{:S(2)}) collective-permute-start(f32[4,2,4,8,512]{4,3,2,1,0:T(8,128)} %bitcast.6.refs_0_), channel_id=1, source_target_pairs={{0,24},{8,0},{16,8},{24,16},{1,25},{9,1},{17,9},{25,17},{2,26},{10... | collective-permute-start | bytes 1572872 | tf_op jit(solution)/shard_map/gather_y/ppermute | solution.py:125
  91.2 0.0 collective-permute-done.3.refs_0_
  91.2 3.6 %across_y.1 = f32[128,1024]{1,0:T(8,128)S(1)} custom-call(s32[1]{0:T(128)} %bitcast.1.core_ref, f32[4,2,4,8,512]{4,3,2,1,0:T(8,128)S(1)} %collective-permute-done.3.refs_0_, f32[1024,512]{1,0:T(8,128)S(1)} %slab.1.refs_1_.refs_2_, f32[1024,512]{1,0:T(8,128)} %collective-permute-done.refs_2_.refs_3_), custom_call_target="tpu_custom_call" | custom-call | flops 1 | bytes 1 | tf_op jit(solution)/shard_map/across_y/pallas_call | solution.py:77
  94.9 0.0 copy-start.1
  94.9 0.8 copy-done.1
  95.7 0.0 all-to-all-done.1.own_ref
  95.7 4.8 %all-to-all-start.3 = ((f32[4,4,1,8,1024]{4,3,2,1,0:T(8,128)}), f32[4,4,1,8,1024]{4,3,2,1,0:T(8,128)S(1)}, u32[]{:S(2)}, u32[]{:S(2)}) async-start(f32[4,4,1,8,1024]{4,3,2,1,0:T(8,128)} %bitcast.13), calls=%async_computation.3 | async-start | bytes 1048576 | tf_op jit(solution)/shard_map/across_y/all_to_all | solution.py:129
  100.5 0.0 collective-permute-done.1.refs_0_
  100.5 4.8 %collective-permute-done.2.refs_1_ = f32[4,2,4,8,512]{4,3,2,1,0:T(8,128)} collective-permute-done((f32[4,2,4,8,512]{4,3,2,1,0:T(8,128)}, f32[4,2,4,8,512]{4,3,2,1,0:T(8,128)}, u32[]{:S(2)}, u32[]{:S(2)}) %collective-permute-start.2) | collective-permute-done | bytes 524320 | tf_op jit(solution)/shard_map/gather_y/ppermute | solution.py:125
  105.3 5.3 %sides_y.1 = f32[256,1024]{1,0:T(8,128)} custom-call(s32[1]{0:T(128)} %bitcast.1.core_ref, f32[4,2,4,8,512]{4,3,2,1,0:T(8,128)} %collective-permute-done.1.refs_0_, f32[4,2,4,8,512]{4,3,2,1,0:T(8,128)} %collective-permute-done.2.refs_1_, f32[1024,512]{1,0:T(8,128)S(1)} %slab.1.refs_1_.refs_2_, f32[1024,512]{1,0:T(8,128)} %collective-permute-done.refs_2_.refs_3_), custom_call_target="tpu_custom_call" | custom-call | flops 1 | bytes 1 | tf_op jit(solution)/shard_map/sides_y/pallas_call | solution.py:77
  110.6 0.0 all-to-all-done.3.across_ref
  110.6 4.5 %all-to-all-start.2 = ((f32[4,4,2,8,1024]{4,3,2,1,0:T(8,128)}), f32[4,4,2,8,1024]{4,3,2,1,0:T(8,128)S(1)}, u32[]{:S(2)}, u32[]{:S(2)}) async-start(f32[4,4,2,8,1024]{4,3,2,1,0:T(8,128)} %bitcast.8), calls=%async_computation.2 | async-start | bytes 2097152 | tf_op jit(solution)/shard_map/sides_y/all_to_all | solution.py:129
  115.2 12.8 %all-to-all-done.2.sides_ref = f32[4,4,2,8,1024]{4,3,2,1,0:T(8,128)S(1)} async-done(((f32[4,4,2,8,1024]{4,3,2,1,0:T(8,128)}), f32[4,4,2,8,1024]{4,3,2,1,0:T(8,128)S(1)}, u32[]{:S(2)}, u32[]{:S(2)}) %all-to-all-start.2) | async-done | bytes 1048608 | tf_op jit(solution)/shard_map/sides_y/all_to_all | solution.py:129
  128.0 1.5 %shard_map.37 = f32[4,4,8,1024]{3,2,1,0:T(8,128)} custom-call(s32[1]{0:T(128)} %bitcast.y_ref, f32[4,4,1,8,1024]{4,3,2,1,0:T(8,128)S(1)} %all-to-all-done.1.own_ref, f32[4,4,2,8,1024]{4,3,2,1,0:T(8,128)S(1)} %all-to-all-done.2.sides_ref, f32[4,4,1,8,1024]{4,3,2,1,0:T(8,128)S(1)} %all-to-all-done.3.across_ref), custom_call_target="tpu_custom_call" | custom-call | flops 1 | bytes 1 | tf_op jit(solution)/shard_map/pallas_call | solution.py:110
  (1 shorter events, 0.0 us)
Async XLA Ops:
  0.0 57.8 %copy-start.2 = (s32[8,4]{0,1:T(4,128)S(1)}, s32[8,4]{0,1:T(4,128)}, u32[]{:S(2)}) copy-start(s32[8,4]{0,1:T(4,128)} %param.5) | copy-start | bytes 388
  53.6 19.5 %all-to-all-start = ((f32[8,4,8,512]{3,2,1,0:T(8,128)}), f32[8,4,8,512]{3,2,1,0:T(8,128)}, u32[]{:S(2)}, u32[]{:S(2)}) async-start(f32[8,4,8,512]{3,2,1,0:T(8,128)} %bitcast.5), calls=%async_computation | async-start | bytes 1048576 | tf_op jit(solution)/shard_map/gather_near/all_to_all | solution.py:143
  57.9 1.6 %copy-start = (f32[1024,512]{1,0:T(8,128)S(1)}, f32[1024,512]{1,0:T(8,128)}, u32[]{:S(2)}) copy-start(f32[1024,512]{1,0:T(8,128)} %v_ref.1) | copy-start | bytes 6291460
  60.3 16.0 %collective-permute-start = (f32[1024,512]{1,0:T(8,128)S(1)}, f32[1024,512]{1,0:T(8,128)}, u32[]{:S(2)}, u32[]{:S(2)}) collective-permute-start(f32[1024,512]{1,0:T(8,128)S(1)} %slab.1.refs_1_.refs_2_), channel_id=1, source_target_pairs={{0,1},{1,0},{2,3},{3,2},{4,5},{5,4},{6,7},{7,6},{8,9},{9,8},{10,11... | collective-permute-start | bytes 6291464 | tf_op jit(solution)/shard_map/slab/ppermute | solution.py:137
  73.2 18.1 %collective-permute-start.3 = (f32[4,2,4,8,512]{4,3,2,1,0:T(8,128)}, f32[4,2,4,8,512]{4,3,2,1,0:T(8,128)S(1)}, u32[]{:S(2)}, u32[]{:S(2)}) collective-permute-start(f32[4,2,4,8,512]{4,3,2,1,0:T(8,128)} %bitcast.6.refs_0_), channel_id=1, source_target_pairs={{0,16},{8,24},{16,0},{24,8},{1,17},{9,25},{17,1},{25,9},{2,18},{10... | collective-permute-start | bytes 1572872 | tf_op jit(solution)/shard_map/gather_y/ppermute | solution.py:125
  80.9 14.8 %all-to-all-start.1 = ((f32[4,4,1,8,1024]{4,3,2,1,0:T(8,128)}), f32[4,4,1,8,1024]{4,3,2,1,0:T(8,128)S(1)}, u32[]{:S(2)}, u32[]{:S(2)}) async-start(f32[4,4,1,8,1024]{4,3,2,1,0:T(8,128)} %bitcast.7), calls=%async_computation.1 | async-start | bytes 1048576 | tf_op jit(solution)/shard_map/own_y/all_to_all | solution.py:129
  85.2 15.3 %collective-permute-start.1 = (f32[4,2,4,8,512]{4,3,2,1,0:T(8,128)}, f32[4,2,4,8,512]{4,3,2,1,0:T(8,128)}, u32[]{:S(2)}, u32[]{:S(2)}) collective-permute-start(f32[4,2,4,8,512]{4,3,2,1,0:T(8,128)} %bitcast.6.refs_0_), channel_id=1, source_target_pairs={{0,8},{8,16},{16,24},{24,0},{1,9},{9,17},{17,25},{25,1},{2,10},{10... | collective-permute-start | bytes 1572872 | tf_op jit(solution)/shard_map/gather_y/ppermute | solution.py:125
  89.3 16.0 %collective-permute-start.2 = (f32[4,2,4,8,512]{4,3,2,1,0:T(8,128)}, f32[4,2,4,8,512]{4,3,2,1,0:T(8,128)}, u32[]{:S(2)}, u32[]{:S(2)}) collective-permute-start(f32[4,2,4,8,512]{4,3,2,1,0:T(8,128)} %bitcast.6.refs_0_), channel_id=1, source_target_pairs={{0,24},{8,0},{16,8},{24,16},{1,25},{9,1},{17,9},{25,17},{2,26},{10... | collective-permute-start | bytes 1572872 | tf_op jit(solution)/shard_map/gather_y/ppermute | solution.py:125
  94.9 0.8 copy-start.1
  95.7 15.0 %all-to-all-start.3 = ((f32[4,4,1,8,1024]{4,3,2,1,0:T(8,128)}), f32[4,4,1,8,1024]{4,3,2,1,0:T(8,128)S(1)}, u32[]{:S(2)}, u32[]{:S(2)}) async-start(f32[4,4,1,8,1024]{4,3,2,1,0:T(8,128)} %bitcast.13), calls=%async_computation.3 | async-start | bytes 1048576 | tf_op jit(solution)/shard_map/across_y/all_to_all | solution.py:129
  110.6 17.4 %all-to-all-start.2 = ((f32[4,4,2,8,1024]{4,3,2,1,0:T(8,128)}), f32[4,4,2,8,1024]{4,3,2,1,0:T(8,128)S(1)}, u32[]{:S(2)}, u32[]{:S(2)}) async-start(f32[4,4,2,8,1024]{4,3,2,1,0:T(8,128)} %bitcast.8), calls=%async_computation.2 | async-start | bytes 2097152 | tf_op jit(solution)/shard_map/sides_y/all_to_all | solution.py:129

commit v10 on v9

--- a/solution.py
+++ b/solution.py
@@ -10,6 +10,7 @@
 BLK = 128
 NT = (((1,), (1,)), ((), ()))
 COLS = 256
+WIDE = 512
 PARAMS = pltpu.CompilerParams(vmem_limit_bytes=48 * 2**20)
 COST = pl.CostEstimate(flops=1, bytes_accessed=1, transcendentals=0)
 
@@ -79,10 +80,10 @@
         out_shape=jax.ShapeDtypeStruct((rows, width), jnp.float32),
         grid_spec=pltpu.PrefetchScalarGridSpec(
             num_scalar_prefetch=1,
-            grid=(width // COLS,),
+            grid=(width // WIDE,),
             in_specs=[pl.BlockSpec((4, 2, 4, 8, depth), lambda i, core: (0, 0, 0, 0, 0))] * len(chunks)
-            + [pl.BlockSpec((COLS, depth), lambda i, core: (i, 0))] * 2,
-            out_specs=pl.BlockSpec((rows, COLS), lambda i, core: (0, i)),
+            + [pl.BlockSpec((WIDE, depth), lambda i, core: (i, 0))] * 2,
+            out_specs=pl.BlockSpec((rows, WIDE), lambda i, core: (0, i)),
             scratch_shapes=[pltpu.VMEM((2, 2 * rows, depth), jnp.bfloat16)],
         ),
         compiler_params=PARAMS,
@@ -93,27 +94,28 @@
 def finish_body(y_ref, own_ref, sides_ref, across_ref, out_ref):
     me = y_ref[0]
 
-    def put(offset, part_ref, k):
-        place = lax.rem(me + offset, 4)
-        out_ref[0, place] = (part_ref[0, 0, k] + part_ref[1, 0, k]) + (part_ref[2, 0, k] + part_ref[3, 0, k])
+    def put(offset, rows):
+        out_ref[0, lax.rem(me + offset, 4)] = rows
 
-    put(0, own_ref, 0)
-    put(3, sides_ref, 0)
-    put(1, sides_ref, 1)
-    put(2, across_ref, 0)
+    def summed(k):
+        return (sides_ref[0, 0, k] + sides_ref[1, 0, k]) + (sides_ref[2, 0, k] + sides_ref[3, 0, k])
+
+    put(0, own_ref[0])
+    put(3, summed(0))
+    put(1, summed(1))
+    put(2, across_ref[0])
 
 
 def finish(y, own, sides, across):
-    def part(count):
-        return pl.BlockSpec((4, 1, count, 8, 1024), lambda low, y: (0, low, 0, 0, 0))
-
+    total = pl.BlockSpec((1, 8, 1024), lambda low, y: (low, 0, 0))
+    parts = pl.BlockSpec((4, 1, 2, 8, 1024), lambda low, y: (0, low, 0, 0, 0))
     return pl.pallas_call(
         finish_body,
         out_shape=jax.ShapeDtypeStruct((4, 4, 8, 1024), jnp.float32),
         grid_spec=pltpu.PrefetchScalarGridSpec(
             num_scalar_prefetch=1,
             grid=(4,),
-            in_specs=[part(1), part(2), part(1)],
+            in_specs=[total, parts, total],
             out_specs=pl.BlockSpec((1, 4, 8, 1024), lambda low, y: (low, 0, 0, 0)),
         ),
         compiler_params=PARAMS,
@@ -123,6 +125,10 @@
 
 def around(value, hops):
     return lax.ppermute(value, "y", [(i, (i + hops) % 4) for i in range(4)])
+
+
+def summed_over_x(partial):
+    return lax.psum_scatter(partial, "x", scatter_dimension=0, tiled=True).reshape(4, 8, 1024)
 
 
 def over_x(partial):
@@ -145,11 +151,11 @@
         below, above = around(near, 1), around(near, 3)
         across = around(near, 2)
     with jax.named_scope("own_y"):
-        own = over_x(ladder(core, [near], slabs))
+        own = summed_over_x(ladder(core, [near], slabs))
     with jax.named_scope("sides_y"):
         sides = over_x(ladder(core, [below, above], slabs))
     with jax.named_scope("across_y"):
-        opposite = over_x(ladder(core, [across], slabs))
+        opposite = summed_over_x(ladder(core, [across], slabs))
     return finish(me, own, sides, opposite).reshape(128, 1024)
 
 

time: 130 us -> 166 us (1.28)
  waiting for transfers between devices: 28.2 us -> 61.4 us
  between operations: 0.11 us -> 13.5 us
  starting transfers between devices: 29.2 us -> 19.3 us
  Pallas kernels: 15.9 us -> 13.8 us
    reduce_scatter x0 -> x2, waiting for transfers between devices: none -> 20.3 us  [summed_over_x(): lax.psum_scatter(partial, 'x', scatter_dimension=0, tiled=True)]
    ppermute x3, waiting for transfers between devices: 4.84 us -> 15.4 us  [around(): return lax.ppermute(value, 'y', [(i, (i + hops) % 4) for i in range(4)])]
    all_to_all x3 -> x1, starting transfers between devices: 13.6 us -> 4.29 us  [over_x(): return lax.all_to_all(partial.reshape(4, 4, -1, 8, 1024), 'x', 0, 0)]
    all_to_all x1, waiting for transfers between devices: 10.5 us -> 6.5 us  [per_device(): near = lax.all_to_all(spread, ('zl', 'core'), 0, 0).reshape(4, 2, 4, 8, 512)]
    ppermute x1, waiting for transfers between devices: 0.01 us -> 3.91 us  [per_device(): slabs = (kept, lax.ppermute(kept, 'core', [(0, 1), (1, 0)]))]
    all_to_all x3 -> x1, waiting for transfers between devices: 12.8 us -> 15.3 us  [over_x(): return lax.all_to_all(partial.reshape(4, 4, -1, 8, 1024), 'x', 0, 0)]
    pallas_call x3, Pallas kernels: 13.5 us -> 11.5 us  [ladder(): pl.pallas_call(functools.partial(ladder_body, len(chunks)), out_shape=jax...]
    unnamed x7 -> x9, local copies, waits for them, and re-layouts: 2.47 us -> 3.48 us
  transfers between devices with their start and end apart: 8 -> 8, of which waited for: 3 -> 7; matrix products, arithmetic and copies ran while one was open for 0% -> 0% of each run, Pallas kernels for 11% -> 5%
where the time goes in v10:
time: 166 us; the launch traced here: 165 us
  waiting for transfers between devices  61.4 us (37%)
  blocking collectives  52.8 us (32%)
  starting transfers between devices  19.3 us (12%)
  Pallas kernels  13.8 us (8%)
  between operations  13.5 us (8%)
  local copies, waits for them, and re-layouts  4.35 us (3%)
    all_gather x1, blocking collectives, per_device(): far = lax.all_gather(amplitudes, 'zh')  52.8 us
    reduce_scatter x2, waiting for transfers between devices, summed_over_x(): lax.psum_scatter(partial, 'x', scatter_dimension=0, tiled=True)  20.3 us
    ppermute x3, waiting for transfers between devices, around(): return lax.ppermute(value, 'y', [(i, (i + hops) % 4) for i in range(4)])  15.4 us
    all_to_all x1, waiting for transfers between devices, over_x(): return lax.all_to_all(partial.reshape(4, 4, -1, 8, 1024), 'x', 0, 0)  15.3 us
    pallas_call x3, Pallas kernels, ladder(): pl.pallas_call(functools.partial(ladder_body, len(chunks)), out_shape=jax...  11.5 us
    ppermute x3, starting transfers between devices, around(): return lax.ppermute(value, 'y', [(i, (i + hops) % 4) for i in range(4)])  9.15 us
    all_to_all x1, waiting for transfers between devices, per_device(): near = lax.all_to_all(spread, ('zl', 'core'), 0, 0).reshape(4, 2, 4, 8, 512)  6.5 us
    all_to_all x1, starting transfers between devices, over_x(): return lax.all_to_all(partial.reshape(4, 4, -1, 8, 1024), 'x', 0, 0)  4.29 us
  transfers between devices with their start and end apart: 8, of which 7 were waited for; matrix products, arithmetic and copies ran while one was open for 0% of the time, Pallas kernels for 5%

profile of v10, /device:TPU:24, one launch (start us, length us, event | category | flops | bytes accessed | tf_op | source)
XLA Modules:
  0.0 165.1 jit_solution(12387153412116707106)
XLA Ops:
  6.5 0.0 copy-start.3
  6.5 52.8 %all-gather = f32[64,512]{1,0:T(8,128)S(1)} all-gather(f32[8,512]{1,0:T(8,128)} %param.4), channel_id=2, replica_groups=mesh['zh'=8,'zl'=4,'y'=4,'x'=4,'core'=2] {'zh'}, dimensions={0}, use_global_device_ids=true | all-gather | bytes 147456 | tf_op jit(solution)/shard_map/gather_far/all_gather | solution.py:145
  59.3 0.9 broadcast_in_dim.16
  60.2 3.5 %all-to-all-start = ((f32[8,4,8,512]{3,2,1,0:T(8,128)}), f32[8,4,8,512]{3,2,1,0:T(8,128)S(1)}, u32[]{:S(2)}, u32[]{:S(2)}) async-start(f32[8,4,8,512]{3,2,1,0:T(8,128)} %bitcast.5), calls=%async_computation | async-start | bytes 1048576 | tf_op jit(solution)/shard_map/gather_near/all_to_all | solution.py:149
  63.7 0.0 reduce-scatter.3.cloned.1.call-start
  63.7 0.0 copy-done.3
  63.7 0.1 copy.5.allowed_ref
  63.8 0.0 copy-start
  63.8 1.6 copy-done
  65.4 0.8 slab.1.refs_1_.refs_2_
  66.3 2.3 %collective-permute-start = (f32[1024,512]{1,0:T(8,128)S(1)}, f32[1024,512]{1,0:T(8,128)}, u32[]{:S(2)}, u32[]{:S(2)}) collective-permute-start(f32[1024,512]{1,0:T(8,128)S(1)} %slab.1.refs_1_.refs_2_), channel_id=1, source_target_pairs={{0,1},{1,0},{2,3},{3,2},{4,5},{5,4},{6,7},{7,6},{8,9},{9,8},{10,11... | collective-permute-start | bytes 6291464 | tf_op jit(solution)/shard_map/slab/ppermute | solution.py:143
  68.5 3.9 %collective-permute-done.refs_2_.refs_3_ = f32[1024,512]{1,0:T(8,128)} collective-permute-done((f32[1024,512]{1,0:T(8,128)S(1)}, f32[1024,512]{1,0:T(8,128)}, u32[]{:S(2)}, u32[]{:S(2)}) %collective-permute-start) | collective-permute-done | bytes 2097184 | tf_op jit(solution)/shard_map/slab/ppermute | solution.py:143
  72.5 6.5 %all-to-all-done = f32[8,4,8,512]{3,2,1,0:T(8,128)S(1)} async-done(((f32[8,4,8,512]{3,2,1,0:T(8,128)}), f32[8,4,8,512]{3,2,1,0:T(8,128)S(1)}, u32[]{:S(2)}, u32[]{:S(2)}) %all-to-all-start) | async-done | bytes 524320 | tf_op jit(solution)/shard_map/gather_near/all_to_all | solution.py:149
  79.0 3.6 %own_y.1 = f32[128,1024]{1,0:T(8,128)} custom-call(s32[1]{0:T(128)} %bitcast.1.core_ref, f32[4,2,4,8,512]{4,3,2,1,0:T(8,128)S(1)} %bitcast.13, f32[1024,512]{1,0:T(8,128)S(1)} %slab.1.refs_1_.refs_2_, f32[1024,512]{1,0:T(8,128)} %collective-permute-done.refs_2_.refs_3_), custom_call_target="tpu_custom_call" | custom-call | flops 1 | bytes 1 | tf_op jit(solution)/shard_map/own_y/pallas_call | solution.py:78
  82.5 0.0 reduce-scatter.3.cloned.1.call-update
  82.5 0.0 reduce-scatter.5.cloned.1.call-start
  82.6 3.1 %collective-permute-start.3 = (f32[4,2,4,8,512]{4,3,2,1,0:T(8,128)S(1)}, f32[4,2,4,8,512]{4,3,2,1,0:T(8,128)S(1)}, u32[]{:S(2)}, u32[]{:S(2)}) collective-permute-start(f32[4,2,4,8,512]{4,3,2,1,0:T(8,128)S(1)} %bitcast.14), channel_id=1, source_target_pairs={{0,16},{8,24},{16,0},{24,8},{1,17},{9,25},{17,1},{25,9},{2,18},{10... | collective-permute-start | bytes 1572872 | tf_op jit(solution)/shard_map/gather_y/ppermute | solution.py:127
  85.7 4.1 %collective-permute-start.1 = (f32[4,2,4,8,512]{4,3,2,1,0:T(8,128)S(1)}, f32[4,2,4,8,512]{4,3,2,1,0:T(8,128)S(1)}, u32[]{:S(2)}, u32[]{:S(2)}) collective-permute-start(f32[4,2,4,8,512]{4,3,2,1,0:T(8,128)S(1)} %bitcast.15), channel_id=1, source_target_pairs={{0,8},{8,16},{16,24},{24,0},{1,9},{9,17},{17,25},{25,1},{2,10},{10... | collective-permute-start | bytes 1572872 | tf_op jit(solution)/shard_map/gather_y/ppermute | solution.py:127
  89.8 1.9 %collective-permute-start.2 = (f32[4,2,4,8,512]{4,3,2,1,0:T(8,128)S(1)}, f32[4,2,4,8,512]{4,3,2,1,0:T(8,128)}, u32[]{:S(2)}, u32[]{:S(2)}) collective-permute-start(f32[4,2,4,8,512]{4,3,2,1,0:T(8,128)S(1)} %bitcast.16), channel_id=1, source_target_pairs={{0,24},{8,0},{16,8},{24,16},{1,25},{9,1},{17,9},{25,17},{2,26},{10... | collective-permute-start | bytes 1572872 | tf_op jit(solution)/shard_map/gather_y/ppermute | solution.py:127
  91.8 9.1 %collective-permute-done.3.refs_0_ = f32[4,2,4,8,512]{4,3,2,1,0:T(8,128)S(1)} collective-permute-done((f32[4,2,4,8,512]{4,3,2,1,0:T(8,128)S(1)}, f32[4,2,4,8,512]{4,3,2,1,0:T(8,128)S(1)}, u32[]{:S(2)}, u32[]{:S(2)}) %collective-permute-start.3) | collective-permute-done | bytes 524320 | tf_op jit(solution)/shard_map/gather_y/ppermute | solution.py:127
  100.9 3.6 %across_y.1 = f32[128,1024]{1,0:T(8,128)} custom-call(s32[1]{0:T(128)} %bitcast.1.core_ref, f32[4,2,4,8,512]{4,3,2,1,0:T(8,128)S(1)} %collective-permute-done.3.refs_0_, f32[1024,512]{1,0:T(8,128)S(1)} %slab.1.refs_1_.refs_2_, f32[1024,512]{1,0:T(8,128)} %collective-permute-done.refs_2_.refs_3_), custom_call_target="tpu_custom_call" | custom-call | flops 1 | bytes 1 | tf_op jit(solution)/shard_map/across_y/pallas_call | solution.py:78
  104.4 0.0 reduce-scatter.5.cloned.1.call-update
  104.4 3.8 %collective-permute-done.1.refs_0_ = f32[4,2,4,8,512]{4,3,2,1,0:T(8,128)S(1)} collective-permute-done((f32[4,2,4,8,512]{4,3,2,1,0:T(8,128)S(1)}, f32[4,2,4,8,512]{4,3,2,1,0:T(8,128)S(1)}, u32[]{:S(2)}, u32[]{:S(2)}) %collective-permute-start.1) | collective-permute-done | bytes 524320 | tf_op jit(solution)/shard_map/gather_y/ppermute | solution.py:127
  108.3 2.5 %collective-permute-done.2.refs_1_ = f32[4,2,4,8,512]{4,3,2,1,0:T(8,128)} collective-permute-done((f32[4,2,4,8,512]{4,3,2,1,0:T(8,128)S(1)}, f32[4,2,4,8,512]{4,3,2,1,0:T(8,128)}, u32[]{:S(2)}, u32[]{:S(2)}) %collective-permute-start.2) | collective-permute-done | bytes 524320 | tf_op jit(solution)/shard_map/gather_y/ppermute | solution.py:127
  110.8 4.4 %sides_y.1 = f32[256,1024]{1,0:T(8,128)} custom-call(s32[1]{0:T(128)} %bitcast.1.core_ref, f32[4,2,4,8,512]{4,3,2,1,0:T(8,128)S(1)} %collective-permute-done.1.refs_0_, f32[4,2,4,8,512]{4,3,2,1,0:T(8,128)} %collective-permute-done.2.refs_1_, f32[1024,512]{1,0:T(8,128)S(1)} %slab.1.refs_1_.refs_2_, f32[1024,512]{1,0:T(8,128)} %collective-permute-done.refs_2_.refs_3_), custom_call_target="tpu_custom_call" | custom-call | flops 1 | bytes 1 | tf_op jit(solution)/shard_map/sides_y/pallas_call | solution.py:78
  115.1 4.3 %all-to-all-start.1 = ((f32[4,4,2,8,1024]{4,3,2,1,0:T(8,128)}), f32[4,4,2,8,1024]{4,3,2,1,0:T(8,128)S(1)}, u32[]{:S(2)}, u32[]{:S(2)}) async-start(f32[4,4,2,8,1024]{4,3,2,1,0:T(8,128)} %bitcast.8), calls=%async_computation.2 | async-start | bytes 2097152 | tf_op jit(solution)/shard_map/sides_y/all_to_all | solution.py:135
  119.4 0.0 reduce-scatter.3.cloned.1.call-done
  119.4 15.3 %all-to-all-done.1.sides_ref = f32[4,4,2,8,1024]{4,3,2,1,0:T(8,128)S(1)} async-done(((f32[4,4,2,8,1024]{4,3,2,1,0:T(8,128)}), f32[4,4,2,8,1024]{4,3,2,1,0:T(8,128)S(1)}, u32[]{:S(2)}, u32[]{:S(2)}) %all-to-all-start.1) | async-done | bytes 1048608 | tf_op jit(solution)/shard_map/sides_y/all_to_all | solution.py:135
  134.7 20.3 %reduce-scatter.5.cloned.1.call-done = f32[32,1024]{1,0:T(8,128)} async-done(((f32[128,1024]{1,0:T(8,128)}), f32[32,1024]{1,0:T(8,128)}) %reduce-scatter.5.cloned.1.call-update) | async-done | bytes 131088 | tf_op jit(solution)/shard_map/across_y/reduce_scatter | solution.py:131
  155.0 0.0 copy-start.1
  155.0 0.9 copy-done.1
  155.9 0.0 copy-start.2
  155.9 0.9 copy-done.2
  156.8 1.5 shard_map.37
  (1 shorter events, 0.0 us)
Async XLA Ops:
  6.5 57.2 %copy-start.3 = (s32[8,4]{0,1:T(4,128)S(1)}, s32[8,4]{0,1:T(4,128)}, u32[]{:S(2)}) copy-start(s32[8,4]{0,1:T(4,128)} %param.5) | copy-start | bytes 388
  60.2 18.8 %all-to-all-start = ((f32[8,4,8,512]{3,2,1,0:T(8,128)}), f32[8,4,8,512]{3,2,1,0:T(8,128)S(1)}, u32[]{:S(2)}, u32[]{:S(2)}) async-start(f32[8,4,8,512]{3,2,1,0:T(8,128)} %bitcast.5), calls=%async_computation | async-start | bytes 1048576 | tf_op jit(solution)/shard_map/gather_near/all_to_all | solution.py:149
  63.7 55.8 %reduce-scatter.3.cloned.1.call-start = ((), (), s32[]{:S(2)}) async-start(), calls=%async_computation.4 | async-start | bytes 655360 | tf_op jit(solution)/shard_map/own_y/reduce_scatter | solution.py:131
  63.8 1.6 copy-start
  66.3 6.2 %collective-permute-start = (f32[1024,512]{1,0:T(8,128)S(1)}, f32[1024,512]{1,0:T(8,128)}, u32[]{:S(2)}, u32[]{:S(2)}) collective-permute-start(f32[1024,512]{1,0:T(8,128)S(1)} %slab.1.refs_1_.refs_2_), channel_id=1, source_target_pairs={{0,1},{1,0},{2,3},{3,2},{4,5},{5,4},{6,7},{7,6},{8,9},{9,8},{10,11... | collective-permute-start | bytes 6291464 | tf_op jit(solution)/shard_map/slab/ppermute | solution.py:143
  82.5 72.5 %reduce-scatter.5.cloned.1.call-start = ((), (), s32[]{:S(2)}) async-start(), calls=%async_computation.5 | async-start | bytes 655360 | tf_op jit(solution)/shard_map/across_y/reduce_scatter | solution.py:131
  82.6 18.3 %collective-permute-start.3 = (f32[4,2,4,8,512]{4,3,2,1,0:T(8,128)S(1)}, f32[4,2,4,8,512]{4,3,2,1,0:T(8,128)S(1)}, u32[]{:S(2)}, u32[]{:S(2)}) collective-permute-start(f32[4,2,4,8,512]{4,3,2,1,0:T(8,128)S(1)} %bitcast.14), channel_id=1, source_target_pairs={{0,16},{8,24},{16,0},{24,8},{1,17},{9,25},{17,1},{25,9},{2,18},{10... | collective-permute-start | bytes 1572872 | tf_op jit(solution)/shard_map/gather_y/ppermute | solution.py:127
  85.7 22.5 %collective-permute-start.1 = (f32[4,2,4,8,512]{4,3,2,1,0:T(8,128)S(1)}, f32[4,2,4,8,512]{4,3,2,1,0:T(8,128)S(1)}, u32[]{:S(2)}, u32[]{:S(2)}) collective-permute-start(f32[4,2,4,8,512]{4,3,2,1,0:T(8,128)S(1)} %bitcast.15), channel_id=1, source_target_pairs={{0,8},{8,16},{16,24},{24,0},{1,9},{9,17},{17,25},{25,1},{2,10},{10... | collective-permute-start | bytes 1572872 | tf_op jit(solution)/shard_map/gather_y/ppermute | solution.py:127
  89.8 20.9 %collective-permute-start.2 = (f32[4,2,4,8,512]{4,3,2,1,0:T(8,128)S(1)}, f32[4,2,4,8,512]{4,3,2,1,0:T(8,128)}, u32[]{:S(2)}, u32[]{:S(2)}) collective-permute-start(f32[4,2,4,8,512]{4,3,2,1,0:T(8,128)S(1)} %bitcast.16), channel_id=1, source_target_pairs={{0,24},{8,0},{16,8},{24,16},{1,25},{9,1},{17,9},{25,17},{2,26},{10... | collective-permute-start | bytes 1572872 | tf_op jit(solution)/shard_map/gather_y/ppermute | solution.py:127
  115.1 19.6 %all-to-all-start.1 = ((f32[4,4,2,8,1024]{4,3,2,1,0:T(8,128)}), f32[4,4,2,8,1024]{4,3,2,1,0:T(8,128)S(1)}, u32[]{:S(2)}, u32[]{:S(2)}) async-start(f32[4,4,2,8,1024]{4,3,2,1,0:T(8,128)} %bitcast.8), calls=%async_computation.2 | async-start | bytes 2097152 | tf_op jit(solution)/shard_map/sides_y/all_to_all | solution.py:135
  155.0 0.9 copy-start.1
  155.9 0.9 copy-start.2
Sparse Core Ops, SparseCore 0:
  82.7 29.5 reduce-scatter.2
  115.6 39.3 reduce-scatter.4

commit v11 on v9

--- a/solution.py
+++ b/solution.py
@@ -10,6 +10,7 @@
 BLK = 128
 NT = (((1,), (1,)), ((), ()))
 COLS = 256
+WIDE = 512
 PARAMS = pltpu.CompilerParams(vmem_limit_bytes=48 * 2**20)
 COST = pl.CostEstimate(flops=1, bytes_accessed=1, transcendentals=0)
 
@@ -79,10 +80,10 @@
         out_shape=jax.ShapeDtypeStruct((rows, width), jnp.float32),
         grid_spec=pltpu.PrefetchScalarGridSpec(
             num_scalar_prefetch=1,
-            grid=(width // COLS,),
+            grid=(width // WIDE,),
             in_specs=[pl.BlockSpec((4, 2, 4, 8, depth), lambda i, core: (0, 0, 0, 0, 0))] * len(chunks)
-            + [pl.BlockSpec((COLS, depth), lambda i, core: (i, 0))] * 2,
-            out_specs=pl.BlockSpec((rows, COLS), lambda i, core: (0, i)),
+            + [pl.BlockSpec((WIDE, depth), lambda i, core: (i, 0))] * 2,
+            out_specs=pl.BlockSpec((rows, WIDE), lambda i, core: (0, i)),
             scratch_shapes=[pltpu.VMEM((2, 2 * rows, depth), jnp.bfloat16)],
         ),
         compiler_params=PARAMS,

time: 130 us -> 128 us (0.985)
  Pallas kernels: 15.9 us -> 13.5 us
    pallas_call x3, Pallas kernels: 13.5 us -> 11.1 us  [ladder(): pl.pallas_call(functools.partial(ladder_body, len(chunks)), out_shape=jax...]
  transfers between devices with their start and end apart: 8 -> 8, of which waited for: 3 -> 4; matrix products, arithmetic and copies ran while one was open for 0% -> 0% of each run, Pallas kernels for 11% -> 9%
where the time goes in v11:
time: 128 us
  blocking collectives  52.8 us (41%)
  starting transfers between devices  29.2 us (23%)
  waiting for transfers between devices  29 us (23%)
  Pallas kernels  13.5 us (11%)
  local copies, waits for them, and re-layouts  3.33 us (3%)
    all_gather x1, blocking collectives, per_device(): far = lax.all_gather(amplitudes, 'zh')  52.8 us
    all_to_all x3, starting transfers between devices, over_x(): return lax.all_to_all(partial.reshape(4, 4, -1, 8, 1024), 'x', 0, 0)  13.6 us
    all_to_all x3, waiting for transfers between devices, over_x(): return lax.all_to_all(partial.reshape(4, 4, -1, 8, 1024), 'x', 0, 0)  12.9 us
    pallas_call x3, Pallas kernels, ladder(): pl.pallas_call(functools.partial(ladder_body, len(chunks)), out_shape=jax...  11.1 us
    all_to_all x1, waiting for transfers between devices, per_device(): near = lax.all_to_all(spread, ('zl', 'core'), 0, 0).reshape(4, 2, 4, 8, 512)  10.5 us
    ppermute x3, starting transfers between devices, around(): return lax.ppermute(value, 'y', [(i, (i + hops) % 4) for i in range(4)])  9.13 us
    ppermute x3, waiting for transfers between devices, around(): return lax.ppermute(value, 'y', [(i, (i + hops) % 4) for i in range(4)])  5.62 us
    all_to_all x1, starting transfers between devices, per_device(): near = lax.all_to_all(spread, ('zl', 'core'), 0, 0).reshape(4, 2, 4, 8, 512)  4.15 us
  transfers between devices with their start and end apart: 8, of which 4 were waited for; matrix products, arithmetic and copies ran while one was open for 0% of the time, Pallas kernels for 9%

profile of v11, /device:TPU:24, one launch (start us, length us, event | category | flops | bytes accessed | tf_op | source)
XLA Modules:
  0.0 127.9 jit_solution(17182956237263822898)
XLA Ops:
  0.0 0.0 copy-start.2
  0.0 52.8 %all-gather = f32[64,512]{1,0:T(8,128)S(1)} all-gather(f32[8,512]{1,0:T(8,128)} %param.4), channel_id=2, replica_groups=mesh['zh'=8,'zl'=4,'y'=4,'x'=4,'core'=2] {'zh'}, dimensions={0}, use_global_device_ids=true | all-gather | bytes 147456 | tf_op jit(solution)/shard_map/gather_far/all_gather | solution.py:140
  52.8 0.9 broadcast_in_dim.16
  53.6 4.2 %all-to-all-start = ((f32[8,4,8,512]{3,2,1,0:T(8,128)}), f32[8,4,8,512]{3,2,1,0:T(8,128)}, u32[]{:S(2)}, u32[]{:S(2)}) async-start(f32[8,4,8,512]{3,2,1,0:T(8,128)} %bitcast.5), calls=%async_computation | async-start | bytes 1048576 | tf_op jit(solution)/shard_map/gather_near/all_to_all | solution.py:144
  57.8 0.0 copy-done.2
  57.8 0.1 copy.5.allowed_ref
  57.9 0.0 copy-start
  57.9 1.6 %copy-done = f32[1024,512]{1,0:T(8,128)S(1)} copy-done((f32[1024,512]{1,0:T(8,128)S(1)}, f32[1024,512]{1,0:T(8,128)}, u32[]{:S(2)}) %copy-start) | copy-done | bytes 2097176
  59.5 0.8 slab.1.refs_1_.refs_2_
  60.3 2.3 %collective-permute-start = (f32[1024,512]{1,0:T(8,128)S(1)}, f32[1024,512]{1,0:T(8,128)}, u32[]{:S(2)}, u32[]{:S(2)}) collective-permute-start(f32[1024,512]{1,0:T(8,128)S(1)} %slab.1.refs_1_.refs_2_), channel_id=1, source_target_pairs={{0,1},{1,0},{2,3},{3,2},{4,5},{5,4},{6,7},{7,6},{8,9},{9,8},{10,11... | collective-permute-start | bytes 6291464 | tf_op jit(solution)/shard_map/slab/ppermute | solution.py:138
  62.6 10.5 %all-to-all-done = f32[8,4,8,512]{3,2,1,0:T(8,128)} async-done(((f32[8,4,8,512]{3,2,1,0:T(8,128)}), f32[8,4,8,512]{3,2,1,0:T(8,128)}, u32[]{:S(2)}, u32[]{:S(2)}) %all-to-all-start) | async-done | bytes 524320 | tf_op jit(solution)/shard_map/gather_near/all_to_all | solution.py:144
  73.2 3.1 %collective-permute-start.3 = (f32[4,2,4,8,512]{4,3,2,1,0:T(8,128)}, f32[4,2,4,8,512]{4,3,2,1,0:T(8,128)S(1)}, u32[]{:S(2)}, u32[]{:S(2)}) collective-permute-start(f32[4,2,4,8,512]{4,3,2,1,0:T(8,128)} %bitcast.6.refs_0_), channel_id=1, source_target_pairs={{0,16},{8,24},{16,0},{24,8},{1,17},{9,25},{17,1},{25,9},{2,18},{10... | collective-permute-start | bytes 1572872 | tf_op jit(solution)/shard_map/gather_y/ppermute | solution.py:126
  76.3 0.0 collective-permute-done.refs_2_.refs_3_
  76.3 3.7 %own_y.1 = f32[128,1024]{1,0:T(8,128)} custom-call(s32[1]{0:T(128)} %bitcast.1.core_ref, f32[4,2,4,8,512]{4,3,2,1,0:T(8,128)} %bitcast.6.refs_0_, f32[1024,512]{1,0:T(8,128)S(1)} %slab.1.refs_1_.refs_2_, f32[1024,512]{1,0:T(8,128)} %collective-permute-done.refs_2_.refs_3_), custom_call_target="tpu_custom_call" | custom-call | flops 1 | bytes 1 | tf_op jit(solution)/shard_map/own_y/pallas_call | solution.py:78
  80.0 4.3 %all-to-all-start.1 = ((f32[4,4,1,8,1024]{4,3,2,1,0:T(8,128)}), f32[4,4,1,8,1024]{4,3,2,1,0:T(8,128)S(1)}, u32[]{:S(2)}, u32[]{:S(2)}) async-start(f32[4,4,1,8,1024]{4,3,2,1,0:T(8,128)} %bitcast.7), calls=%async_computation.1 | async-start | bytes 1048576 | tf_op jit(solution)/shard_map/own_y/all_to_all | solution.py:130
  84.3 4.1 %collective-permute-start.1 = (f32[4,2,4,8,512]{4,3,2,1,0:T(8,128)}, f32[4,2,4,8,512]{4,3,2,1,0:T(8,128)}, u32[]{:S(2)}, u32[]{:S(2)}) collective-permute-start(f32[4,2,4,8,512]{4,3,2,1,0:T(8,128)} %bitcast.6.refs_0_), channel_id=1, source_target_pairs={{0,8},{8,16},{16,24},{24,0},{1,9},{9,17},{17,25},{25,1},{2,10},{10... | collective-permute-start | bytes 1572872 | tf_op jit(solution)/shard_map/gather_y/ppermute | solution.py:126
  88.4 1.9 %collective-permute-start.2 = (f32[4,2,4,8,512]{4,3,2,1,0:T(8,128)}, f32[4,2,4,8,512]{4,3,2,1,0:T(8,128)}, u32[]{:S(2)}, u32[]{:S(2)}) collective-permute-start(f32[4,2,4,8,512]{4,3,2,1,0:T(8,128)} %bitcast.6.refs_0_), channel_id=1, source_target_pairs={{0,24},{8,0},{16,8},{24,16},{1,25},{9,1},{17,9},{25,17},{2,26},{10... | collective-permute-start | bytes 1572872 | tf_op jit(solution)/shard_map/gather_y/ppermute | solution.py:126
  90.3 0.0 collective-permute-done.3.refs_0_
  90.3 2.9 %across_y.1 = f32[128,1024]{1,0:T(8,128)S(1)} custom-call(s32[1]{0:T(128)} %bitcast.1.core_ref, f32[4,2,4,8,512]{4,3,2,1,0:T(8,128)S(1)} %collective-permute-done.3.refs_0_, f32[1024,512]{1,0:T(8,128)S(1)} %slab.1.refs_1_.refs_2_, f32[1024,512]{1,0:T(8,128)} %collective-permute-done.refs_2_.refs_3_), custom_call_target="tpu_custom_call" | custom-call | flops 1 | bytes 1 | tf_op jit(solution)/shard_map/across_y/pallas_call | solution.py:78
  93.2 0.0 copy-start.1
  93.2 0.8 copy-done.1
  94.0 0.0 all-to-all-done.1.own_ref
  94.0 4.8 %all-to-all-start.3 = ((f32[4,4,1,8,1024]{4,3,2,1,0:T(8,128)}), f32[4,4,1,8,1024]{4,3,2,1,0:T(8,128)S(1)}, u32[]{:S(2)}, u32[]{:S(2)}) async-start(f32[4,4,1,8,1024]{4,3,2,1,0:T(8,128)} %bitcast.13), calls=%async_computation.3 | async-start | bytes 1048576 | tf_op jit(solution)/shard_map/across_y/all_to_all | solution.py:130
  98.8 0.6 collective-permute-done.1.refs_0_
  99.4 5.0 %collective-permute-done.2.refs_1_ = f32[4,2,4,8,512]{4,3,2,1,0:T(8,128)} collective-permute-done((f32[4,2,4,8,512]{4,3,2,1,0:T(8,128)}, f32[4,2,4,8,512]{4,3,2,1,0:T(8,128)}, u32[]{:S(2)}, u32[]{:S(2)}) %collective-permute-start.2) | collective-permute-done | bytes 524320 | tf_op jit(solution)/shard_map/gather_y/ppermute | solution.py:126
  104.4 4.5 %sides_y.1 = f32[256,1024]{1,0:T(8,128)} custom-call(s32[1]{0:T(128)} %bitcast.1.core_ref, f32[4,2,4,8,512]{4,3,2,1,0:T(8,128)} %collective-permute-done.1.refs_0_, f32[4,2,4,8,512]{4,3,2,1,0:T(8,128)} %collective-permute-done.2.refs_1_, f32[1024,512]{1,0:T(8,128)S(1)} %slab.1.refs_1_.refs_2_, f32[1024,512]{1,0:T(8,128)} %collective-permute-done.refs_2_.refs_3_), custom_call_target="tpu_custom_call" | custom-call | flops 1 | bytes 1 | tf_op jit(solution)/shard_map/sides_y/pallas_call | solution.py:78
  109.0 0.0 all-to-all-done.3.across_ref
  109.0 4.5 %all-to-all-start.2 = ((f32[4,4,2,8,1024]{4,3,2,1,0:T(8,128)}), f32[4,4,2,8,1024]{4,3,2,1,0:T(8,128)S(1)}, u32[]{:S(2)}, u32[]{:S(2)}) async-start(f32[4,4,2,8,1024]{4,3,2,1,0:T(8,128)} %bitcast.8), calls=%async_computation.2 | async-start | bytes 2097152 | tf_op jit(solution)/shard_map/sides_y/all_to_all | solution.py:130
  113.5 12.9 %all-to-all-done.2.sides_ref = f32[4,4,2,8,1024]{4,3,2,1,0:T(8,128)S(1)} async-done(((f32[4,4,2,8,1024]{4,3,2,1,0:T(8,128)}), f32[4,4,2,8,1024]{4,3,2,1,0:T(8,128)S(1)}, u32[]{:S(2)}, u32[]{:S(2)}) %all-to-all-start.2) | async-done | bytes 1048608 | tf_op jit(solution)/shard_map/sides_y/all_to_all | solution.py:130
  126.3 1.5 %shard_map.37 = f32[4,4,8,1024]{3,2,1,0:T(8,128)} custom-call(s32[1]{0:T(128)} %bitcast.y_ref, f32[4,4,1,8,1024]{4,3,2,1,0:T(8,128)S(1)} %all-to-all-done.1.own_ref, f32[4,4,2,8,1024]{4,3,2,1,0:T(8,128)S(1)} %all-to-all-done.2.sides_ref, f32[4,4,1,8,1024]{4,3,2,1,0:T(8,128)S(1)} %all-to-all-done.3.across_ref), custom_call_target="tpu_custom_call" | custom-call | flops 1 | bytes 1 | tf_op jit(solution)/shard_map/pallas_call | solution.py:111
  (1 shorter events, 0.0 us)
Async XLA Ops:
  0.0 57.8 %copy-start.2 = (s32[8,4]{0,1:T(4,128)S(1)}, s32[8,4]{0,1:T(4,128)}, u32[]{:S(2)}) copy-start(s32[8,4]{0,1:T(4,128)} %param.5) | copy-start | bytes 388
  53.6 19.5 %all-to-all-start = ((f32[8,4,8,512]{3,2,1,0:T(8,128)}), f32[8,4,8,512]{3,2,1,0:T(8,128)}, u32[]{:S(2)}, u32[]{:S(2)}) async-start(f32[8,4,8,512]{3,2,1,0:T(8,128)} %bitcast.5), calls=%async_computation | async-start | bytes 1048576 | tf_op jit(solution)/shard_map/gather_near/all_to_all | solution.py:144
  57.9 1.6 %copy-start = (f32[1024,512]{1,0:T(8,128)S(1)}, f32[1024,512]{1,0:T(8,128)}, u32[]{:S(2)}) copy-start(f32[1024,512]{1,0:T(8,128)} %v_ref.1) | copy-start | bytes 6291460
  60.3 16.0 %collective-permute-start = (f32[1024,512]{1,0:T(8,128)S(1)}, f32[1024,512]{1,0:T(8,128)}, u32[]{:S(2)}, u32[]{:S(2)}) collective-permute-start(f32[1024,512]{1,0:T(8,128)S(1)} %slab.1.refs_1_.refs_2_), channel_id=1, source_target_pairs={{0,1},{1,0},{2,3},{3,2},{4,5},{5,4},{6,7},{7,6},{8,9},{9,8},{10,11... | collective-permute-start | bytes 6291464 | tf_op jit(solution)/shard_map/slab/ppermute | solution.py:138
  73.2 17.2 %collective-permute-start.3 = (f32[4,2,4,8,512]{4,3,2,1,0:T(8,128)}, f32[4,2,4,8,512]{4,3,2,1,0:T(8,128)S(1)}, u32[]{:S(2)}, u32[]{:S(2)}) collective-permute-start(f32[4,2,4,8,512]{4,3,2,1,0:T(8,128)} %bitcast.6.refs_0_), channel_id=1, source_target_pairs={{0,16},{8,24},{16,0},{24,8},{1,17},{9,25},{17,1},{25,9},{2,18},{10... | collective-permute-start | bytes 1572872 | tf_op jit(solution)/shard_map/gather_y/ppermute | solution.py:126
  80.0 14.0 %all-to-all-start.1 = ((f32[4,4,1,8,1024]{4,3,2,1,0:T(8,128)}), f32[4,4,1,8,1024]{4,3,2,1,0:T(8,128)S(1)}, u32[]{:S(2)}, u32[]{:S(2)}) async-start(f32[4,4,1,8,1024]{4,3,2,1,0:T(8,128)} %bitcast.7), calls=%async_computation.1 | async-start | bytes 1048576 | tf_op jit(solution)/shard_map/own_y/all_to_all | solution.py:130
  84.3 15.1 %collective-permute-start.1 = (f32[4,2,4,8,512]{4,3,2,1,0:T(8,128)}, f32[4,2,4,8,512]{4,3,2,1,0:T(8,128)}, u32[]{:S(2)}, u32[]{:S(2)}) collective-permute-start(f32[4,2,4,8,512]{4,3,2,1,0:T(8,128)} %bitcast.6.refs_0_), channel_id=1, source_target_pairs={{0,8},{8,16},{16,24},{24,0},{1,9},{9,17},{17,25},{25,1},{2,10},{10... | collective-permute-start | bytes 1572872 | tf_op jit(solution)/shard_map/gather_y/ppermute | solution.py:126
  88.4 16.0 %collective-permute-start.2 = (f32[4,2,4,8,512]{4,3,2,1,0:T(8,128)}, f32[4,2,4,8,512]{4,3,2,1,0:T(8,128)}, u32[]{:S(2)}, u32[]{:S(2)}) collective-permute-start(f32[4,2,4,8,512]{4,3,2,1,0:T(8,128)} %bitcast.6.refs_0_), channel_id=1, source_target_pairs={{0,24},{8,0},{16,8},{24,16},{1,25},{9,1},{17,9},{25,17},{2,26},{10... | collective-permute-start | bytes 1572872 | tf_op jit(solution)/shard_map/gather_y/ppermute | solution.py:126
  93.2 0.8 copy-start.1
  94.0 14.9 %all-to-all-start.3 = ((f32[4,4,1,8,1024]{4,3,2,1,0:T(8,128)}), f32[4,4,1,8,1024]{4,3,2,1,0:T(8,128)S(1)}, u32[]{:S(2)}, u32[]{:S(2)}) async-start(f32[4,4,1,8,1024]{4,3,2,1,0:T(8,128)} %bitcast.13), calls=%async_computation.3 | async-start | bytes 1048576 | tf_op jit(solution)/shard_map/across_y/all_to_all | solution.py:130
  109.0 17.4 %all-to-all-start.2 = ((f32[4,4,2,8,1024]{4,3,2,1,0:T(8,128)}), f32[4,4,2,8,1024]{4,3,2,1,0:T(8,128)S(1)}, u32[]{:S(2)}, u32[]{:S(2)}) async-start(f32[4,4,2,8,1024]{4,3,2,1,0:T(8,128)} %bitcast.8), calls=%async_computation.2 | async-start | bytes 2097152 | tf_op jit(solution)/shard_map/sides_y/all_to_all | solution.py:130

commit v12 on v11

--- a/solution.py
+++ b/solution.py
@@ -94,13 +94,13 @@
 def finish_body(y_ref, own_ref, sides_ref, across_ref, out_ref):
     me = y_ref[0]
 
-    def put(offset, part_ref, k):
-        place = lax.rem(me + offset, 4)
+    def put(bits, part_ref, k):
+        place = lax.bitwise_xor(me, bits)
         out_ref[0, place] = (part_ref[0, 0, k] + part_ref[1, 0, k]) + (part_ref[2, 0, k] + part_ref[3, 0, k])
 
     put(0, own_ref, 0)
-    put(3, sides_ref, 0)
-    put(1, sides_ref, 1)
+    put(1, sides_ref, 0)
+    put(3, sides_ref, 1)
     put(2, across_ref, 0)
 
 
@@ -122,8 +122,8 @@
     )(y, own, sides, across)
 
 
-def around(value, hops):
-    return lax.ppermute(value, "y", [(i, (i + hops) % 4) for i in range(4)])
+def swapped(value, bits):
+    return lax.ppermute(value, "y", [(i, i ^ bits) for i in range(4)])
 
 
 def over_x(partial):
@@ -143,12 +143,12 @@
         spread = jnp.broadcast_to(by_core, (4, 2, 4, 8, 512)).reshape(8, 4, 8, 512)
         near = lax.all_to_all(spread, ("zl", "core"), 0, 0).reshape(4, 2, 4, 8, 512)
     with jax.named_scope("gather_y"):
-        below, above = around(near, 1), around(near, 3)
-        across = around(near, 2)
+        first, second = swapped(near, 1), swapped(near, 3)
+        across = swapped(near, 2)
     with jax.named_scope("own_y"):
         own = over_x(ladder(core, [near], slabs))
     with jax.named_scope("sides_y"):
-        sides = over_x(ladder(core, [below, above], slabs))
+        sides = over_x(ladder(core, [first, second], slabs))
     with jax.named_scope("across_y"):
         opposite = over_x(ladder(core, [across], slabs))
     return finish(me, own, sides, opposite).reshape(128, 1024)

time: 128 us -> 128 us (level); the launches traced: 128 us -> 126 us
  waiting for transfers between devices: 29 us -> 27.2 us
    ppermute x3, waiting for transfers between devices: 5.62 us -> 3.06 us  [swapped(): return lax.ppermute(value, 'y', [(i, i ^ bits) for i in range(4)])]
where the time goes in v12:
time: 128 us; the launch traced here: 126 us
  blocking collectives  52.8 us (41%)
  starting transfers between devices  29.3 us (23%)
  waiting for transfers between devices  27.2 us (21%)
  Pallas kernels  13.5 us (11%)
  local copies, waits for them, and re-layouts  3.33 us (3%)
    all_gather x1, blocking collectives, per_device(): far = lax.all_gather(amplitudes, 'zh')  52.8 us
    all_to_all x3, waiting for transfers between devices, over_x(): return lax.all_to_all(partial.reshape(4, 4, -1, 8, 1024), 'x', 0, 0)  13.6 us
    all_to_all x3, starting transfers between devices, over_x(): return lax.all_to_all(partial.reshape(4, 4, -1, 8, 1024), 'x', 0, 0)  13.1 us
    pallas_call x3, Pallas kernels, ladder(): pl.pallas_call(functools.partial(ladder_body, len(chunks)), out_shape=jax...  11.1 us
    all_to_all x1, waiting for transfers between devices, per_device(): near = lax.all_to_all(spread, ('zl', 'core'), 0, 0).reshape(4, 2, 4, 8, 512)  10.5 us
    ppermute x3, starting transfers between devices, swapped(): return lax.ppermute(value, 'y', [(i, i ^ bits) for i in range(4)])  9.79 us
    all_to_all x1, starting transfers between devices, per_device(): near = lax.all_to_all(spread, ('zl', 'core'), 0, 0).reshape(4, 2, 4, 8, 512)  4.15 us
    ppermute x3, waiting for transfers between devices, swapped(): return lax.ppermute(value, 'y', [(i, i ^ bits) for i in range(4)])  3.06 us
  transfers between devices with their start and end apart: 8, of which 4 were waited for; matrix products, arithmetic and copies ran while one was open for 0% of the time, Pallas kernels for 9%

profile of v12, /device:TPU:24, one launch (start us, length us, event | category | flops | bytes accessed | tf_op | source)
XLA Modules:
  0.0 126.3 jit_solution(4942719444729738713)
XLA Ops:
  0.0 0.0 copy-start.2
  0.0 52.8 %all-gather = f32[64,512]{1,0:T(8,128)S(1)} all-gather(f32[8,512]{1,0:T(8,128)} %param.4), channel_id=2, replica_groups=mesh['zh'=8,'zl'=4,'y'=4,'x'=4,'core'=2] {'zh'}, dimensions={0}, use_global_device_ids=true | all-gather | bytes 147456 | tf_op jit(solution)/shard_map/gather_far/all_gather | solution.py:140
  52.8 0.9 broadcast_in_dim.16
  53.6 4.2 %all-to-all-start = ((f32[8,4,8,512]{3,2,1,0:T(8,128)}), f32[8,4,8,512]{3,2,1,0:T(8,128)}, u32[]{:S(2)}, u32[]{:S(2)}) async-start(f32[8,4,8,512]{3,2,1,0:T(8,128)} %bitcast.5), calls=%async_computation | async-start | bytes 1048576 | tf_op jit(solution)/shard_map/gather_near/all_to_all | solution.py:144
  57.8 0.0 copy-done.2
  57.8 0.1 copy.5.allowed_ref
  57.9 0.0 copy-start
  57.9 1.6 %copy-done = f32[1024,512]{1,0:T(8,128)S(1)} copy-done((f32[1024,512]{1,0:T(8,128)S(1)}, f32[1024,512]{1,0:T(8,128)}, u32[]{:S(2)}) %copy-start) | copy-done | bytes 2097176
  59.5 0.8 slab.1.refs_1_.refs_2_
  60.3 2.3 %collective-permute-start = (f32[1024,512]{1,0:T(8,128)S(1)}, f32[1024,512]{1,0:T(8,128)}, u32[]{:S(2)}, u32[]{:S(2)}) collective-permute-start(f32[1024,512]{1,0:T(8,128)S(1)} %slab.1.refs_1_.refs_2_), channel_id=1, source_target_pairs={{0,1},{1,0},{2,3},{3,2},{4,5},{5,4},{6,7},{7,6},{8,9},{9,8},{10,11... | collective-permute-start | bytes 6291464 | tf_op jit(solution)/shard_map/slab/ppermute | solution.py:138
  62.6 10.5 %all-to-all-done = f32[8,4,8,512]{3,2,1,0:T(8,128)} async-done(((f32[8,4,8,512]{3,2,1,0:T(8,128)}), f32[8,4,8,512]{3,2,1,0:T(8,128)}, u32[]{:S(2)}, u32[]{:S(2)}) %all-to-all-start) | async-done | bytes 524320 | tf_op jit(solution)/shard_map/gather_near/all_to_all | solution.py:144
  73.2 3.1 %collective-permute-start.3 = (f32[4,2,4,8,512]{4,3,2,1,0:T(8,128)}, f32[4,2,4,8,512]{4,3,2,1,0:T(8,128)S(1)}, u32[]{:S(2)}, u32[]{:S(2)}) collective-permute-start(f32[4,2,4,8,512]{4,3,2,1,0:T(8,128)} %bitcast.6.refs_0_), channel_id=1, source_target_pairs={{0,16},{8,24},{16,0},{24,8},{1,17},{9,25},{17,1},{25,9},{2,18},{10... | collective-permute-start | bytes 1572872 | tf_op jit(solution)/shard_map/gather_y/ppermute | solution.py:126
  76.3 0.0 collective-permute-done.refs_2_.refs_3_
  76.3 3.7 %own_y.1 = f32[128,1024]{1,0:T(8,128)} custom-call(s32[1]{0:T(128)} %bitcast.1.core_ref, f32[4,2,4,8,512]{4,3,2,1,0:T(8,128)} %bitcast.6.refs_0_, f32[1024,512]{1,0:T(8,128)S(1)} %slab.1.refs_1_.refs_2_, f32[1024,512]{1,0:T(8,128)} %collective-permute-done.refs_2_.refs_3_), custom_call_target="tpu_custom_call" | custom-call | flops 1 | bytes 1 | tf_op jit(solution)/shard_map/own_y/pallas_call | solution.py:78
  80.0 4.3 %all-to-all-start.1 = ((f32[4,4,1,8,1024]{4,3,2,1,0:T(8,128)}), f32[4,4,1,8,1024]{4,3,2,1,0:T(8,128)S(1)}, u32[]{:S(2)}, u32[]{:S(2)}) async-start(f32[4,4,1,8,1024]{4,3,2,1,0:T(8,128)} %bitcast.7), calls=%async_computation.1 | async-start | bytes 1048576 | tf_op jit(solution)/shard_map/own_y/all_to_all | solution.py:130
  84.3 1.9 %collective-permute-start.1 = (f32[4,2,4,8,512]{4,3,2,1,0:T(8,128)}, f32[4,2,4,8,512]{4,3,2,1,0:T(8,128)}, u32[]{:S(2)}, u32[]{:S(2)}) collective-permute-start(f32[4,2,4,8,512]{4,3,2,1,0:T(8,128)} %bitcast.6.refs_0_), channel_id=1, source_target_pairs={{0,8},{8,0},{16,24},{24,16},{1,9},{9,1},{17,25},{25,17},{2,10},{10... | collective-permute-start | bytes 1572872 | tf_op jit(solution)/shard_map/gather_y/ppermute | solution.py:126
  86.2 4.7 %collective-permute-start.2 = (f32[4,2,4,8,512]{4,3,2,1,0:T(8,128)}, f32[4,2,4,8,512]{4,3,2,1,0:T(8,128)}, u32[]{:S(2)}, u32[]{:S(2)}) collective-permute-start(f32[4,2,4,8,512]{4,3,2,1,0:T(8,128)} %bitcast.6.refs_0_), channel_id=1, source_target_pairs={{0,24},{8,16},{16,8},{24,0},{1,25},{9,17},{17,9},{25,1},{2,26},{10... | collective-permute-start | bytes 1572872 | tf_op jit(solution)/shard_map/gather_y/ppermute | solution.py:126
  91.0 0.0 collective-permute-done.3.refs_0_
  91.0 2.9 %across_y.1 = f32[128,1024]{1,0:T(8,128)S(1)} custom-call(s32[1]{0:T(128)} %bitcast.1.core_ref, f32[4,2,4,8,512]{4,3,2,1,0:T(8,128)S(1)} %collective-permute-done.3.refs_0_, f32[1024,512]{1,0:T(8,128)S(1)} %slab.1.refs_1_.refs_2_, f32[1024,512]{1,0:T(8,128)} %collective-permute-done.refs_2_.refs_3_), custom_call_target="tpu_custom_call" | custom-call | flops 1 | bytes 1 | tf_op jit(solution)/shard_map/across_y/pallas_call | solution.py:78
  93.9 0.0 copy-start.1
  93.9 0.8 copy-done.1
  94.7 0.0 all-to-all-done.1.own_ref
  94.7 4.8 %all-to-all-start.3 = ((f32[4,4,1,8,1024]{4,3,2,1,0:T(8,128)}), f32[4,4,1,8,1024]{4,3,2,1,0:T(8,128)S(1)}, u32[]{:S(2)}, u32[]{:S(2)}) async-start(f32[4,4,1,8,1024]{4,3,2,1,0:T(8,128)} %bitcast.13), calls=%async_computation.3 | async-start | bytes 1048576 | tf_op jit(solution)/shard_map/across_y/all_to_all | solution.py:130
  99.5 0.0 collective-permute-done.1.refs_0_
  99.5 3.1 %collective-permute-done.2.refs_1_ = f32[4,2,4,8,512]{4,3,2,1,0:T(8,128)} collective-permute-done((f32[4,2,4,8,512]{4,3,2,1,0:T(8,128)}, f32[4,2,4,8,512]{4,3,2,1,0:T(8,128)}, u32[]{:S(2)}, u32[]{:S(2)}) %collective-permute-start.2) | collective-permute-done | bytes 524320 | tf_op jit(solution)/shard_map/gather_y/ppermute | solution.py:126
  102.5 4.5 %sides_y.1 = f32[256,1024]{1,0:T(8,128)} custom-call(s32[1]{0:T(128)} %bitcast.1.core_ref, f32[4,2,4,8,512]{4,3,2,1,0:T(8,128)} %collective-permute-done.1.refs_0_, f32[4,2,4,8,512]{4,3,2,1,0:T(8,128)} %collective-permute-done.2.refs_1_, f32[1024,512]{1,0:T(8,128)S(1)} %slab.1.refs_1_.refs_2_, f32[1024,512]{1,0:T(8,128)} %collective-permute-done.refs_2_.refs_3_), custom_call_target="tpu_custom_call" | custom-call | flops 1 | bytes 1 | tf_op jit(solution)/shard_map/sides_y/pallas_call | solution.py:78
  107.1 0.5 all-to-all-done.3.across_ref
  107.6 4.0 %all-to-all-start.2 = ((f32[4,4,2,8,1024]{4,3,2,1,0:T(8,128)}), f32[4,4,2,8,1024]{4,3,2,1,0:T(8,128)S(1)}, u32[]{:S(2)}, u32[]{:S(2)}) async-start(f32[4,4,2,8,1024]{4,3,2,1,0:T(8,128)} %bitcast.8), calls=%async_computation.2 | async-start | bytes 2097152 | tf_op jit(solution)/shard_map/sides_y/all_to_all | solution.py:130
  111.6 13.1 %all-to-all-done.2.sides_ref = f32[4,4,2,8,1024]{4,3,2,1,0:T(8,128)S(1)} async-done(((f32[4,4,2,8,1024]{4,3,2,1,0:T(8,128)}), f32[4,4,2,8,1024]{4,3,2,1,0:T(8,128)S(1)}, u32[]{:S(2)}, u32[]{:S(2)}) %all-to-all-start.2) | async-done | bytes 1048608 | tf_op jit(solution)/shard_map/sides_y/all_to_all | solution.py:130
  124.7 1.5 %shard_map.37 = f32[4,4,8,1024]{3,2,1,0:T(8,128)} custom-call(s32[1]{0:T(128)} %bitcast.y_ref, f32[4,4,1,8,1024]{4,3,2,1,0:T(8,128)S(1)} %all-to-all-done.1.own_ref, f32[4,4,2,8,1024]{4,3,2,1,0:T(8,128)S(1)} %all-to-all-done.2.sides_ref, f32[4,4,1,8,1024]{4,3,2,1,0:T(8,128)S(1)} %all-to-all-done.3.across_ref), custom_call_target="tpu_custom_call" | custom-call | flops 1 | bytes 1 | tf_op jit(solution)/shard_map/pallas_call | solution.py:111
  (1 shorter events, 0.0 us)
Async XLA Ops:
  0.0 57.8 %copy-start.2 = (s32[8,4]{0,1:T(4,128)S(1)}, s32[8,4]{0,1:T(4,128)}, u32[]{:S(2)}) copy-start(s32[8,4]{0,1:T(4,128)} %param.5) | copy-start | bytes 388
  53.6 19.5 %all-to-all-start = ((f32[8,4,8,512]{3,2,1,0:T(8,128)}), f32[8,4,8,512]{3,2,1,0:T(8,128)}, u32[]{:S(2)}, u32[]{:S(2)}) async-start(f32[8,4,8,512]{3,2,1,0:T(8,128)} %bitcast.5), calls=%async_computation | async-start | bytes 1048576 | tf_op jit(solution)/shard_map/gather_near/all_to_all | solution.py:144
  57.9 1.6 %copy-start = (f32[1024,512]{1,0:T(8,128)S(1)}, f32[1024,512]{1,0:T(8,128)}, u32[]{:S(2)}) copy-start(f32[1024,512]{1,0:T(8,128)} %v_ref.1) | copy-start | bytes 6291460
  60.3 16.0 %collective-permute-start = (f32[1024,512]{1,0:T(8,128)S(1)}, f32[1024,512]{1,0:T(8,128)}, u32[]{:S(2)}, u32[]{:S(2)}) collective-permute-start(f32[1024,512]{1,0:T(8,128)S(1)} %slab.1.refs_1_.refs_2_), channel_id=1, source_target_pairs={{0,1},{1,0},{2,3},{3,2},{4,5},{5,4},{6,7},{7,6},{8,9},{9,8},{10,11... | collective-permute-start | bytes 6291464 | tf_op jit(solution)/shard_map/slab/ppermute | solution.py:138
  73.2 17.8 %collective-permute-start.3 = (f32[4,2,4,8,512]{4,3,2,1,0:T(8,128)}, f32[4,2,4,8,512]{4,3,2,1,0:T(8,128)S(1)}, u32[]{:S(2)}, u32[]{:S(2)}) collective-permute-start(f32[4,2,4,8,512]{4,3,2,1,0:T(8,128)} %bitcast.6.refs_0_), channel_id=1, source_target_pairs={{0,16},{8,24},{16,0},{24,8},{1,17},{9,25},{17,1},{25,9},{2,18},{10... | collective-permute-start | bytes 1572872 | tf_op jit(solution)/shard_map/gather_y/ppermute | solution.py:126
  80.0 14.7 %all-to-all-start.1 = ((f32[4,4,1,8,1024]{4,3,2,1,0:T(8,128)}), f32[4,4,1,8,1024]{4,3,2,1,0:T(8,128)S(1)}, u32[]{:S(2)}, u32[]{:S(2)}) async-start(f32[4,4,1,8,1024]{4,3,2,1,0:T(8,128)} %bitcast.7), calls=%async_computation.1 | async-start | bytes 1048576 | tf_op jit(solution)/shard_map/own_y/all_to_all | solution.py:130
  84.3 15.2 %collective-permute-start.1 = (f32[4,2,4,8,512]{4,3,2,1,0:T(8,128)}, f32[4,2,4,8,512]{4,3,2,1,0:T(8,128)}, u32[]{:S(2)}, u32[]{:S(2)}) collective-permute-start(f32[4,2,4,8,512]{4,3,2,1,0:T(8,128)} %bitcast.6.refs_0_), channel_id=1, source_target_pairs={{0,8},{8,0},{16,24},{24,16},{1,9},{9,1},{17,25},{25,17},{2,10},{10... | collective-permute-start | bytes 1572872 | tf_op jit(solution)/shard_map/gather_y/ppermute | solution.py:126
  86.2 16.3 %collective-permute-start.2 = (f32[4,2,4,8,512]{4,3,2,1,0:T(8,128)}, f32[4,2,4,8,512]{4,3,2,1,0:T(8,128)}, u32[]{:S(2)}, u32[]{:S(2)}) collective-permute-start(f32[4,2,4,8,512]{4,3,2,1,0:T(8,128)} %bitcast.6.refs_0_), channel_id=1, source_target_pairs={{0,24},{8,16},{16,8},{24,0},{1,25},{9,17},{17,9},{25,1},{2,26},{10... | collective-permute-start | bytes 1572872 | tf_op jit(solution)/shard_map/gather_y/ppermute | solution.py:126
  93.9 0.8 copy-start.1
  94.7 12.9 %all-to-all-start.3 = ((f32[4,4,1,8,1024]{4,3,2,1,0:T(8,128)}), f32[4,4,1,8,1024]{4,3,2,1,0:T(8,128)S(1)}, u32[]{:S(2)}, u32[]{:S(2)}) async-start(f32[4,4,1,8,1024]{4,3,2,1,0:T(8,128)} %bitcast.13), calls=%async_computation.3 | async-start | bytes 1048576 | tf_op jit(solution)/shard_map/across_y/all_to_all | solution.py:130
  107.6 17.1 %all-to-all-start.2 = ((f32[4,4,2,8,1024]{4,3,2,1,0:T(8,128)}), f32[4,4,2,8,1024]{4,3,2,1,0:T(8,128)S(1)}, u32[]{:S(2)}, u32[]{:S(2)}) async-start(f32[4,4,2,8,1024]{4,3,2,1,0:T(8,128)} %bitcast.8), calls=%async_computation.2 | async-start | bytes 2097152 | tf_op jit(solution)/shard_map/sides_y/all_to_all | solution.py:130

commit v13 on v12

--- a/solution.py
+++ b/solution.py
@@ -86,7 +86,7 @@
             out_specs=pl.BlockSpec((rows, WIDE), lambda i, core: (0, i)),
             scratch_shapes=[pltpu.VMEM((2, 2 * rows, depth), jnp.bfloat16)],
         ),
-        compiler_params=PARAMS,
+        compiler_params=pltpu.CompilerParams(vmem_limit_bytes=32 * 2**20),
         cost_estimate=COST,
     )(core, *chunks, *slabs)
 
@@ -96,7 +96,9 @@
 
     def put(bits, part_ref, k):
         place = lax.bitwise_xor(me, bits)
-        out_ref[0, place] = (part_ref[0, 0, k] + part_ref[1, 0, k]) + (part_ref[2, 0, k] + part_ref[3, 0, k])
+        for low in range(2):
+            a, b, c, d = (part_ref[x, low, k] for x in range(4))
+            out_ref[low, place] = (a + b) + (c + d)
 
     put(0, own_ref, 0)
     put(1, sides_ref, 0)
@@ -106,16 +108,16 @@
 
 def finish(y, own, sides, across):
     def part(count):
-        return pl.BlockSpec((4, 1, count, 8, 1024), lambda low, y: (0, low, 0, 0, 0))
+        return pl.BlockSpec((4, 2, count, 8, 1024), lambda low, y: (0, low, 0, 0, 0))
 
     return pl.pallas_call(
         finish_body,
         out_shape=jax.ShapeDtypeStruct((4, 4, 8, 1024), jnp.float32),
         grid_spec=pltpu.PrefetchScalarGridSpec(
             num_scalar_prefetch=1,
-            grid=(4,),
+            grid=(2,),
             in_specs=[part(1), part(2), part(1)],
-            out_specs=pl.BlockSpec((1, 4, 8, 1024), lambda low, y: (low, 0, 0, 0)),
+            out_specs=pl.BlockSpec((2, 4, 8, 1024), lambda low, y: (low, 0, 0, 0)),
         ),
         compiler_params=PARAMS,
         cost_estimate=COST,

time: 128 us -> 127 us (level)
  transfers between devices with their start and end apart: 8 -> 8, of which waited for: 4 -> 4; matrix products, arithmetic and copies ran while one was open for 0% -> 0% of each run, Pallas kernels for 9% -> 10%
where the time goes in v13:
time: 127 us; the launch traced here: 126 us
  blocking collectives  52.8 us (42%)
  starting transfers between devices  29.3 us (23%)
  waiting for transfers between devices  27.2 us (21%)
  Pallas kernels  13 us (10%)
  local copies, waits for them, and re-layouts  3.33 us (3%)
    all_gather x1, blocking collectives, per_device(): far = lax.all_gather(amplitudes, 'zh')  52.8 us
    all_to_all x3, waiting for transfers between devices, over_x(): return lax.all_to_all(partial.reshape(4, 4, -1, 8, 1024), 'x', 0, 0)  13.6 us
    all_to_all x3, starting transfers between devices, over_x(): return lax.all_to_all(partial.reshape(4, 4, -1, 8, 1024), 'x', 0, 0)  13.1 us
    pallas_call x3, Pallas kernels, ladder(): pl.pallas_call(functools.partial(ladder_body, len(chunks)), out_shape=jax...  11.1 us
    all_to_all x1, waiting for transfers between devices, per_device(): near = lax.all_to_all(spread, ('zl', 'core'), 0, 0).reshape(4, 2, 4, 8, 512)  10.5 us
    ppermute x3, starting transfers between devices, swapped(): return lax.ppermute(value, 'y', [(i, i ^ bits) for i in range(4)])  9.79 us
    all_to_all x1, starting transfers between devices, per_device(): near = lax.all_to_all(spread, ('zl', 'core'), 0, 0).reshape(4, 2, 4, 8, 512)  4.15 us
    ppermute x3, waiting for transfers between devices, swapped(): return lax.ppermute(value, 'y', [(i, i ^ bits) for i in range(4)])  3.06 us
  transfers between devices with their start and end apart: 8, of which 4 were waited for; matrix products, arithmetic and copies ran while one was open for 0% of the time, Pallas kernels for 10%

profile of v13, /device:TPU:24, one launch (start us, length us, event | category | flops | bytes accessed | tf_op | source)
XLA Modules:
  0.0 125.7 jit_solution(5637531012414572262)
XLA Ops:
  0.0 0.0 copy-start.2
  0.0 52.8 %all-gather = f32[64,512]{1,0:T(8,128)S(1)} all-gather(f32[8,512]{1,0:T(8,128)} %param.4), channel_id=2, replica_groups=mesh['zh'=8,'zl'=4,'y'=4,'x'=4,'core'=2] {'zh'}, dimensions={0}, use_global_device_ids=true | all-gather | bytes 147456 | tf_op jit(solution)/shard_map/gather_far/all_gather | solution.py:142
  52.8 0.9 broadcast_in_dim.16
  53.6 4.2 %all-to-all-start = ((f32[8,4,8,512]{3,2,1,0:T(8,128)}), f32[8,4,8,512]{3,2,1,0:T(8,128)}, u32[]{:S(2)}, u32[]{:S(2)}) async-start(f32[8,4,8,512]{3,2,1,0:T(8,128)} %bitcast.5), calls=%async_computation | async-start | bytes 1048576 | tf_op jit(solution)/shard_map/gather_near/all_to_all | solution.py:146
  57.8 0.0 copy-done.2
  57.8 0.1 copy.5.allowed_ref
  57.9 0.0 copy-start
  57.9 1.6 %copy-done = f32[1024,512]{1,0:T(8,128)S(1)} copy-done((f32[1024,512]{1,0:T(8,128)S(1)}, f32[1024,512]{1,0:T(8,128)}, u32[]{:S(2)}) %copy-start) | copy-done | bytes 2097176
  59.5 0.8 slab.1.refs_1_.refs_2_
  60.3 2.3 %collective-permute-start = (f32[1024,512]{1,0:T(8,128)S(1)}, f32[1024,512]{1,0:T(8,128)}, u32[]{:S(2)}, u32[]{:S(2)}) collective-permute-start(f32[1024,512]{1,0:T(8,128)S(1)} %slab.1.refs_1_.refs_2_), channel_id=1, source_target_pairs={{0,1},{1,0},{2,3},{3,2},{4,5},{5,4},{6,7},{7,6},{8,9},{9,8},{10,11... | collective-permute-start | bytes 6291464 | tf_op jit(solution)/shard_map/slab/ppermute | solution.py:140
  62.6 10.5 %all-to-all-done = f32[8,4,8,512]{3,2,1,0:T(8,128)} async-done(((f32[8,4,8,512]{3,2,1,0:T(8,128)}), f32[8,4,8,512]{3,2,1,0:T(8,128)}, u32[]{:S(2)}, u32[]{:S(2)}) %all-to-all-start) | async-done | bytes 524320 | tf_op jit(solution)/shard_map/gather_near/all_to_all | solution.py:146
  73.2 3.1 %collective-permute-start.3 = (f32[4,2,4,8,512]{4,3,2,1,0:T(8,128)}, f32[4,2,4,8,512]{4,3,2,1,0:T(8,128)S(1)}, u32[]{:S(2)}, u32[]{:S(2)}) collective-permute-start(f32[4,2,4,8,512]{4,3,2,1,0:T(8,128)} %bitcast.6.refs_0_), channel_id=1, source_target_pairs={{0,16},{8,24},{16,0},{24,8},{1,17},{9,25},{17,1},{25,9},{2,18},{10... | collective-permute-start | bytes 1572872 | tf_op jit(solution)/shard_map/gather_y/ppermute | solution.py:128
  76.3 0.0 collective-permute-done.refs_2_.refs_3_
  76.3 3.7 %own_y.1 = f32[128,1024]{1,0:T(8,128)} custom-call(s32[1]{0:T(128)} %bitcast.1.core_ref, f32[4,2,4,8,512]{4,3,2,1,0:T(8,128)} %bitcast.6.refs_0_, f32[1024,512]{1,0:T(8,128)S(1)} %slab.1.refs_1_.refs_2_, f32[1024,512]{1,0:T(8,128)} %collective-permute-done.refs_2_.refs_3_), custom_call_target="tpu_custom_call" | custom-call | flops 1 | bytes 1 | tf_op jit(solution)/shard_map/own_y/pallas_call | solution.py:78
  80.0 4.3 %all-to-all-start.1 = ((f32[4,4,1,8,1024]{4,3,2,1,0:T(8,128)}), f32[4,4,1,8,1024]{4,3,2,1,0:T(8,128)S(1)}, u32[]{:S(2)}, u32[]{:S(2)}) async-start(f32[4,4,1,8,1024]{4,3,2,1,0:T(8,128)} %bitcast.7), calls=%async_computation.1 | async-start | bytes 1048576 | tf_op jit(solution)/shard_map/own_y/all_to_all | solution.py:132
  84.3 1.9 %collective-permute-start.1 = (f32[4,2,4,8,512]{4,3,2,1,0:T(8,128)}, f32[4,2,4,8,512]{4,3,2,1,0:T(8,128)}, u32[]{:S(2)}, u32[]{:S(2)}) collective-permute-start(f32[4,2,4,8,512]{4,3,2,1,0:T(8,128)} %bitcast.6.refs_0_), channel_id=1, source_target_pairs={{0,8},{8,0},{16,24},{24,16},{1,9},{9,1},{17,25},{25,17},{2,10},{10... | collective-permute-start | bytes 1572872 | tf_op jit(solution)/shard_map/gather_y/ppermute | solution.py:128
  86.2 4.7 %collective-permute-start.2 = (f32[4,2,4,8,512]{4,3,2,1,0:T(8,128)}, f32[4,2,4,8,512]{4,3,2,1,0:T(8,128)}, u32[]{:S(2)}, u32[]{:S(2)}) collective-permute-start(f32[4,2,4,8,512]{4,3,2,1,0:T(8,128)} %bitcast.6.refs_0_), channel_id=1, source_target_pairs={{0,24},{8,16},{16,8},{24,0},{1,25},{9,17},{17,9},{25,1},{2,26},{10... | collective-permute-start | bytes 1572872 | tf_op jit(solution)/shard_map/gather_y/ppermute | solution.py:128
  91.0 0.0 collective-permute-done.3.refs_0_
  91.0 2.9 %across_y.1 = f32[128,1024]{1,0:T(8,128)S(1)} custom-call(s32[1]{0:T(128)} %bitcast.1.core_ref, f32[4,2,4,8,512]{4,3,2,1,0:T(8,128)S(1)} %collective-permute-done.3.refs_0_, f32[1024,512]{1,0:T(8,128)S(1)} %slab.1.refs_1_.refs_2_, f32[1024,512]{1,0:T(8,128)} %collective-permute-done.refs_2_.refs_3_), custom_call_target="tpu_custom_call" | custom-call | flops 1 | bytes 1 | tf_op jit(solution)/shard_map/across_y/pallas_call | solution.py:78
  93.9 0.0 copy-start.1
  93.9 0.8 copy-done.1
  94.7 0.0 all-to-all-done.1.own_ref
  94.7 4.8 %all-to-all-start.3 = ((f32[4,4,1,8,1024]{4,3,2,1,0:T(8,128)}), f32[4,4,1,8,1024]{4,3,2,1,0:T(8,128)S(1)}, u32[]{:S(2)}, u32[]{:S(2)}) async-start(f32[4,4,1,8,1024]{4,3,2,1,0:T(8,128)} %bitcast.13), calls=%async_computation.3 | async-start | bytes 1048576 | tf_op jit(solution)/shard_map/across_y/all_to_all | solution.py:132
  99.5 0.0 collective-permute-done.1.refs_0_
  99.5 3.1 %collective-permute-done.2.refs_1_ = f32[4,2,4,8,512]{4,3,2,1,0:T(8,128)} collective-permute-done((f32[4,2,4,8,512]{4,3,2,1,0:T(8,128)}, f32[4,2,4,8,512]{4,3,2,1,0:T(8,128)}, u32[]{:S(2)}, u32[]{:S(2)}) %collective-permute-start.2) | collective-permute-done | bytes 524320 | tf_op jit(solution)/shard_map/gather_y/ppermute | solution.py:128
  102.5 4.5 %sides_y.1 = f32[256,1024]{1,0:T(8,128)} custom-call(s32[1]{0:T(128)} %bitcast.1.core_ref, f32[4,2,4,8,512]{4,3,2,1,0:T(8,128)} %collective-permute-done.1.refs_0_, f32[4,2,4,8,512]{4,3,2,1,0:T(8,128)} %collective-permute-done.2.refs_1_, f32[1024,512]{1,0:T(8,128)S(1)} %slab.1.refs_1_.refs_2_, f32[1024,512]{1,0:T(8,128)} %collective-permute-done.refs_2_.refs_3_), custom_call_target="tpu_custom_call" | custom-call | flops 1 | bytes 1 | tf_op jit(solution)/shard_map/sides_y/pallas_call | solution.py:78
  107.1 0.5 all-to-all-done.3.across_ref
  107.6 4.0 %all-to-all-start.2 = ((f32[4,4,2,8,1024]{4,3,2,1,0:T(8,128)}), f32[4,4,2,8,1024]{4,3,2,1,0:T(8,128)S(1)}, u32[]{:S(2)}, u32[]{:S(2)}) async-start(f32[4,4,2,8,1024]{4,3,2,1,0:T(8,128)} %bitcast.8), calls=%async_computation.2 | async-start | bytes 2097152 | tf_op jit(solution)/shard_map/sides_y/all_to_all | solution.py:132
  111.6 13.1 %all-to-all-done.2.sides_ref = f32[4,4,2,8,1024]{4,3,2,1,0:T(8,128)S(1)} async-done(((f32[4,4,2,8,1024]{4,3,2,1,0:T(8,128)}), f32[4,4,2,8,1024]{4,3,2,1,0:T(8,128)S(1)}, u32[]{:S(2)}, u32[]{:S(2)}) %all-to-all-start.2) | async-done | bytes 1048608 | tf_op jit(solution)/shard_map/sides_y/all_to_all | solution.py:132
  124.7 1.0 shard_map.37
  (1 shorter events, 0.0 us)
Async XLA Ops:
  0.0 57.8 %copy-start.2 = (s32[8,4]{0,1:T(4,128)S(1)}, s32[8,4]{0,1:T(4,128)}, u32[]{:S(2)}) copy-start(s32[8,4]{0,1:T(4,128)} %param.5) | copy-start | bytes 388
  53.6 19.5 %all-to-all-start = ((f32[8,4,8,512]{3,2,1,0:T(8,128)}), f32[8,4,8,512]{3,2,1,0:T(8,128)}, u32[]{:S(2)}, u32[]{:S(2)}) async-start(f32[8,4,8,512]{3,2,1,0:T(8,128)} %bitcast.5), calls=%async_computation | async-start | bytes 1048576 | tf_op jit(solution)/shard_map/gather_near/all_to_all | solution.py:146
  57.9 1.6 %copy-start = (f32[1024,512]{1,0:T(8,128)S(1)}, f32[1024,512]{1,0:T(8,128)}, u32[]{:S(2)}) copy-start(f32[1024,512]{1,0:T(8,128)} %v_ref.1) | copy-start | bytes 6291460
  60.3 16.0 %collective-permute-start = (f32[1024,512]{1,0:T(8,128)S(1)}, f32[1024,512]{1,0:T(8,128)}, u32[]{:S(2)}, u32[]{:S(2)}) collective-permute-start(f32[1024,512]{1,0:T(8,128)S(1)} %slab.1.refs_1_.refs_2_), channel_id=1, source_target_pairs={{0,1},{1,0},{2,3},{3,2},{4,5},{5,4},{6,7},{7,6},{8,9},{9,8},{10,11... | collective-permute-start | bytes 6291464 | tf_op jit(solution)/shard_map/slab/ppermute | solution.py:140
  73.2 17.8 %collective-permute-start.3 = (f32[4,2,4,8,512]{4,3,2,1,0:T(8,128)}, f32[4,2,4,8,512]{4,3,2,1,0:T(8,128)S(1)}, u32[]{:S(2)}, u32[]{:S(2)}) collective-permute-start(f32[4,2,4,8,512]{4,3,2,1,0:T(8,128)} %bitcast.6.refs_0_), channel_id=1, source_target_pairs={{0,16},{8,24},{16,0},{24,8},{1,17},{9,25},{17,1},{25,9},{2,18},{10... | collective-permute-start | bytes 1572872 | tf_op jit(solution)/shard_map/gather_y/ppermute | solution.py:128
  80.0 14.7 %all-to-all-start.1 = ((f32[4,4,1,8,1024]{4,3,2,1,0:T(8,128)}), f32[4,4,1,8,1024]{4,3,2,1,0:T(8,128)S(1)}, u32[]{:S(2)}, u32[]{:S(2)}) async-start(f32[4,4,1,8,1024]{4,3,2,1,0:T(8,128)} %bitcast.7), calls=%async_computation.1 | async-start | bytes 1048576 | tf_op jit(solution)/shard_map/own_y/all_to_all | solution.py:132
  84.3 15.2 %collective-permute-start.1 = (f32[4,2,4,8,512]{4,3,2,1,0:T(8,128)}, f32[4,2,4,8,512]{4,3,2,1,0:T(8,128)}, u32[]{:S(2)}, u32[]{:S(2)}) collective-permute-start(f32[4,2,4,8,512]{4,3,2,1,0:T(8,128)} %bitcast.6.refs_0_), channel_id=1, source_target_pairs={{0,8},{8,0},{16,24},{24,16},{1,9},{9,1},{17,25},{25,17},{2,10},{10... | collective-permute-start | bytes 1572872 | tf_op jit(solution)/shard_map/gather_y/ppermute | solution.py:128
  86.2 16.3 %collective-permute-start.2 = (f32[4,2,4,8,512]{4,3,2,1,0:T(8,128)}, f32[4,2,4,8,512]{4,3,2,1,0:T(8,128)}, u32[]{:S(2)}, u32[]{:S(2)}) collective-permute-start(f32[4,2,4,8,512]{4,3,2,1,0:T(8,128)} %bitcast.6.refs_0_), channel_id=1, source_target_pairs={{0,24},{8,16},{16,8},{24,0},{1,25},{9,17},{17,9},{25,1},{2,26},{10... | collective-permute-start | bytes 1572872 | tf_op jit(solution)/shard_map/gather_y/ppermute | solution.py:128
  93.9 0.8 copy-start.1
  94.7 12.9 %all-to-all-start.3 = ((f32[4,4,1,8,1024]{4,3,2,1,0:T(8,128)}), f32[4,4,1,8,1024]{4,3,2,1,0:T(8,128)S(1)}, u32[]{:S(2)}, u32[]{:S(2)}) async-start(f32[4,4,1,8,1024]{4,3,2,1,0:T(8,128)} %bitcast.13), calls=%async_computation.3 | async-start | bytes 1048576 | tf_op jit(solution)/shard_map/across_y/all_to_all | solution.py:132
  107.6 17.1 %all-to-all-start.2 = ((f32[4,4,2,8,1024]{4,3,2,1,0:T(8,128)}), f32[4,4,2,8,1024]{4,3,2,1,0:T(8,128)S(1)}, u32[]{:S(2)}, u32[]{:S(2)}) async-start(f32[4,4,2,8,1024]{4,3,2,1,0:T(8,128)} %bitcast.8), calls=%async_computation.2 | async-start | bytes 2097152 | tf_op jit(solution)/shard_map/sides_y/all_to_all | solution.py:132

commit v14 on v13

--- a/solution.py
+++ b/solution.py
@@ -10,7 +10,7 @@
 BLK = 128
 NT = (((1,), (1,)), ((), ()))
 COLS = 256
-WIDE = 512
+WIDE = 1024
 PARAMS = pltpu.CompilerParams(vmem_limit_bytes=48 * 2**20)
 COST = pl.CostEstimate(flops=1, bytes_accessed=1, transcendentals=0)
 
@@ -86,7 +86,7 @@
             out_specs=pl.BlockSpec((rows, WIDE), lambda i, core: (0, i)),
             scratch_shapes=[pltpu.VMEM((2, 2 * rows, depth), jnp.bfloat16)],
         ),
-        compiler_params=pltpu.CompilerParams(vmem_limit_bytes=32 * 2**20),
+        compiler_params=pltpu.CompilerParams(vmem_limit_bytes=48 * 2**20),
         cost_estimate=COST,
     )(core, *chunks, *slabs)
 

time: 127 us -> 128 us (level)
  no operation moved by 1% of the time
where the time goes in v14:
time: 128 us; the launch traced here: 126 us
  blocking collectives  52.8 us (41%)
  starting transfers between devices  29.4 us (23%)
  waiting for transfers between devices  27 us (21%)
  Pallas kernels  13.5 us (11%)
  local copies, waits for them, and re-layouts  3.33 us (3%)
    all_gather x1, blocking collectives, per_device(): far = lax.all_gather(amplitudes, 'zh')  52.8 us
    all_to_all x3, waiting for transfers between devices, over_x(): return lax.all_to_all(partial.reshape(4, 4, -1, 8, 1024), 'x', 0, 0)  13.5 us
    all_to_all x3, starting transfers between devices, over_x(): return lax.all_to_all(partial.reshape(4, 4, -1, 8, 1024), 'x', 0, 0)  13.2 us
    pallas_call x3, Pallas kernels, ladder(): pl.pallas_call(functools.partial(ladder_body, len(chunks)), out_shape=jax...  11.6 us
    all_to_all x1, waiting for transfers between devices, per_device(): near = lax.all_to_all(spread, ('zl', 'core'), 0, 0).reshape(4, 2, 4, 8, 512)  10.5 us
    ppermute x3, starting transfers between devices, swapped(): return lax.ppermute(value, 'y', [(i, i ^ bits) for i in range(4)])  9.79 us
    all_to_all x1, starting transfers between devices, per_device(): near = lax.all_to_all(spread, ('zl', 'core'), 0, 0).reshape(4, 2, 4, 8, 512)  4.15 us
    ppermute x3, waiting for transfers between devices, swapped(): return lax.ppermute(value, 'y', [(i, i ^ bits) for i in range(4)])  2.96 us
  transfers between devices with their start and end apart: 8, of which 4 were waited for; matrix products, arithmetic and copies ran while one was open for 0% of the time, Pallas kernels for 10%

profile of v14, /device:TPU:24, one launch (start us, length us, event | category | flops | bytes accessed | tf_op | source)
XLA Modules:
  0.0 126.2 jit_solution(9992376929172252721)
XLA Ops:
  0.0 0.0 copy-start.2
  0.0 52.8 %all-gather = f32[64,512]{1,0:T(8,128)S(1)} all-gather(f32[8,512]{1,0:T(8,128)} %param.4), channel_id=2, replica_groups=mesh['zh'=8,'zl'=4,'y'=4,'x'=4,'core'=2] {'zh'}, dimensions={0}, use_global_device_ids=true | all-gather | bytes 147456 | tf_op jit(solution)/shard_map/gather_far/all_gather | solution.py:142
  52.8 0.9 broadcast_in_dim.16
  53.6 4.2 %all-to-all-start = ((f32[8,4,8,512]{3,2,1,0:T(8,128)}), f32[8,4,8,512]{3,2,1,0:T(8,128)}, u32[]{:S(2)}, u32[]{:S(2)}) async-start(f32[8,4,8,512]{3,2,1,0:T(8,128)} %bitcast.5), calls=%async_computation | async-start | bytes 1048576 | tf_op jit(solution)/shard_map/gather_near/all_to_all | solution.py:146
  57.8 0.0 copy-done.2
  57.8 0.1 copy.5.allowed_ref
  57.9 0.0 copy-start
  57.9 1.6 %copy-done = f32[1024,512]{1,0:T(8,128)S(1)} copy-done((f32[1024,512]{1,0:T(8,128)S(1)}, f32[1024,512]{1,0:T(8,128)}, u32[]{:S(2)}) %copy-start) | copy-done | bytes 2097176
  59.5 0.8 slab.1.refs_1_.refs_2_
  60.3 2.3 %collective-permute-start = (f32[1024,512]{1,0:T(8,128)S(1)}, f32[1024,512]{1,0:T(8,128)}, u32[]{:S(2)}, u32[]{:S(2)}) collective-permute-start(f32[1024,512]{1,0:T(8,128)S(1)} %slab.1.refs_1_.refs_2_), channel_id=1, source_target_pairs={{0,1},{1,0},{2,3},{3,2},{4,5},{5,4},{6,7},{7,6},{8,9},{9,8},{10,11... | collective-permute-start | bytes 6291464 | tf_op jit(solution)/shard_map/slab/ppermute | solution.py:140
  62.6 10.5 %all-to-all-done = f32[8,4,8,512]{3,2,1,0:T(8,128)} async-done(((f32[8,4,8,512]{3,2,1,0:T(8,128)}), f32[8,4,8,512]{3,2,1,0:T(8,128)}, u32[]{:S(2)}, u32[]{:S(2)}) %all-to-all-start) | async-done | bytes 524320 | tf_op jit(solution)/shard_map/gather_near/all_to_all | solution.py:146
  73.2 3.1 %collective-permute-start.3 = (f32[4,2,4,8,512]{4,3,2,1,0:T(8,128)}, f32[4,2,4,8,512]{4,3,2,1,0:T(8,128)S(1)}, u32[]{:S(2)}, u32[]{:S(2)}) collective-permute-start(f32[4,2,4,8,512]{4,3,2,1,0:T(8,128)} %bitcast.6.refs_0_), channel_id=1, source_target_pairs={{0,16},{8,24},{16,0},{24,8},{1,17},{9,25},{17,1},{25,9},{2,18},{10... | collective-permute-start | bytes 1572872 | tf_op jit(solution)/shard_map/gather_y/ppermute | solution.py:128
  76.3 0.0 collective-permute-done.refs_2_.refs_3_
  76.3 3.9 %own_y.1 = f32[128,1024]{1,0:T(8,128)} custom-call(s32[1]{0:T(128)} %bitcast.1.core_ref, f32[4,2,4,8,512]{4,3,2,1,0:T(8,128)} %bitcast.6.refs_0_, f32[1024,512]{1,0:T(8,128)S(1)} %slab.1.refs_1_.refs_2_, f32[1024,512]{1,0:T(8,128)} %collective-permute-done.refs_2_.refs_3_), custom_call_target="tpu_custom_call" | custom-call | flops 1 | bytes 1 | tf_op jit(solution)/shard_map/own_y/pallas_call | solution.py:78
  80.3 4.3 %all-to-all-start.1 = ((f32[4,4,1,8,1024]{4,3,2,1,0:T(8,128)}), f32[4,4,1,8,1024]{4,3,2,1,0:T(8,128)S(1)}, u32[]{:S(2)}, u32[]{:S(2)}) async-start(f32[4,4,1,8,1024]{4,3,2,1,0:T(8,128)} %bitcast.7), calls=%async_computation.1 | async-start | bytes 1048576 | tf_op jit(solution)/shard_map/own_y/all_to_all | solution.py:132
  84.6 1.9 %collective-permute-start.1 = (f32[4,2,4,8,512]{4,3,2,1,0:T(8,128)}, f32[4,2,4,8,512]{4,3,2,1,0:T(8,128)}, u32[]{:S(2)}, u32[]{:S(2)}) collective-permute-start(f32[4,2,4,8,512]{4,3,2,1,0:T(8,128)} %bitcast.6.refs_0_), channel_id=1, source_target_pairs={{0,8},{8,0},{16,24},{24,16},{1,9},{9,1},{17,25},{25,17},{2,10},{10... | collective-permute-start | bytes 1572872 | tf_op jit(solution)/shard_map/gather_y/ppermute | solution.py:128
  86.5 4.8 %collective-permute-start.2 = (f32[4,2,4,8,512]{4,3,2,1,0:T(8,128)}, f32[4,2,4,8,512]{4,3,2,1,0:T(8,128)}, u32[]{:S(2)}, u32[]{:S(2)}) collective-permute-start(f32[4,2,4,8,512]{4,3,2,1,0:T(8,128)} %bitcast.6.refs_0_), channel_id=1, source_target_pairs={{0,24},{8,16},{16,8},{24,0},{1,25},{9,17},{17,9},{25,1},{2,26},{10... | collective-permute-start | bytes 1572872 | tf_op jit(solution)/shard_map/gather_y/ppermute | solution.py:128
  91.2 0.0 collective-permute-done.3.refs_0_
  91.2 3.0 %across_y.1 = f32[128,1024]{1,0:T(8,128)S(1)} custom-call(s32[1]{0:T(128)} %bitcast.1.core_ref, f32[4,2,4,8,512]{4,3,2,1,0:T(8,128)S(1)} %collective-permute-done.3.refs_0_, f32[1024,512]{1,0:T(8,128)S(1)} %slab.1.refs_1_.refs_2_, f32[1024,512]{1,0:T(8,128)} %collective-permute-done.refs_2_.refs_3_), custom_call_target="tpu_custom_call" | custom-call | flops 1 | bytes 1 | tf_op jit(solution)/shard_map/across_y/pallas_call | solution.py:78
  94.2 0.0 copy-start.1
  94.2 0.8 copy-done.1
  95.0 0.0 all-to-all-done.1.own_ref
  95.0 4.8 %all-to-all-start.3 = ((f32[4,4,1,8,1024]{4,3,2,1,0:T(8,128)}), f32[4,4,1,8,1024]{4,3,2,1,0:T(8,128)S(1)}, u32[]{:S(2)}, u32[]{:S(2)}) async-start(f32[4,4,1,8,1024]{4,3,2,1,0:T(8,128)} %bitcast.13), calls=%async_computation.3 | async-start | bytes 1048576 | tf_op jit(solution)/shard_map/across_y/all_to_all | solution.py:132
  99.8 0.0 collective-permute-done.1.refs_0_
  99.8 3.0 %collective-permute-done.2.refs_1_ = f32[4,2,4,8,512]{4,3,2,1,0:T(8,128)} collective-permute-done((f32[4,2,4,8,512]{4,3,2,1,0:T(8,128)}, f32[4,2,4,8,512]{4,3,2,1,0:T(8,128)}, u32[]{:S(2)}, u32[]{:S(2)}) %collective-permute-start.2) | collective-permute-done | bytes 524320 | tf_op jit(solution)/shard_map/gather_y/ppermute | solution.py:128
  102.8 4.7 %sides_y.1 = f32[256,1024]{1,0:T(8,128)} custom-call(s32[1]{0:T(128)} %bitcast.1.core_ref, f32[4,2,4,8,512]{4,3,2,1,0:T(8,128)} %collective-permute-done.1.refs_0_, f32[4,2,4,8,512]{4,3,2,1,0:T(8,128)} %collective-permute-done.2.refs_1_, f32[1024,512]{1,0:T(8,128)S(1)} %slab.1.refs_1_.refs_2_, f32[1024,512]{1,0:T(8,128)} %collective-permute-done.refs_2_.refs_3_), custom_call_target="tpu_custom_call" | custom-call | flops 1 | bytes 1 | tf_op jit(solution)/shard_map/sides_y/pallas_call | solution.py:78
  107.5 0.4 all-to-all-done.3.across_ref
  107.9 4.1 %all-to-all-start.2 = ((f32[4,4,2,8,1024]{4,3,2,1,0:T(8,128)}), f32[4,4,2,8,1024]{4,3,2,1,0:T(8,128)S(1)}, u32[]{:S(2)}, u32[]{:S(2)}) async-start(f32[4,4,2,8,1024]{4,3,2,1,0:T(8,128)} %bitcast.8), calls=%async_computation.2 | async-start | bytes 2097152 | tf_op jit(solution)/shard_map/sides_y/all_to_all | solution.py:132
  112.0 13.1 %all-to-all-done.2.sides_ref = f32[4,4,2,8,1024]{4,3,2,1,0:T(8,128)S(1)} async-done(((f32[4,4,2,8,1024]{4,3,2,1,0:T(8,128)}), f32[4,4,2,8,1024]{4,3,2,1,0:T(8,128)S(1)}, u32[]{:S(2)}, u32[]{:S(2)}) %all-to-all-start.2) | async-done | bytes 1048608 | tf_op jit(solution)/shard_map/sides_y/all_to_all | solution.py:132
  125.1 1.0 shard_map.37
  (1 shorter events, 0.0 us)
Async XLA Ops:
  0.0 57.8 %copy-start.2 = (s32[8,4]{0,1:T(4,128)S(1)}, s32[8,4]{0,1:T(4,128)}, u32[]{:S(2)}) copy-start(s32[8,4]{0,1:T(4,128)} %param.5) | copy-start | bytes 388
  53.6 19.5 %all-to-all-start = ((f32[8,4,8,512]{3,2,1,0:T(8,128)}), f32[8,4,8,512]{3,2,1,0:T(8,128)}, u32[]{:S(2)}, u32[]{:S(2)}) async-start(f32[8,4,8,512]{3,2,1,0:T(8,128)} %bitcast.5), calls=%async_computation | async-start | bytes 1048576 | tf_op jit(solution)/shard_map/gather_near/all_to_all | solution.py:146
  57.9 1.6 %copy-start = (f32[1024,512]{1,0:T(8,128)S(1)}, f32[1024,512]{1,0:T(8,128)}, u32[]{:S(2)}) copy-start(f32[1024,512]{1,0:T(8,128)} %v_ref.1) | copy-start | bytes 6291460
  60.3 16.0 %collective-permute-start = (f32[1024,512]{1,0:T(8,128)S(1)}, f32[1024,512]{1,0:T(8,128)}, u32[]{:S(2)}, u32[]{:S(2)}) collective-permute-start(f32[1024,512]{1,0:T(8,128)S(1)} %slab.1.refs_1_.refs_2_), channel_id=1, source_target_pairs={{0,1},{1,0},{2,3},{3,2},{4,5},{5,4},{6,7},{7,6},{8,9},{9,8},{10,11... | collective-permute-start | bytes 6291464 | tf_op jit(solution)/shard_map/slab/ppermute | solution.py:140
  73.2 18.1 %collective-permute-start.3 = (f32[4,2,4,8,512]{4,3,2,1,0:T(8,128)}, f32[4,2,4,8,512]{4,3,2,1,0:T(8,128)S(1)}, u32[]{:S(2)}, u32[]{:S(2)}) collective-permute-start(f32[4,2,4,8,512]{4,3,2,1,0:T(8,128)} %bitcast.6.refs_0_), channel_id=1, source_target_pairs={{0,16},{8,24},{16,0},{24,8},{1,17},{9,25},{17,1},{25,9},{2,18},{10... | collective-permute-start | bytes 1572872 | tf_op jit(solution)/shard_map/gather_y/ppermute | solution.py:128
  80.3 14.8 %all-to-all-start.1 = ((f32[4,4,1,8,1024]{4,3,2,1,0:T(8,128)}), f32[4,4,1,8,1024]{4,3,2,1,0:T(8,128)S(1)}, u32[]{:S(2)}, u32[]{:S(2)}) async-start(f32[4,4,1,8,1024]{4,3,2,1,0:T(8,128)} %bitcast.7), calls=%async_computation.1 | async-start | bytes 1048576 | tf_op jit(solution)/shard_map/own_y/all_to_all | solution.py:132
  84.6 15.3 %collective-permute-start.1 = (f32[4,2,4,8,512]{4,3,2,1,0:T(8,128)}, f32[4,2,4,8,512]{4,3,2,1,0:T(8,128)}, u32[]{:S(2)}, u32[]{:S(2)}) collective-permute-start(f32[4,2,4,8,512]{4,3,2,1,0:T(8,128)} %bitcast.6.refs_0_), channel_id=1, source_target_pairs={{0,8},{8,0},{16,24},{24,16},{1,9},{9,1},{17,25},{25,17},{2,10},{10... | collective-permute-start | bytes 1572872 | tf_op jit(solution)/shard_map/gather_y/ppermute | solution.py:128
  86.5 16.3 %collective-permute-start.2 = (f32[4,2,4,8,512]{4,3,2,1,0:T(8,128)}, f32[4,2,4,8,512]{4,3,2,1,0:T(8,128)}, u32[]{:S(2)}, u32[]{:S(2)}) collective-permute-start(f32[4,2,4,8,512]{4,3,2,1,0:T(8,128)} %bitcast.6.refs_0_), channel_id=1, source_target_pairs={{0,24},{8,16},{16,8},{24,0},{1,25},{9,17},{17,9},{25,1},{2,26},{10... | collective-permute-start | bytes 1572872 | tf_op jit(solution)/shard_map/gather_y/ppermute | solution.py:128
  94.2 0.8 copy-start.1
  95.0 12.9 %all-to-all-start.3 = ((f32[4,4,1,8,1024]{4,3,2,1,0:T(8,128)}), f32[4,4,1,8,1024]{4,3,2,1,0:T(8,128)S(1)}, u32[]{:S(2)}, u32[]{:S(2)}) async-start(f32[4,4,1,8,1024]{4,3,2,1,0:T(8,128)} %bitcast.13), calls=%async_computation.3 | async-start | bytes 1048576 | tf_op jit(solution)/shard_map/across_y/all_to_all | solution.py:132
  107.9 17.2 %all-to-all-start.2 = ((f32[4,4,2,8,1024]{4,3,2,1,0:T(8,128)}), f32[4,4,2,8,1024]{4,3,2,1,0:T(8,128)S(1)}, u32[]{:S(2)}, u32[]{:S(2)}) async-start(f32[4,4,2,8,1024]{4,3,2,1,0:T(8,128)} %bitcast.8), calls=%async_computation.2 | async-start | bytes 2097152 | tf_op jit(solution)/shard_map/sides_y/all_to_all | solution.py:132
